TPU v7x, 32 devices: a whole 2x2x4 slice. The times are simulated.
32 devices in a mesh: dp: 8 (over z, y), tensor: 4 (over x, core).
Axes of the slice: x: 2, y: 2, z: 4, core: 2. Of those that a mesh axis runs over, the one named last changes fastest.
Arguments:
- tokens: bfloat16 [4096, 768], P(('dp', 'tensor')), may hold values from -6 to 6
- doc_start: int32 [4096], P('dp'), may hold values from 0 to 511, as said below
- routes: int32 [4096, 2], P(('dp', 'tensor')), may hold values from 0 to 7, all different within a row; in each aligned block of 128 rows (0 to 127, 128 to 255, ...) at most 48 rows name the same one
- gain_attn: float32 [768], replicated, may hold values from 0.5 to 1.5
- w_qkv: bfloat16 [768, 3, 768], P('dp', None, 'tensor'), may hold values from -0.21875 to 0.21875
- w_out: bfloat16 [768, 768], P('dp', 'tensor'), may hold values from -1.25 to 1.25
- rel_bias: float32 [32, 12], replicated, may hold values from -4 to 4
- gain_ffn: float32 [768], replicated, may hold values from 0.5 to 1.5
- router: bfloat16 [768, 8], replicated, may hold values from -0.15625 to 0.15625
- w_in: bfloat16 [8, 768, 3072], P('dp', None, 'tensor'), may hold values from -0.21875 to 0.21875
- w_exp_out: bfloat16 [8, 3072, 768], P('dp', 'tensor'), may hold values from -0.109375 to 0.109375
- out_grad: bfloat16 [4096, 768], P(('dp', 'tensor')), may hold values from -6 to 6
Outputs:
- mixed_out: bfloat16 [4096, 768], P(('dp', 'tensor'))
- input_grad: bfloat16 [4096, 768], P(('dp', 'tensor'))
- grad_gain_attn: float32 [768], replicated
- grad_w_qkv: float32 [768, 3, 768], P('dp', None, 'tensor')
- grad_w_out: float32 [768, 768], P('dp', 'tensor')
- grad_rel_bias: float32 [32, 12], replicated
- grad_gain_ffn: float32 [768], replicated
- grad_router: float32 [768, 8], replicated
- grad_w_in: float32 [8, 768, 3072], P('dp', None, 'tensor')
- grad_w_exp_out: float32 [8, 3072, 768], P('dp', 'tensor')
Inputs may be any that keep to these rules, and one draw needn't show every extreme that they name: `doc_start`: the position, within the group of 512 tokens of its index of dp, at which a token's document begins; a group holds one or two documents, the first of half of 512 tokens or more. `routes`: a token's two experts differ; among the 128 rows of one device no expert is named by more than 48 rows, a bound that some block reaches.
All inputs are finite; a program needn't handle non-finite values.
Results may differ from a plain program's by a relative error of at most 0.012.
Values may be sent and summed in bfloat16 or wider, within the bound.
No kernel may reach another device: no remote copies, remote signals or barrier semaphores. Data moves between devices by JAX's collectives and lax.ppermute only.
A program may use at most 128 MiB of HBM per device.

v0:
```python
import jax
import jax.numpy as jnp
import numpy as np
from jax import lax
from jax.sharding import PartitionSpec as P

HEADS = 12
HDIM = 64
BUCKETS = 32


LIMITS = np.array([19, 21, 24, 27, 31, 35, 40, 46, 52, 59, 67, 77, 87, 99, 113], np.int32)
HIGHEST_PRECISION = lax.Precision.HIGHEST


def bucket_table(length):
    distance = jnp.arange(length, dtype=jnp.int32)
    beyond = jnp.sum((distance[:, None] >= jnp.asarray(LIMITS)[None, :]).astype(jnp.int32), axis=1)
    bucket = jnp.where(distance < 16, distance, 16 + beyond)
    return (bucket[:, None] == jnp.arange(BUCKETS, dtype=jnp.int32)[None, :]).astype(jnp.float32)


def toeplitz(line):
    heads_here, length = line.shape
    circle = jnp.concatenate(
        [line[:, :1], jnp.zeros((heads_here, length), line.dtype), jnp.flip(line[:, 1:], 1)], axis=1
    )
    tiled = jnp.tile(circle, (1, length))
    sheared = tiled[:, : length * (2 * length - 1)].reshape(heads_here, length, 2 * length - 1)
    return sheared[:, :, :length]


def diagonal_sums(grid):
    heads_here, length, _ = grid.shape
    padded = jnp.concatenate(
        [jnp.zeros((heads_here, length, length - 1), grid.dtype), grid], axis=2
    )
    flat = padded.reshape(heads_here, length * (2 * length - 1))
    flat = jnp.concatenate([flat, jnp.zeros((heads_here, length), grid.dtype)], axis=1)
    sheared = flat.reshape(heads_here, length, 2 * length)
    return jnp.flip(jnp.sum(sheared[:, :, :length], axis=1), axis=1)


def scores_of(query_rows, key_rows, bias_grid, allowed):
    raw = (
        jnp.einsum("hid,hjd->hij", query_rows, key_rows, preferred_element_type=jnp.float32)
        * HDIM ** (-0.5)
        + bias_grid
    )
    return jnp.where(allowed[None], raw, -1000000000.0)


def gelu_tanh(values_in):
    return jax.nn.gelu(values_in, approximate=True)


def to_experts(slot_block):
    return lax.all_to_all(slot_block, "dp", split_axis=0, concat_axis=0, tiled=True)


def from_experts(slot_block):
    return lax.all_to_all(slot_block, "dp", split_axis=0, concat_axis=0, tiled=True)


def spread_rows(slot_block):
    return lax.all_gather(slot_block, "tensor", axis=0, tiled=True)


def slot_sums(left, right, contract):
    return lax.psum_scatter(
        lax.dot_general(
            left, right, (((1,), (contract,)), ((), ())), preferred_element_type=jnp.float32
        ),
        "tensor",
        scatter_dimension=0,
        tiled=True,
    )


def body(
    tokens,
    doc_start,
    routes,
    gain_attn,
    w_qkv,
    w_out,
    rel_bias,
    gain_ffn,
    router,
    w_in,
    w_exp_out,
    out_grad,
):
    pieces = lax.axis_size("tensor")
    piece_id = lax.axis_index("tensor")
    senders = lax.axis_size("dp")
    tok_dev = tokens.shape[0]
    model_width = tokens.shape[1]
    length = tok_dev * pieces
    top_k = routes.shape[1]
    experts_all = router.shape[1]
    capacity = max(2, 3 * tok_dev * top_k // (2 * experts_all))
    own_first = piece_id * tok_dev
    weights_qkv, weights_out = (
        lax.all_gather(w_qkv, "dp", axis=0, tiled=True),
        lax.all_gather(w_out, "dp", axis=0, tiled=True),
    )
    heads_dev = weights_out.shape[1] // HDIM
    head_cols = heads_dev * HDIM
    own_rows = tokens.astype(jnp.float32)
    whole_rows = lax.all_gather(tokens, "tensor", axis=0, tiled=True).astype(jnp.float32)
    scale_one = lax.rsqrt(jnp.mean(whole_rows * whole_rows, axis=1, keepdims=True) + 1e-06)
    normed_one = (whole_rows * scale_one * gain_attn).astype(jnp.bfloat16)
    projected = jnp.einsum(
        "td,dcf->tcf", normed_one, weights_qkv, preferred_element_type=jnp.float32
    ).astype(jnp.bfloat16)
    per_head = projected.reshape(length, 3, heads_dev, HDIM).transpose(1, 2, 0, 3)
    query_rows, key_rows, value_rows = (per_head[0], per_head[1], per_head[2])
    place = jnp.arange(length, dtype=jnp.int32)
    allowed = (place[None, :] <= place[:, None]) & (place[None, :] >= doc_start[:, None])
    buckets = bucket_table(length)
    own_bias = lax.dynamic_slice_in_dim(rel_bias, piece_id * heads_dev, heads_dev, 1)
    bias_line = jnp.einsum("bh,nb->hn", own_bias, buckets, precision=HIGHEST_PRECISION)
    bias_grid = toeplitz(bias_line)
    scores = scores_of(query_rows, key_rows, bias_grid, allowed)
    peak = jnp.max(scores, axis=2, keepdims=True)
    shifted = jnp.exp(scores - peak)
    totals = jnp.sum(shifted, axis=2, keepdims=True)
    log_total = peak + jnp.log(totals)
    attention = (shifted / totals).astype(jnp.bfloat16)
    attended = jnp.einsum(
        "hij,hjd->hid", attention, value_rows, preferred_element_type=jnp.float32
    ).astype(jnp.bfloat16)
    attended_rows = attended.transpose(1, 0, 2).reshape(length, head_cols)
    partial_out = jnp.einsum(
        "tf,df->td", attended_rows, weights_out, preferred_element_type=jnp.float32
    )
    mixed_own = own_rows + lax.psum_scatter(partial_out, "tensor", scatter_dimension=0, tiled=True)
    scale_two = lax.rsqrt(jnp.mean(mixed_own * mixed_own, axis=1, keepdims=True) + 1e-06)
    normed_two = (mixed_own * scale_two * gain_ffn).astype(jnp.bfloat16)
    logits = jnp.dot(normed_two, router, preferred_element_type=jnp.float32)
    expert_iota = jnp.arange(experts_all, dtype=jnp.int32)
    picks = (routes[:, :, None] == expert_iota[None, None, :]).astype(jnp.float32)
    chosen = jnp.einsum("tke,te->tk", picks, logits, precision=HIGHEST_PRECISION)
    gates = jax.nn.softmax(chosen, axis=1)
    flat_ids = routes.reshape(-1)
    member = (flat_ids[:, None] == expert_iota[None, :]).astype(jnp.int32)
    slot_rank = jnp.sum(member * (jnp.cumsum(member, axis=0) - 1), axis=1)
    slot_index = flat_ids * capacity + slot_rank
    select = (
        slot_index[None, :] == jnp.arange(experts_all * capacity, dtype=jnp.int32)[:, None]
    ).astype(jnp.bfloat16)
    route_rows = jnp.repeat(normed_two, top_k, axis=0)
    outgoing = jnp.dot(select, route_rows, preferred_element_type=jnp.float32).astype(jnp.bfloat16)
    incoming = to_experts(outgoing.reshape(experts_all, capacity, model_width)).reshape(
        senders * capacity, model_width
    )
    full_in, full_out = (w_in[0], w_exp_out[0])
    expert_rows = spread_rows(incoming)
    pre_act = jnp.dot(expert_rows, full_in, preferred_element_type=jnp.float32)
    hidden = gelu_tanh(pre_act).astype(jnp.bfloat16)
    expert_out = slot_sums(hidden, full_out, 0)
    returned = from_experts(
        expert_out.astype(jnp.bfloat16).reshape(senders, capacity, model_width)
    ).reshape(experts_all * capacity, model_width)
    route_out = jnp.einsum(
        "sr,sd->rd", select, returned, preferred_element_type=jnp.float32
    ).reshape(tok_dev, top_k, model_width)
    result = (mixed_own + jnp.sum(gates[:, :, None] * route_out, axis=1)).astype(jnp.bfloat16)
    grad_rows = out_grad.astype(jnp.float32)
    gate_grad = jnp.einsum("tkd,td->tk", route_out, grad_rows, precision=HIGHEST_PRECISION)
    route_grad = (
        (gates[:, :, None] * grad_rows[:, None, :])
        .reshape(tok_dev * top_k, model_width)
        .astype(jnp.bfloat16)
    )
    outgoing_grad = jnp.dot(select, route_grad, preferred_element_type=jnp.float32).astype(
        jnp.bfloat16
    )
    incoming_grad = to_experts(outgoing_grad.reshape(experts_all, capacity, model_width)).reshape(
        senders * capacity, model_width
    )
    out_grad_rows = spread_rows(incoming_grad)
    grad_hidden_out = jnp.einsum(
        "rf,rd->fd", hidden, out_grad_rows, preferred_element_type=jnp.float32
    )
    hidden_grad = jnp.einsum(
        "rd,fd->rf", out_grad_rows, full_out, preferred_element_type=jnp.float32
    )
    pre_grad = jax.vjp(gelu_tanh, pre_act)[1](hidden_grad)[0].astype(jnp.bfloat16)
    grad_hidden_in = jnp.einsum(
        "rd,rf->df", expert_rows, pre_grad, preferred_element_type=jnp.float32
    )
    row_grad = slot_sums(pre_grad, full_in, 1)
    grad_in_shard, grad_out_shard = (grad_hidden_in, grad_hidden_out)
    back_grad = from_experts(
        row_grad.astype(jnp.bfloat16).reshape(senders, capacity, model_width)
    ).reshape(experts_all * capacity, model_width)
    normed_two_grad = (
        jnp.einsum("sr,sd->rd", select, back_grad, preferred_element_type=jnp.float32)
        .reshape(tok_dev, top_k, model_width)
        .sum(axis=1)
    )
    gate_delta = gates * (gate_grad - jnp.sum(gates * gate_grad, axis=1, keepdims=True))
    logit_grad = jnp.einsum("tk,tke->te", gate_delta, picks, precision=HIGHEST_PRECISION)
    router_grad = jnp.einsum(
        "td,te->de", normed_two.astype(jnp.float32), logit_grad, precision=HIGHEST_PRECISION
    )
    normed_two_grad = normed_two_grad + jnp.einsum(
        "te,de->td", logit_grad, router.astype(jnp.float32), precision=HIGHEST_PRECISION
    )
    gain_ffn_grad = jnp.sum(normed_two_grad * mixed_own * scale_two, axis=0)
    scaled_two = normed_two_grad * gain_ffn
    cubed_two = scale_two * scale_two * scale_two
    mixed_grad = (
        grad_rows
        + scale_two * scaled_two
        - mixed_own * cubed_two * jnp.mean(scaled_two * mixed_own, axis=1, keepdims=True)
    )
    mixed_whole = lax.all_gather(mixed_grad.astype(jnp.bfloat16), "tensor", axis=0, tiled=True)
    grad_w_out = jnp.einsum(
        "td,tf->df", mixed_whole, attended_rows, preferred_element_type=jnp.float32
    )
    attended_grad = jnp.einsum(
        "td,df->tf", mixed_whole, weights_out, preferred_element_type=jnp.float32
    ).astype(jnp.bfloat16)
    attended_grad = attended_grad.reshape(length, heads_dev, HDIM).transpose(1, 0, 2)
    again = jnp.exp(scores_of(query_rows, key_rows, bias_grid, allowed) - log_total)
    value_grad = jnp.einsum(
        "hij,hid->hjd",
        again.astype(jnp.bfloat16),
        attended_grad,
        preferred_element_type=jnp.float32,
    )
    prob_grad = jnp.einsum(
        "hid,hjd->hij", attended_grad, value_rows, preferred_element_type=jnp.float32
    )
    score_grad = (again * (prob_grad - jnp.sum(again * prob_grad, axis=2, keepdims=True))).astype(
        jnp.bfloat16
    )
    query_grad = jnp.einsum(
        "hij,hjd->hid", score_grad, key_rows, preferred_element_type=jnp.float32
    ) * HDIM ** (-0.5)
    key_grad = jnp.einsum(
        "hij,hid->hjd", score_grad, query_rows, preferred_element_type=jnp.float32
    ) * HDIM ** (-0.5)
    line_grad = diagonal_sums(score_grad.astype(jnp.float32))
    bias_own_grad = jnp.einsum("hn,nb->bh", line_grad, buckets, precision=HIGHEST_PRECISION)
    bias_grad = lax.dynamic_update_slice_in_dim(
        jnp.zeros((BUCKETS, HEADS), jnp.float32), bias_own_grad, piece_id * heads_dev, 1
    )
    proj_grad = jnp.stack([query_grad, key_grad, value_grad]).astype(jnp.bfloat16)
    proj_grad = proj_grad.transpose(2, 0, 1, 3).reshape(length, 3, head_cols)
    grad_w_qkv = jnp.einsum(
        "td,tcf->dcf", normed_one, proj_grad, preferred_element_type=jnp.float32
    )
    normed_one_grad = lax.psum_scatter(
        jnp.einsum("tcf,dcf->td", proj_grad, weights_qkv, preferred_element_type=jnp.float32),
        "tensor",
        scatter_dimension=0,
        tiled=True,
    )
    scale_own = lax.dynamic_slice_in_dim(scale_one, own_first, tok_dev, 0)
    scaled_one = normed_one_grad * gain_attn
    cubed_one = scale_own * scale_own * scale_own
    input_own = scale_own * scaled_one - own_rows * cubed_one * jnp.mean(
        scaled_one * own_rows, axis=1, keepdims=True
    )
    input_grad = (mixed_grad + input_own).astype(jnp.bfloat16)
    gain_attn_grad = jnp.sum(normed_one_grad * own_rows * scale_own, axis=0)
    grad_qkv_shard, grad_out_proj = (
        lax.psum_scatter(grad_w_qkv, "dp", scatter_dimension=0, tiled=True),
        lax.psum_scatter(grad_w_out, "dp", scatter_dimension=0, tiled=True),
    )
    summed = lax.psum((gain_attn_grad, gain_ffn_grad, router_grad, bias_grad), ("dp", "tensor"))
    return (
        result,
        input_grad,
        summed[0],
        grad_qkv_shard,
        grad_out_proj,
        summed[3],
        summed[1],
        summed[2],
        grad_in_shard[None],
        grad_out_shard[None],
    )


def solution(mesh):
    in_specs = (
        P(("dp", "tensor"), None),
        P("dp"),
        P(("dp", "tensor"), None),
        P(),
        P("dp", None, "tensor"),
        P("dp", "tensor"),
        P(),
        P(),
        P(),
        P("dp", None, "tensor"),
        P("dp", "tensor", None),
        P(("dp", "tensor"), None),
    )
    out_specs = (
        P(("dp", "tensor"), None),
        P(("dp", "tensor"), None),
        P(),
        P("dp", None, "tensor"),
        P("dp", "tensor"),
        P(),
        P(),
        P(),
        P("dp", None, "tensor"),
        P("dp", "tensor", None),
    )
    return jax.shard_map(body, mesh=mesh, in_specs=in_specs, out_specs=out_specs, check_vma=False)
```

profile of v0, /device:TPU:0, one launch (start us, length us, event | category | flops | bytes accessed | tf_op | source)
XLA Modules:
  0.0 625.5 jit_solution(15961776350656371197)
XLA Ops:
  12.7 35.2 %all_gather.20 = bf16[768,192]{1,0:T(8,128)(2,1)} all-gather(bf16[96,192]{1,0:T(8,128)(2,1)} %param.18), channel_id=1, replica_groups=mesh['dp'=8,'tensor'=4] {'dp'}, dimensions={0}, use_global_device_ids=true | all-gather | bytes 331776 | tf_op jit(solution)/shard_map/all_gather | solution.py:106
  47.9 8.8 %all_gather.18 = bf16[512,768]{1,0:T(8,128)(2,1)S(1)} all-gather(bf16[128,768]{1,0:T(8,128)(2,1)} %param.13), channel_id=1, replica_groups=mesh['dp'=8,'tensor'=4] {'tensor'}, dimensions={0}, use_global_device_ids=true | all-gather | bytes 983040 | tf_op jit(solution)/shard_map/all_gather | solution.py:111
  56.9 39.0 %all_gather.19 = bf16[768,3,192]{2,1,0:T(4,128)(2,1)S(1)} all-gather(bf16[96,3,192]{2,1,0:T(4,128)(2,1)S(1)} %copy.81), channel_id=1, replica_groups=mesh['dp'=8,'tensor'=4] {'dp'}, dimensions={0}, use_global_device_ids=true | all-gather | bytes 995328 | tf_op jit(solution)/shard_map/all_gather | solution.py:105
  104.3 7.1 %copy.111 = f32[1,3,512,1024]{3,1,2,0:T(4,128)S(1)} copy(f32[1,3,512,1024]{3,2,1,0:T(8,128)} %broadcast_bitcast_fusion) | data formatting | bytes 12582912
  115.7 13.2 %reshape.238 = f32[3,512,1023]{2,1,0:T(8,128)} reshape(f32[3,523776]{1,0:T(4,128)} %slice.49) | data formatting | bytes 12570624 | tf_op jit(solution)/shard_map/reshape | solution.py:29
  144.6 25.0 %reduce-scatter.7.cloned.1.call-done = f32[128,768]{1,0:T(8,128)} async-done(((f32[512,768]{1,0:T(8,128)}), f32[128,768]{1,0:T(8,128)}) %reduce-scatter.7.cloned.1.call-update) | async-done | bytes 393232 | tf_op jit(solution)/shard_map/reduce_scatter | solution.py:138
  173.8 22.0 %all_to_all.20 = bf16[8,48,768]{2,1,0:T(8,128)(2,1)} all-to-all(bf16[8,48,768]{2,1,0:T(8,128)(2,1)S(1)} %bitcast.149), channel_id=1, replica_groups=mesh['dp'=8,'tensor'=4] {'dp'}, dimensions={0} | all-to-all | bytes 1179648 | tf_op jit(solution)/shard_map/all_to_all | solution.py:58
  196.3 21.2 %all-gather.3.cloned.1.call-done = bf16[1536,768]{1,0:T(8,128)(2,1)} async-done(((bf16[384,768]{1,0:T(8,128)(2,1)}), bf16[1536,768]{1,0:T(8,128)(2,1)}) %all-gather.3.cloned.1.call-update) | async-done | bytes 2359312 | tf_op jit(solution)/shard_map/all_gather | solution.py:66
  228.8 48.0 %reduce-scatter.9.cloned.1.call-done = f32[384,768]{1,0:T(8,128)} async-done(((f32[1536,768]{1,0:T(8,128)}), f32[384,768]{1,0:T(8,128)}) %reduce-scatter.9.cloned.1.call-update) | async-done | bytes 1179664 | tf_op jit(solution)/shard_map/reduce_scatter | solution.py:70
  292.3 8.2 %all-to-all-done.1 = bf16[8,48,768]{2,1,0:T(8,128)(2,1)} async-done(((bf16[8,48,768]{2,1,0:T(8,128)(2,1)}), bf16[8,48,768]{2,1,0:T(8,128)(2,1)}, u32[]{:S(2)}, u32[]{:S(2)}) %all-to-all-start.1) | async-done | bytes 589856 | tf_op jit(solution)/shard_map/all_to_all | solution.py:62
  309.0 20.2 %all_to_all.21 = bf16[8,48,768]{2,1,0:T(8,128)(2,1)} all-to-all(bf16[8,48,768]{2,1,0:T(8,128)(2,1)S(1)} %bitcast.148), channel_id=1, replica_groups=mesh['dp'=8,'tensor'=4] {'dp'}, dimensions={0} | all-to-all | bytes 1179648 | tf_op jit(solution)/shard_map/all_to_all | solution.py:58
  329.5 21.5 %all-gather.5.cloned.1.call-done = bf16[1536,768]{1,0:T(8,128)(2,1)} async-done(((bf16[384,768]{1,0:T(8,128)(2,1)}), bf16[1536,768]{1,0:T(8,128)(2,1)}) %all-gather.5.cloned.1.call-update) | async-done | bytes 2359312 | tf_op jit(solution)/shard_map/all_gather | solution.py:66
  351.0 7.7 %fusion.6 = bf16[1536,768]{1,0:T(8,128)(2,1)S(1)} fusion(f32[1536,768]{1,0:T(8,128)} %copy-done.46, bf16[1536,768]{1,0:T(8,128)(2,1)} %all-gather.5.cloned.1.call-done, bf16[1,768,768]{2,1,0:T(8,128)(2,1)S(1)} %copy-done), kind=kOutput, calls=%fused_computation.8 | convolution fusion | flops 1835532288 | bytes 10616832 | tf_op jit(solution)/shard_map/rd,fd->rf/dot_general | solution.py:187
  364.4 47.9 %reduce-scatter.11.cloned.1.call-done = f32[384,768]{1,0:T(8,128)} async-done(((f32[1536,768]{1,0:T(8,128)}), f32[384,768]{1,0:T(8,128)}) %reduce-scatter.11.cloned.1.call-update) | async-done | bytes 1179664 | tf_op jit(solution)/shard_map/reduce_scatter | solution.py:70
  414.5 5.6 all-to-all-start.3
  421.9 14.1 %all-to-all-done.3 = bf16[8,48,768]{2,1,0:T(8,128)(2,1)S(1)} async-done(((bf16[8,48,768]{2,1,0:T(8,128)(2,1)}), bf16[8,48,768]{2,1,0:T(8,128)(2,1)S(1)}, u32[]{:S(2)}, u32[]{:S(2)}) %all-to-all-start.3) | async-done | bytes 589856 | tf_op jit(solution)/shard_map/all_to_all | solution.py:62
  438.0 7.7 %all_gather.23 = bf16[512,768]{1,0:T(8,128)(2,1)S(1)} all-gather(bf16[128,768]{1,0:T(8,128)(2,1)S(1)} %get-tuple-element.20), channel_id=1, replica_groups=mesh['dp'=8,'tensor'=4] {'tensor'}, dimensions={0}, use_global_device_ids=true | all-gather | bytes 983040 | tf_op jit(solution)/shard_map/all_gather | solution.py:220
  457.5 6.4 %convolution_bitcast_fusion.1 = f32[1,768,768]{2,1,0:T(8,128)} fusion(bf16[1536,768]{1,0:T(8,128)(2,1)} %all-gather.3.cloned.1.call-done, bf16[1536,768]{1,0:T(8,128)(2,1)} %copy-done.12), kind=kOutput, calls=%fused_computation.24 | convolution fusion | flops 1811939328 | bytes 7077888 | tf_op jit(solution)/shard_map/rd,rf->df/dot_general | solution.py:191
  464.0 6.3 %convolution_bitcast_fusion = f32[1,768,768]{2,1,0:T(8,128)} fusion(bf16[1536,768]{1,0:T(8,128)(2,1)S(1)} %copy-done.44, f32[1536,768]{1,0:T(8,128)} %copy-done.46), kind=kOutput, calls=%fused_computation.23 | convolution fusion | flops 1822556160 | bytes 9437184 | tf_op jit(solution)/shard_map/rf,rd->fd/dot_general | solution.py:184
  476.2 7.0 %reshape.268 = bf16[1571328]{0:T(1024)(128)(2,1)} reshape(bf16[3,512,1023]{2,1,0:T(8,128)(2,1)} %concatenate.10.clone) | data formatting | bytes 6285312
  483.2 5.5 reshape.253
  496.2 39.4 %all-reduce.2 = (f32[768]{0:T(1024)}, f32[32,12]{0,1:T(8,128)}, f32[768]{0:T(1024)}, f32[768,8]{0,1:T(8,128)}) all-reduce(f32[768]{0:T(1024)S(1)} %get-tuple-element.12, f32[32,12]{0,1:T(8,128)S(1)} %dynamic_update_slice.3, f32[768]{0:T(1024)S(1)} %get-tuple-element.10, ...), channel_id=1, replica_groups=mesh['dp'=8,'tensor'=4] {'dp','tensor'}, use_global_device_ids=true, to_apply=%region_21.22 | all-reduce | flops 8064 | bytes 64512 | tf_op jit(solution)/shard_map/psum | solution.py:275
  537.5 8.5 %reduce-scatter.17.cloned.1.call-done = f32[96,192]{1,0:T(8,128)} async-done(((f32[768,192]{1,0:T(8,128)}), f32[96,192]{1,0:T(8,128)}) %reduce-scatter.17.cloned.1.call-update) | async-done | bytes 73744 | tf_op jit(solution)/shard_map/reduce_scatter | solution.py:273
  546.0 72.4 %reduce-scatter.15.cloned.1.call-done = f32[96,3,192]{2,0,1:T(8,128)} async-done(((f32[768,3,192]{2,0,1:T(8,128)}), f32[96,3,192]{2,0,1:T(8,128)}) %reduce-scatter.15.cloned.1.call-update) | async-done | bytes 221200 | tf_op jit(solution)/shard_map/reduce_scatter | solution.py:272
  (206 shorter events, 112.4 us)
Async XLA Ops:
  7.2 216.5 %copy-start = (bf16[1,768,768]{2,1,0:T(8,128)(2,1)S(1)}, bf16[1,768,768]{2,1,0:T(8,128)(2,1)}, u32[]{:S(2)}) copy-start(bf16[1,768,768]{2,1,0:T(8,128)(2,1)} %param.23) | copy-start | bytes 3538948
  7.2 162.4 %reduce-scatter.7.cloned.1.call-start = ((), (), s32[]{:S(2)}) async-start(), calls=%async_computation.10 | async-start | bytes 1966080 | tf_op jit(solution)/shard_map/reduce_scatter | solution.py:138
  12.7 85.2 %copy-start.27 = (f32[768]{0:T(1024)S(1)}, f32[768]{0:T(1024)}, u32[]{:S(2)}) copy-start(f32[768]{0:T(1024)} %param.16) | copy-start | bytes 9220
  56.7 43.1 %copy-start.4 = (bf16[512,768]{1,0:T(8,128)(2,1)}, bf16[512,768]{1,0:T(8,128)(2,1)S(1)}, u32[]{:S(2)}) copy-start(bf16[512,768]{1,0:T(8,128)(2,1)S(1)} %all_gather.18) | copy-start | bytes 2359300
  143.1 74.3 %all-gather.3.cloned.1.call-start = ((), (), s32[]{:S(2)}) async-start(), calls=%async_computation.11 | async-start | bytes 2949120 | tf_op jit(solution)/shard_map/all_gather | solution.py:66
  144.6 76.9 %copy-start.34 = (s32[256]{0:T(256)}, s32[256]{0:T(256)S(1)}, u32[]{:S(2)}) copy-start(s32[256]{0:T(256)S(1)} %multiply_add_fusion) | copy-start | bytes 3076
  171.2 50.3 %copy-start.36 = (f32[128]{0:T(128)}, f32[128]{0:T(128)S(1)}, u32[]{:S(2)}) copy-start(f32[128]{0:T(128)S(1)} %get-tuple-element.28) | copy-start | bytes 1540
  171.3 117.8 %copy-start.10 = (bf16[128,768]{1,0:T(8,128)(2,1)}, bf16[128,768]{1,0:T(8,128)(2,1)S(1)}, u32[]{:S(2)}) copy-start(bf16[128,768]{1,0:T(8,128)(2,1)S(1)} %multiply_convert_fusion.4) | copy-start | bytes 589828
  195.8 81.0 %reduce-scatter.9.cloned.1.call-start = ((), (), s32[]{:S(2)}) async-start(), calls=%async_computation.12 | async-start | bytes 5898240 | tf_op jit(solution)/shard_map/reduce_scatter | solution.py:70
  279.0 21.5 %all-to-all-start.1 = ((bf16[8,48,768]{2,1,0:T(8,128)(2,1)}), bf16[8,48,768]{2,1,0:T(8,128)(2,1)}, u32[]{:S(2)}, u32[]{:S(2)}) async-start(bf16[8,48,768]{2,1,0:T(8,128)(2,1)} %bitcast.20), calls=%async_computation.3 | async-start | bytes 1179648 | tf_op jit(solution)/shard_map/all_to_all | solution.py:62
  284.5 66.5 %all-gather.5.cloned.1.call-start = ((), (), s32[]{:S(2)}) async-start(), calls=%async_computation.13 | async-start | bytes 2949120 | tf_op jit(solution)/shard_map/all_gather | solution.py:66
  329.3 83.0 %reduce-scatter.11.cloned.1.call-start = ((), (), s32[]{:S(2)}) async-start(), calls=%async_computation.14 | async-start | bytes 5898240 | tf_op jit(solution)/shard_map/reduce_scatter | solution.py:70
  364.3 55.9 %copy-start.29 = (f32[3,512]{1,0:T(4,128)S(1)}, f32[3,512]{1,0:T(4,128)}, u32[]{:S(2)}) copy-start(f32[3,512]{1,0:T(4,128)} %copy-done.28) | copy-start | bytes 18436
  364.3 56.8 %copy-start.39 = (f32[128]{0:T(128)S(1)}, f32[128]{0:T(128)}, u32[]{:S(2)}) copy-start(f32[128]{0:T(128)} %get-tuple-element.22) | copy-start | bytes 1540
  364.3 56.9 %copy-start.22 = (s32[128,2]{1,0:T(8,128)S(1)}, s32[128,2]{1,0:T(8,128)}, u32[]{:S(2)}) copy-start(s32[128,2]{1,0:T(8,128)} %copy-done.21) | copy-start | bytes 3076
  364.3 71.7 %copy-start.33 = (s32[128,2]{0,1:T(2,128)S(1)}, s32[128,2]{0,1:T(2,128)}, u32[]{:S(2)}) copy-start(s32[128,2]{0,1:T(2,128)} %multiply_add_fusion.1) | copy-start | bytes 3076
  364.3 72.1 %copy-start.25 = (bf16[768,8]{0,1:T(8,128)(2,1)S(1)}, bf16[768,8]{0,1:T(8,128)(2,1)}, u32[]{:S(2)}) copy-start(bf16[768,8]{0,1:T(8,128)(2,1)} %param.21) | copy-start | bytes 36868
  364.4 72.1 %copy-start.37 = (f32[128]{0:T(128)S(1)}, f32[128]{0:T(128)}, u32[]{:S(2)}) copy-start(f32[128]{0:T(128)} %copy-done.36) | copy-start | bytes 1540
  414.5 21.5 %all-to-all-start.3 = ((bf16[8,48,768]{2,1,0:T(8,128)(2,1)}), bf16[8,48,768]{2,1,0:T(8,128)(2,1)S(1)}, u32[]{:S(2)}, u32[]{:S(2)}) async-start(bf16[8,48,768]{2,1,0:T(8,128)(2,1)} %bitcast.25), calls=%async_computation.6 | async-start | bytes 1179648 | tf_op jit(solution)/shard_map/all_to_all | solution.py:62
  420.1 74.9 %reduce-scatter.13.cloned.1.call-start = ((), (), s32[]{:S(2)}) async-start(), calls=%async_computation.15 | async-start | bytes 1966080 | tf_op jit(solution)/shard_map/reduce_scatter | solution.py:257
  452.2 93.8 %reduce-scatter.17.cloned.1.call-start = ((), (), s32[]{:S(2)}) async-start(), calls=%async_computation.17 | async-start | bytes 884736 | tf_op jit(solution)/shard_map/reduce_scatter | solution.py:273
  453.6 164.8 %reduce-scatter.15.cloned.1.call-start = ((), (), s32[]{:S(2)}) async-start(), calls=%async_computation.16 | async-start | bytes 2654208 | tf_op jit(solution)/shard_map/reduce_scatter | solution.py:272
  492.5 43.1 %copy-start.14 = (f32[128,768]{1,0:T(8,128)S(1)}, f32[128,768]{1,0:T(8,128)}, u32[]{:S(2)}) copy-start(f32[128,768]{1,0:T(8,128)} %get-tuple-element.21) | copy-start | bytes 1179652
  492.6 125.9 %copy-start.1 = (bf16[1,768,768]{2,1,0:T(8,128)(2,1)S(1)}, bf16[1,768,768]{2,1,0:T(8,128)(2,1)}, u32[]{:S(2)}) copy-start(bf16[1,768,768]{2,1,0:T(8,128)(2,1)} %param.23) | copy-start | bytes 3538948
  (34 other events, 308.4 us)
Sparse Core Ops, SparseCore 0:
  143.3 26.2 reduce-scatter.6
  195.9 21.5 all-gather.2
  228.9 47.8 reduce-scatter.8
  329.4 21.5 all-gather.4
  364.4 47.8 reduce-scatter.10
  452.3 27.2 reduce-scatter.12
  483.4 62.5 reduce-scatter.16
  550.4 67.9 reduce-scatter.14
where the time goes:
time: 633 us; the launch traced here: 625 us
  waiting for transfers between devices  267 us (42%)
  blocking collectives  172 us (27%)
  local copies, waits for them, and re-layouts  74.6 us (12%)
  matrix products  63.9 us (10%)
  other arithmetic  20.6 us (3%)
  between operations  15.1 us (2%)
  starting transfers between devices  12.1 us (2%)
    reduce_scatter x2, waiting for transfers between devices, slot_sums(): lax.psum_scatter(lax.dot_general(left, right, (((1,), (contract,)), ((),...  95.9 us
    reduce_scatter x1, waiting for transfers between devices, body(): lax.psum_scatter(grad_w_qkv, 'dp', scatter_dimension=0, tiled=True)  72.4 us
    all_gather x2, waiting for transfers between devices, spread_rows(): return lax.all_gather(slot_block, 'tensor', axis=0, tiled=True)  42.7 us
    all_to_all x2, blocking collectives, to_experts(): lax.all_to_all(slot_block, 'dp', split_axis=0, concat_axis=0, tiled=True)  42.2 us
    psum x1, blocking collectives, body(): lax.psum((gain_attn_grad, gain_ffn_grad, router_grad, bias_grad), ('dp',...  39.4 us
    all_gather x1, blocking collectives, body(): lax.all_gather(w_qkv, 'dp', axis=0, tiled=True)  39 us
    all_gather x1, blocking collectives, body(): lax.all_gather(w_out, 'dp', axis=0, tiled=True)  35.2 us
    unnamed x104, local copies, waits for them, and re-layouts  32.1 us
  transfers between devices with their start and end apart: 10, of which 9 were waited for; matrix products, arithmetic and copies ran while one was open for 9% of the time, Pallas kernels for 0%

commit v1 on v0

v1 whole, which is shorter than its diff:
```python
import functools

import jax
import jax.numpy as jnp
import numpy as np
from jax import lax
from jax.experimental import pallas as pl
from jax.experimental.pallas import tpu as pltpu
from jax.sharding import PartitionSpec as P

HEADS = 12
HDIM = 64
BUCKETS = 32
ROWS = 128
GATE_LANES = 128

LIMITS = np.array([19, 21, 24, 27, 31, 35, 40, 46, 52, 59, 67, 77, 87, 99, 113], np.int32)
HIGHEST = lax.Precision.HIGHEST
F32 = jnp.float32
BF16 = jnp.bfloat16
VMEM_BYTES = 48 * 1024 * 1024

NN = (((1,), (0,)), ((), ()))
NT = (((1,), (1,)), ((), ()))
TN = (((0,), (0,)), ((), ()))


def dot(left, right, dims=NN, precision=None):
    return lax.dot_general(left, right, dims, preferred_element_type=F32, precision=precision)


def iota(shape, axis):
    return lax.broadcasted_iota(jnp.int32, shape, axis)


def bucket_of(distance):
    bucket = jnp.minimum(distance, 16)
    for limit in LIMITS:
        bucket = bucket + (distance >= int(limit)).astype(jnp.int32)
    return bucket


def in_three(value):
    high = value.astype(BF16)
    rest = value - high.astype(F32)
    middle = rest.astype(BF16)
    low = (rest - middle.astype(F32)).astype(BF16)
    return high, middle, low


def three_lanes(value):
    high, middle, low = in_three(value)
    lane = iota((value.shape[0], GATE_LANES), 1)
    zero = jnp.zeros((value.shape[0], GATE_LANES), F32)
    spread = jnp.where(
        lane == 0,
        high.astype(F32),
        jnp.where(lane == 1, middle.astype(F32), jnp.where(lane == 2, low.astype(F32), zero)),
    )
    return spread.astype(BF16)


def lanes_sum(lanes):
    return jnp.sum(lanes.astype(F32), axis=1, keepdims=True)


def pick(columns, at):
    return columns[:, at : at + 1]


def call(kernel, outs, scratch, args, smem=0, flops=0, name=None):
    spec_vmem = pl.BlockSpec(memory_space=pltpu.VMEM)
    spec_smem = pl.BlockSpec(memory_space=pltpu.SMEM)
    moved = sum(a.size * a.dtype.itemsize for a in list(args) + list(outs))
    return pl.pallas_call(
        kernel,
        out_shape=[jax.ShapeDtypeStruct(o.shape, o.dtype) for o in outs],
        in_specs=[spec_smem] * smem + [spec_vmem] * (len(args) - smem),
        out_specs=[spec_vmem] * len(outs),
        scratch_shapes=scratch,
        compiler_params=pltpu.CompilerParams(vmem_limit_bytes=VMEM_BYTES),
        cost_estimate=pl.CostEstimate(flops=flops, bytes_accessed=moved, transcendentals=0),
        name=name,
    )(*args)


def struct(shape, dtype):
    return jax.ShapeDtypeStruct(shape, dtype)


def slots_kernel(capacity, routes_ref, grad_ref, slot_ref, out_ref):
    tokens = routes_ref.shape[0]
    slots = out_ref.shape[0]
    experts = slots // capacity
    routes = routes_ref[...]
    first, second = routes[:, 0:1], routes[:, 1:2]
    lane = iota((tokens, experts), 1)
    one_first = (first == lane).astype(F32)
    one_second = (second == lane).astype(F32)
    member = (one_first + one_second).astype(BF16)
    below = (iota((tokens, tokens), 1) < iota((tokens, tokens), 0)).astype(F32).astype(BF16)
    earlier = dot(below, member)
    slot_first = first * capacity + jnp.sum(one_first * earlier, axis=1, keepdims=True).astype(
        jnp.int32
    )
    slot_second = second * capacity + jnp.sum(one_second * earlier, axis=1, keepdims=True).astype(
        jnp.int32
    )
    wide = iota((tokens, 128), 1)
    slot_ref[...] = jnp.where(wide == 0, slot_first, slot_second)
    places = iota((tokens, slots), 1)
    chosen = ((slot_first == places) | (slot_second == places)).astype(F32).astype(BF16)
    out_ref[...] = dot(chosen, grad_ref[...], TN).astype(BF16)


def bias_tiles(rel_ref, first_head, heads):
    column = iota((8, 256), 1)
    distance = (ROWS - column) & 255
    bucket = bucket_of(distance)
    tiles = []
    for head in range(heads):
        line = jnp.zeros((8, 256), F32)
        for b in range(BUCKETS):
            line = jnp.where(bucket == b, rel_ref[b, first_head + head], line)
        wide = jnp.broadcast_to(line[0:1, :], (ROWS, 256))
        tiles.append(pltpu.roll(wide, 0, 1, stride=1, stride_axis=0))
    return tiles


def masked_scores(query, keys, tile, far, starts, block):
    width = (block + 1) * ROWS
    raw = dot(query, keys, NT) * HDIM**-0.5
    if block == 0:
        bias = tile[:, ROWS:]
    elif block == 1:
        bias = tile
    else:
        bias = jnp.concatenate([jnp.full((ROWS, width - 2 * ROWS), far, F32), tile], axis=1)
    column = iota((ROWS, width), 1)
    row = iota((ROWS, width), 0) + block * ROWS
    allowed = (column <= row) & (column >= starts)
    return jnp.where(allowed, raw + bias, -1e9)


def forward_kernel(parts, pieces, heads, *refs):
    place_ref, start_ref, rel_ref = refs[:3]
    weights = refs[3 : 3 + parts]
    rows = refs[3 + parts : 3 + parts + pieces]
    gain_ref, doc_ref = refs[3 + parts + pieces : 5 + parts + pieces]
    weight_out, row_out, proj_out, att_out, lse_out, keep_out, send_out = refs[
        5 + parts + pieces : 12 + parts + pieces
    ]
    piece = place_ref[1]
    cols = heads * HDIM
    for at in range(parts):
        depth = weights[at].shape[0]
        weight_out[pl.ds(pl.multiple_of(start_ref[at], 16), depth), :] = weights[at][...]
    for at in range(pieces):
        row_out[pl.ds(pl.multiple_of((piece ^ at) * ROWS, ROWS), ROWS), :] = rows[at][...]
    x = row_out[...].astype(F32)
    scale = lax.rsqrt(jnp.mean(x * x, axis=1, keepdims=True) + 1e-6)
    normed = (x * scale * gain_ref[...]).astype(BF16)
    proj_out[...] = dot(normed, weight_out[:, : 3 * cols]).astype(BF16)
    tiles = bias_tiles(rel_ref, piece * heads, heads)
    blocks = x.shape[0] // ROWS
    proj = proj_out[...]
    wide = iota((ROWS, 128), 1)
    for block in range(blocks):
        here = slice(block * ROWS, (block + 1) * ROWS)
        upto = slice(0, (block + 1) * ROWS)
        starts = doc_ref[here, :]
        done = []
        kept = jnp.zeros((ROWS, 128), F32)
        for head in range(heads):
            at = head * HDIM
            query = proj[here, at : at + HDIM]
            keys = proj[upto, cols + at : cols + at + HDIM]
            values = proj[upto, 2 * cols + at : 2 * cols + at + HDIM]
            far = rel_ref[BUCKETS - 1, piece * heads + head]
            scores = masked_scores(query, keys, tiles[head], far, starts, block)
            peak = jnp.max(scores, axis=1, keepdims=True)
            shifted = jnp.exp(scores - peak)
            total = jnp.sum(shifted, axis=1, keepdims=True)
            attention = (shifted * (1.0 / total)).astype(BF16)
            done.append(dot(attention, values).astype(BF16))
            kept = jnp.where(wide == head, peak + jnp.log(total), kept)
        att_out[here, :] = jnp.concatenate(done, axis=1)
        lse_out[here, :] = kept
    weight_last = weight_out[:, 3 * cols :]
    for at in range(pieces):
        mine = att_out[pl.ds(pl.multiple_of((piece ^ at) * ROWS, ROWS), ROWS), :]
        product = dot(mine, weight_last, NT)
        if at % 2 == 0:
            keep_out[at // 2] = product
        else:
            send_out[at // 2] = product.astype(BF16)


def dispatch_kernel(
    own_ref,
    part_ref,
    near_ref,
    far_ref,
    gain_ref,
    router_ref,
    routes_ref,
    slot_ref,
    mixed_ref,
    normed_ref,
    gates_ref,
    out_ref,
):
    width = own_ref.shape[1]
    tokens = own_ref.shape[0]
    slots = out_ref.shape[0]
    mixed = own_ref[...].astype(F32) + (
        part_ref[...] + near_ref[...].astype(F32) + far_ref[...].astype(F32)
    )
    mixed_ref[...] = mixed
    scale = lax.rsqrt(jnp.mean(mixed * mixed, axis=1, keepdims=True) + 1e-6)
    normed = (mixed * scale * gain_ref[...]).astype(BF16)
    normed_ref[...] = normed
    logits = dot(normed, router_ref[...])
    routes = routes_ref[...]
    lane = iota(logits.shape, 1)
    one = jnp.sum(jnp.where(routes[:, 0:1] == lane, logits, 0.0), axis=1, keepdims=True)
    two = jnp.sum(jnp.where(routes[:, 1:2] == lane, logits, 0.0), axis=1, keepdims=True)
    peak = jnp.maximum(one, two)
    one, two = jnp.exp(one - peak), jnp.exp(two - peak)
    total = one + two
    one, two = one / total, two / total
    wide = iota((tokens, 128), 1)
    gates_ref[...] = jnp.where(wide == 0, one, two)
    places = iota((tokens, slots), 1)
    slot = slot_ref[...]
    first = (slot[:, 0:1] == places).astype(F32).astype(BF16)
    second = (slot[:, 1:2] == places).astype(F32).astype(BF16)
    out_ref[:, :width] = dot(first + second, normed, TN).astype(BF16)
    gate_slots = dot(first, three_lanes(one), TN) + dot(second, three_lanes(two), TN)
    out_ref[:, width:] = gate_slots.astype(BF16)


def gelu_and_slope(x):
    inner = 0.7978845608028654 * (x + 0.044715 * (x * x * x))
    bend = jnp.tanh(inner)
    half = 0.5 * (1.0 + bend)
    slope = half + 0.5 * x * (1.0 - bend * bend) * (
        0.7978845608028654 * (1.0 + 3 * 0.044715 * (x * x))
    )
    return x * half, slope


def expert_kernel(
    own_ref,
    mate_ref,
    in_one,
    in_two,
    back_one,
    back_two,
    hidden_one,
    hidden_two,
    slope_one,
    slope_two,
    keep_ref,
    send_ref,
    total,
    gate_total,
):
    step = pl.program_id(0)
    rows = own_ref.shape[0]
    width = in_one.shape[0]

    @pl.when(step == 0)
    def _():
        total[...] = jnp.zeros_like(total)
        gate_total[...] = jnp.zeros_like(gate_total)

    for side, source in enumerate((own_ref, mate_ref)):
        here = slice(side * rows, (side + 1) * rows)
        slot_rows = source[:, :width]
        gate = lanes_sum(source[:, width:])
        for weights, back, hidden_out, slope_out in (
            (in_one, back_one, hidden_one, slope_one),
            (in_two, back_two, hidden_two, slope_two),
        ):
            pre = dot(slot_rows, weights[...])
            hidden, slope = gelu_and_slope(pre)
            hidden = hidden.astype(BF16)
            pulled = back[here, :]
            pre_grad = (pulled * gate * slope).astype(BF16)
            hidden_out[here, :] = hidden
            slope_out[here, :] = pre_grad
            total[here, :] += dot(pre_grad, weights[...], NT)
            gate_total[here, :] += jnp.sum(hidden.astype(F32) * pulled, axis=1, keepdims=True)

    @pl.when(step == pl.num_programs(0) - 1)
    def _():
        keep_ref[:, :width] = total[:rows, :]
        keep_ref[:, width:] = gate_total[:rows, :]
        send_ref[:, :width] = total[rows:, :].astype(BF16)
        send_ref[:, width:] = three_lanes(gate_total[rows:, 0:1])


def run_experts(own, mate, in_one, in_two, back_one, back_two):
    rows, payload = own.shape
    width, hidden = in_one.shape
    tile = 256
    steps = hidden // tile
    whole = lambda shape: pl.BlockSpec(shape, lambda i: (0, 0))
    column = lambda height: pl.BlockSpec((height, tile), lambda i: (0, i))
    return pl.pallas_call(
        expert_kernel,
        grid=(steps,),
        in_specs=[whole((rows, payload))] * 2 + [column(width)] * 2 + [column(2 * rows)] * 2,
        out_specs=[column(2 * rows)] * 4 + [whole((rows, payload))] * 2,
        out_shape=[struct((2 * rows, hidden), BF16)] * 4
        + [struct((rows, payload), F32), struct((rows, payload), BF16)],
        scratch_shapes=[
            pltpu.VMEM((2 * rows, width), F32),
            pltpu.VMEM((2 * rows, GATE_LANES), F32),
        ],
        compiler_params=pltpu.CompilerParams(vmem_limit_bytes=VMEM_BYTES),
        cost_estimate=pl.CostEstimate(
            flops=8 * 2 * rows * width * hidden, bytes_accessed=16 << 20, transcendentals=0
        ),
        name="experts",
    )(own, mate, in_one, in_two, back_one, back_two)


def merge_kernel(keep_ref, mate_ref, out_ref):
    width = keep_ref.shape[1] - GATE_LANES
    out_ref[:, :width] = (keep_ref[:, :width] + mate_ref[:, :width].astype(F32)).astype(BF16)
    gate = keep_ref[:, width : width + 1] + lanes_sum(mate_ref[:, width:])
    out_ref[:, width:] = three_lanes(gate)


def combine_kernel(
    back_ref,
    slot_ref,
    gates_ref,
    mixed_ref,
    normed_ref,
    router_ref,
    routes_ref,
    grad_ref,
    gain_ref,
    mixed_grad_ref,
    low_ref,
    sums_ref,
):
    tokens, width = grad_ref.shape
    slots = back_ref.shape[0]
    experts = router_ref.shape[1]
    places = iota((tokens, slots), 1)
    slot = slot_ref[...]
    first = (slot[:, 0:1] == places).astype(F32).astype(BF16)
    second = (slot[:, 1:2] == places).astype(F32).astype(BF16)
    lanes = back_ref[:, width:]
    pull_one = jnp.sum(dot(first, lanes), axis=1, keepdims=True)
    pull_two = jnp.sum(dot(second, lanes), axis=1, keepdims=True)
    one, two = gates_ref[:, 0:1], gates_ref[:, 1:2]
    mean_pull = one * pull_one + two * pull_two
    delta_one = one * (pull_one - mean_pull)
    delta_two = two * (pull_two - mean_pull)
    routes = routes_ref[...]
    lane = iota((tokens, experts), 1)
    logit_grad = jnp.where(routes[:, 0:1] == lane, delta_one, 0.0) + jnp.where(
        routes[:, 1:2] == lane, delta_two, 0.0
    )
    high = logit_grad.astype(BF16)
    low = (logit_grad - high.astype(F32)).astype(BF16)
    normed = normed_ref[...]
    router = router_ref[...]
    normed_grad = dot(first + second, back_ref[:, :width]) + (
        dot(high, router, NT) + dot(low, router, NT)
    )
    mixed = mixed_ref[...]
    grad = grad_ref[...].astype(F32)
    scale = lax.rsqrt(jnp.mean(mixed * mixed, axis=1, keepdims=True) + 1e-6)
    scaled = normed_grad * gain_ref[...]
    cubed = scale * scale * scale
    mixed_grad = (
        grad
        + scale * scaled
        - mixed * cubed * jnp.mean(scaled * mixed, axis=1, keepdims=True)
    )
    mixed_grad_ref[...] = mixed_grad
    low_ref[...] = mixed_grad.astype(BF16)
    sums_ref[...] = jnp.zeros_like(sums_ref)
    sums_ref[:experts, :] = dot(high, normed, TN) + dot(low, normed, TN)
    sums_ref[experts : experts + 1, :] = jnp.sum(
        normed_grad * mixed * scale, axis=0, keepdims=True
    )


def result_kernel(back_ref, slot_ref, gates_ref, mixed_ref, out_ref):
    tokens = mixed_ref.shape[0]
    slots = back_ref.shape[0]
    places = iota((tokens, slots), 1)
    slot = slot_ref[...]
    first = (slot[:, 0:1] == places).astype(F32).astype(BF16)
    second = (slot[:, 1:2] == places).astype(F32).astype(BF16)
    back = back_ref[...]
    added = gates_ref[:, 0:1] * dot(first, back) + gates_ref[:, 1:2] * dot(second, back)
    out_ref[...] = (mixed_ref[...] + added).astype(BF16)


def backward_kernel(parts, pieces, heads, *refs):
    place_ref, start_ref, rel_ref = refs[:3]
    lows = refs[3 : 3 + pieces]
    weight_ref, row_ref, proj_ref, att_ref, lse_ref, gain_ref, doc_ref = refs[
        3 + pieces : 10 + pieces
    ]
    outs = refs[10 + pieces :]
    if parts > 1:
        grad_keep, grad_send, keep_out, send_out, sums_out, mixed, grad_proj, normed_grad, grads = outs
    else:
        grad_keep, keep_out, send_out, sums_out, mixed, grad_proj, normed_grad = outs
    piece = place_ref[1]
    cols = heads * HDIM
    for at in range(pieces):
        mixed[pl.ds(pl.multiple_of((piece ^ at) * ROWS, ROWS), ROWS), :] = lows[at][...]
    weight_last = weight_ref[:, 3 * cols :]
    att_grad = dot(mixed[...], weight_last).astype(BF16)
    grad_last = dot(mixed[...], att_ref[...], TN)
    tiles = bias_tiles(rel_ref, piece * heads, heads)
    proj = proj_ref[...]
    length = proj.shape[0]
    blocks = length // ROWS
    bucket_wide = bucket_of(jnp.maximum(ROWS + iota((ROWS, 256), 0) - iota((ROWS, 256), 1), 0))
    target = iota((8, HEADS * BUCKETS), 1)
    bias_row = jnp.zeros((8, HEADS * BUCKETS), F32)
    grads_q, grads_k, grads_v = [], [], []
    for head in range(heads):
        at = head * HDIM
        far = rel_ref[BUCKETS - 1, piece * heads + head]
        key_sum = [jnp.zeros((ROWS, HDIM), F32) for _ in range(blocks)]
        value_sum = [jnp.zeros((ROWS, HDIM), F32) for _ in range(blocks)]
        near_sum = jnp.zeros((ROWS, 256), F32)
        far_sum = jnp.zeros((ROWS, ROWS), F32)
        query_done = []
        for block in range(blocks):
            here = slice(block * ROWS, (block + 1) * ROWS)
            upto = slice(0, (block + 1) * ROWS)
            query = proj[here, at : at + HDIM]
            keys = proj[upto, cols + at : cols + at + HDIM]
            values = proj[upto, 2 * cols + at : 2 * cols + at + HDIM]
            out_grad = att_grad[here, at : at + HDIM]
            scores = masked_scores(query, keys, tiles[head], far, doc_ref[here, :], block)
            again = jnp.exp(scores - lse_ref[here, head : head + 1])
            prob_grad = dot(out_grad, values, NT)
            weighted = again * prob_grad
            score_grad = weighted - again * jnp.sum(weighted, axis=1, keepdims=True)
            score_low = score_grad.astype(BF16)
            value_add = dot(again.astype(BF16), out_grad, TN)
            key_add = dot(score_low, query, TN)
            for other in range(block + 1):
                there = slice(other * ROWS, (other + 1) * ROWS)
                key_sum[other] = key_sum[other] + key_add[there, :]
                value_sum[other] = value_sum[other] + value_add[there, :]
                if other < block - 1:
                    far_sum = far_sum + score_grad[:, there]
            if block == 0:
                near_sum = near_sum + jnp.concatenate(
                    [jnp.zeros((ROWS, ROWS), F32), score_grad], axis=1
                )
            else:
                near_sum = near_sum + score_grad[:, (block - 1) * ROWS :]
            query_done.append(dot(score_low, keys) * HDIM**-0.5)
        grads_q.append(jnp.concatenate(query_done, axis=0))
        grads_k.append(jnp.concatenate(key_sum, axis=0) * HDIM**-0.5)
        grads_v.append(jnp.concatenate(value_sum, axis=0))
        first_lane = (piece * heads + head) * BUCKETS
        for b in range(BUCKETS):
            amount = jnp.sum(jnp.where(bucket_wide == b, near_sum, 0.0))
            if b == BUCKETS - 1:
                amount = amount + jnp.sum(far_sum)
            bias_row = bias_row + jnp.where(target == first_lane + b, amount, 0.0)
    grad_proj[...] = jnp.concatenate(grads_q + grads_k + grads_v, axis=1).astype(BF16)
    x = row_ref[...].astype(F32)
    scale = lax.rsqrt(jnp.mean(x * x, axis=1, keepdims=True) + 1e-6)
    unit = x * scale
    normed = (unit * gain_ref[...]).astype(BF16)
    grad_first = dot(normed, grad_proj[...], TN)
    if parts > 1:
        depth = grad_first.shape[0] // parts
        grads[:, : 3 * cols] = grad_first
        grads[:, 3 * cols :] = grad_last
        for at in range(parts):
            piece_rows = grads[pl.ds(pl.multiple_of(start_ref[at], 16), depth), :]
            if at % 2 == 0:
                grad_keep[at // 2] = piece_rows
            else:
                grad_send[at // 2] = piece_rows.astype(BF16)
    else:
        grad_keep[:, : 3 * cols] = grad_first
        grad_keep[:, 3 * cols :] = grad_last
    normed_grad[...] = dot(grad_proj[...], weight_ref[:, : 3 * cols], NT)
    sums_out[...] = jnp.zeros_like(sums_out)
    sums_out[0:1, :] = jnp.sum(normed_grad[...] * unit, axis=0, keepdims=True)
    sums_out[1:2, : HEADS * BUCKETS] = bias_row[0:1, :]
    for at in range(pieces):
        mine = normed_grad[pl.ds(pl.multiple_of((piece ^ at) * ROWS, ROWS), ROWS), :]
        if at % 2 == 0:
            keep_out[at // 2] = mine
        else:
            send_out[at // 2] = mine.astype(BF16)


def input_kernel(own_ref, gain_ref, mixed_grad_ref, part_ref, near_ref, far_ref, out_ref):
    x = own_ref[...].astype(F32)
    scale = lax.rsqrt(jnp.mean(x * x, axis=1, keepdims=True) + 1e-6)
    scaled = (
        part_ref[...] + near_ref[...].astype(F32) + far_ref[...].astype(F32)
    ) * gain_ref[...]
    cubed = scale * scale * scale
    own = scale * scaled - x * cubed * jnp.mean(scaled * x, axis=1, keepdims=True)
    out_ref[...] = (mixed_grad_ref[...] + own).astype(BF16)


def swap(value, axis, size, mask):
    return lax.ppermute(value, axis, [(i, i ^ mask) for i in range(size)])


def gather_weights(shard, senders):
    mine = lax.axis_index("dp")
    depth = shard.shape[0]
    if senders != 8:
        return [lax.all_gather(shard, "dp", axis=0, tiled=True)], jnp.zeros((1,), jnp.int32)
    parts = {0: shard}
    parts[1] = swap(shard, "dp", senders, 1)
    for mask in (2, 4, 6):
        parts[mask] = swap(shard, "dp", senders, mask)
    for mask in (2, 4, 6):
        parts[mask + 1] = swap(parts[mask], "dp", senders, 1)
    starts = (mine ^ jnp.arange(senders, dtype=jnp.int32)) * depth
    return [parts[i] for i in range(senders)], starts


def scatter_grads(keep, send, senders):
    if senders != 8:
        return lax.psum_scatter(keep, "dp", scatter_dimension=0, tiled=True)
    halves = {}
    for at in (3, 2, 1, 0):
        near = swap(send[at], "dp", senders, 1)
        halves[at] = keep[at] + near.astype(F32)
    total = halves[0]
    arrived = [swap(halves[at].astype(BF16), "dp", senders, 2 * at) for at in (3, 2, 1)]
    for part in arrived:
        total = total + part.astype(F32)
    return total


def scatter_rows(keep, send, pieces):
    near = swap(send, "tensor", pieces, 1)
    other = (keep[1] + near[1].astype(F32)).astype(BF16)
    return keep[0], near[0], swap(other, "tensor", pieces, 2)


def gather_rows(rows, pieces):
    far = swap(rows, "tensor", pieces, 2)
    near = swap(rows, "tensor", pieces, 1)
    last = swap(far, "tensor", pieces, 1)
    return [rows, near, far, last]


def to_all(value, senders, pieces):
    if senders != 8:
        return lax.psum(value, ("dp", "tensor"))
    for axis, size in (("tensor", pieces), ("dp", senders)):
        mask = 1
        while mask < size:
            value = value + swap(value, axis, size, mask)
            mask *= 2
    return value


def exchange(blocks, senders, capacity):
    rows, width = blocks.shape
    return lax.all_to_all(
        blocks.reshape(senders, capacity, width), "dp", split_axis=0, concat_axis=0, tiled=True
    ).reshape(rows, width)


def body(
    tokens,
    doc_start,
    routes,
    gain_attn,
    w_qkv,
    w_out,
    rel_bias,
    gain_ffn,
    router,
    w_in,
    w_exp_out,
    out_grad,
):
    pieces = lax.axis_size("tensor")
    senders = lax.axis_size("dp")
    tok_dev, width = tokens.shape
    length = tok_dev * pieces
    experts = router.shape[1]
    capacity = max(2, 3 * tok_dev * routes.shape[1] // (2 * experts))
    slots = experts * capacity
    heads = w_out.shape[1] // HDIM
    cols = heads * HDIM
    place = jnp.stack([lax.axis_index("dp"), lax.axis_index("tensor")]).astype(jnp.int32)
    gain_one = gain_attn.reshape(1, width)
    gain_two = gain_ffn.reshape(1, width)
    doc_column = doc_start.reshape(length, 1)

    shard = jnp.concatenate([w_qkv.reshape(w_qkv.shape[0], 3 * cols), w_out], axis=1)
    weights, starts = gather_weights(shard, senders)
    rows = gather_rows(tokens, pieces)
    in_one, out_one = w_in[0], w_exp_out[0]
    in_two = swap(in_one, "tensor", pieces, 2)
    out_two = swap(out_one, "tensor", pieces, 2)

    slot, grad_out = call(
        functools.partial(slots_kernel, capacity),
        [struct((tok_dev, 128), jnp.int32), struct((slots, width), BF16)],
        [],
        [routes, out_grad],
        flops=2 * slots * tok_dev * width,
        name="slots",
    )

    whole_weight, whole_rows, projected, attended, lse, keep, send = call(
        functools.partial(forward_kernel, len(weights), pieces, heads),
        [
            struct((width, 4 * cols), BF16),
            struct((length, width), BF16),
            struct((length, 3 * cols), BF16),
            struct((length, cols), BF16),
            struct((length, 128), F32),
            struct((pieces // 2, tok_dev, width), F32),
            struct((pieces // 2, tok_dev, width), BF16),
        ],
        [],
        [place, starts, rel_bias] + weights + rows + [gain_one, doc_column],
        smem=3,
        flops=2 * length * width * 4 * cols + 4 * heads * length * length * HDIM,
        name="attend",
    )
    grad_rows = exchange(grad_out, senders, capacity)
    grad_both = jnp.concatenate([grad_rows, swap(grad_rows, "tensor", pieces, 1)], axis=0)
    back_one = dot(grad_both, out_one, NT)
    back_two = dot(grad_both, out_two, NT)

    part, near, far = scatter_rows(keep, send, pieces)
    mixed, normed_two, gates, outgoing = call(
        dispatch_kernel,
        [
            struct((tok_dev, width), F32),
            struct((tok_dev, width), BF16),
            struct((tok_dev, 128), F32),
            struct((slots, width + GATE_LANES), BF16),
        ],
        [],
        [tokens, part, near, far, gain_two, router, routes, slot],
        flops=2 * slots * tok_dev * width,
        name="dispatch",
    )
    slot_own = exchange(outgoing, senders, capacity)
    slot_mate = swap(slot_own, "tensor", pieces, 1)
    hidden_one, hidden_two, pre_one, pre_two, row_keep, row_send = run_experts(
        slot_own, slot_mate, in_one, in_two, back_one, back_two
    )
    row_mate = swap(row_send, "tensor", pieces, 1)
    (row_out,) = call(
        merge_kernel,
        [struct((slots, width + GATE_LANES), BF16)],
        [],
        [row_keep, row_mate],
        name="merge",
    )
    back = exchange(row_out, senders, capacity)

    slot_rows = jnp.concatenate([slot_own[:, :width], slot_mate[:, :width]], axis=0)
    gate_lanes = jnp.concatenate([slot_own[:, width:], slot_mate[:, width:]], axis=0)
    slot_gates = jnp.sum(gate_lanes.astype(F32), axis=1, keepdims=True)
    route_grad = (slot_gates * grad_both.astype(F32)).astype(BF16)
    partial_out = dot(hidden_one, out_one) + dot(hidden_two, out_two)
    out_mate = swap(partial_out[slots:].astype(BF16), "tensor", pieces, 1)
    expert_out = (partial_out[:slots] + out_mate.astype(F32)).astype(BF16)
    grad_out_two = swap(dot(hidden_two, route_grad, TN).astype(BF16), "tensor", pieces, 2)
    grad_in_two = swap(dot(slot_rows, pre_two, TN).astype(BF16), "tensor", pieces, 2)
    grad_out_sum = dot(hidden_one, route_grad, TN) + grad_out_two.astype(F32)
    grad_in_sum = dot(slot_rows, pre_one, TN) + grad_in_two.astype(F32)

    sum_rows = -(-(experts + 1) // 8) * 8
    mixed_grad, mixed_low, sums_two = call(
        combine_kernel,
        [
            struct((tok_dev, width), F32),
            struct((tok_dev, width), BF16),
            struct((sum_rows, width), F32),
        ],
        [],
        [back, slot, gates, mixed, normed_two, router, routes, out_grad, gain_two],
        flops=2 * slots * tok_dev * width,
        name="combine",
    )
    returned = exchange(expert_out, senders, capacity)
    (result,) = call(
        result_kernel,
        [struct((tok_dev, width), BF16)],
        [],
        [returned, slot, gates, mixed],
        flops=4 * slots * tok_dev * width,
        name="result",
    )

    lows = gather_rows(mixed_low, pieces)
    parts = len(weights)
    if parts > 1:
        grad_outs = [
            struct((parts // 2, width // parts, 4 * cols), F32),
            struct((parts // 2, width // parts, 4 * cols), BF16),
        ]
        grad_scratch = [pltpu.VMEM((width, 4 * cols), F32)]
    else:
        grad_outs = [struct((width, 4 * cols), F32)]
        grad_scratch = []
    *weight_grads, keep, send, sums_one = call(
        functools.partial(backward_kernel, parts, pieces, heads),
        grad_outs
        + [
            struct((pieces // 2, tok_dev, width), F32),
            struct((pieces // 2, tok_dev, width), BF16),
            struct((8, width), F32),
        ],
        [
            pltpu.VMEM((length, width), BF16),
            pltpu.VMEM((length, 3 * cols), BF16),
            pltpu.VMEM((length, width), F32),
        ]
        + grad_scratch,
        [place, starts, rel_bias]
        + lows
        + [whole_weight, whole_rows, projected, attended, lse, gain_one, doc_column],
        smem=3,
        flops=6 * length * width * 4 * cols + 10 * heads * length * length * HDIM,
        name="attend_back",
    )
    weight_sum = scatter_grads(weight_grads[0], weight_grads[-1], senders)
    part, near, far = scatter_rows(keep, send, pieces)
    (input_grad,) = call(
        input_kernel,
        [struct((tok_dev, width), BF16)],
        [],
        [tokens, gain_one, mixed_grad, part, near, far],
        name="input_grad",
    )
    summed = to_all(jnp.concatenate([sums_one, sums_two], axis=0), senders, pieces)
    bias_grad = summed[1, : HEADS * BUCKETS].reshape(HEADS, BUCKETS).T
    return (
        result,
        input_grad,
        summed[0],
        weight_sum[:, : 3 * cols].reshape(-1, 3, cols),
        weight_sum[:, 3 * cols :],
        bias_grad,
        summed[8 + experts],
        summed[8 : 8 + experts].T,
        grad_in_sum[None],
        grad_out_sum[None],
    )


def solution(mesh):
    in_specs = (
        P(("dp", "tensor"), None),
        P("dp"),
        P(("dp", "tensor"), None),
        P(),
        P("dp", None, "tensor"),
        P("dp", "tensor"),
        P(),
        P(),
        P(),
        P("dp", None, "tensor"),
        P("dp", "tensor", None),
        P(("dp", "tensor"), None),
    )
    out_specs = (
        P(("dp", "tensor"), None),
        P(("dp", "tensor"), None),
        P(),
        P("dp", None, "tensor"),
        P("dp", "tensor"),
        P(),
        P(),
        P(),
        P("dp", None, "tensor"),
        P("dp", "tensor", None),
    )
    return jax.shard_map(body, mesh=mesh, in_specs=in_specs, out_specs=out_specs, check_vma=False)
```

time: 633 us -> 259 us (0.41); the launches traced: 625 us -> 258 us
  blocking collectives: 172 us -> 0 us
  waiting for transfers between devices: 267 us -> 103 us
  local copies, waits for them, and re-layouts: 74.6 us -> 31.4 us
  starting transfers between devices: 12.1 us -> 54.7 us
  matrix products: 63.9 us -> 26.7 us
  Pallas kernels: 0 us -> 35.5 us
  other arithmetic: 20.6 us -> 6.32 us
  between operations: 15.1 us -> 1.07 us
    reduce_scatter x6 -> x0, waiting for transfers between devices: 202 us -> none  [the longest x2 95.9 us: slot_sums(): lax.psum_scatter(lax.dot_general(left, right, (((1,), (contract,)), ((),...]
    all_gather x4 -> x0, blocking collectives: 90.6 us -> none  [the longest x1 39 us: body(): lax.all_gather(w_qkv, 'dp', axis=0, tiled=True)]
    ppermute x0 -> x37, waiting for transfers between devices: none -> 80.2 us  [swap(): return lax.ppermute(value, axis, [(i, i ^ mask) for i in range(size)])]
    all_gather x2 -> x0, waiting for transfers between devices: 42.7 us -> none  [spread_rows(): return lax.all_gather(slot_block, 'tensor', axis=0, tiled=True)]
    all_to_all x2 -> x0, blocking collectives: 42.2 us -> none  [to_experts(): lax.all_to_all(slot_block, 'dp', split_axis=0, concat_axis=0, tiled=True)]
    psum x1 -> x0, blocking collectives: 39.4 us -> none  [body(): lax.psum((gain_attn_grad, gain_ffn_grad, router_grad, bias_grad), ('dp',...]
    pallas_call x0 -> x9, Pallas kernels: none -> 35.5 us  [the longest x8 24.5 us: call(): pl.pallas_call(kernel, out_shape=[jax.ShapeDtypeStruct(o.shape, o.dtype)...]
    dot_general x29 -> x8, matrix products: 61.9 us -> 26.7 us  [dot(): lax.dot_general(left, right, dims, preferred_element_type=F32, precision=...]
  transfers between devices with their start and end apart: 10 -> 41, of which waited for: 9 -> 16; matrix products, arithmetic and copies ran while one was open for 9% -> 16% of each run, Pallas kernels for 0% -> 9%
where the time goes in v1:
time: 259 us; the launch traced here: 258 us
  waiting for transfers between devices  103 us (40%)
  starting transfers between devices  54.7 us (21%)
  Pallas kernels  35.5 us (14%)
  local copies, waits for them, and re-layouts  31.4 us (12%)
  matrix products  26.7 us (10%)
  other arithmetic  6.32 us (2%)
    ppermute x37, waiting for transfers between devices, swap(): return lax.ppermute(value, axis, [(i, i ^ mask) for i in range(size)])  80.2 us
    ppermute x37, starting transfers between devices, swap(): return lax.ppermute(value, axis, [(i, i ^ mask) for i in range(size)])  33.7 us
    dot_general x8, matrix products, dot(): lax.dot_general(left, right, dims, preferred_element_type=F32, precision=...  26.7 us
    pallas_call x8, Pallas kernels, call(): pl.pallas_call(kernel, out_shape=[jax.ShapeDtypeStruct(o.shape, o.dtype)...  24.5 us
    unnamed x106, local copies, waits for them, and re-layouts  23.9 us
    all_to_all x4, waiting for transfers between devices, exchange(): lax.all_to_all(blocks.reshape(senders, capacity, width), 'dp', split_axis...  22.4 us
    all_to_all x4, starting transfers between devices, exchange(): lax.all_to_all(blocks.reshape(senders, capacity, width), 'dp', split_axis...  21 us
    pallas_call x1, Pallas kernels, run_experts(): pl.pallas_call(expert_kernel, grid=(steps,), in_specs=[whole((rows, paylo...  11.1 us
  transfers between devices with their start and end apart: 41, of which 16 were waited for; matrix products, arithmetic and copies ran while one was open for 16% of the time, Pallas kernels for 9%

profile of v1, /device:TPU:0, one launch (start us, length us, event | category | flops | bytes accessed | tf_op | source)
XLA Modules:
  0.0 258.2 jit_solution(8090464659697175202)
XLA Ops:
  15.1 4.9 %all-to-all-start.1 = ((bf16[8,48,768]{2,1,0:T(8,128)(2,1)}), bf16[8,48,768]{2,1,0:T(8,128)(2,1)}, u32[]{:S(2)}, u32[]{:S(2)}) async-start(bf16[8,48,768]{2,1,0:T(8,128)(2,1)} %bitcast.10), calls=%async_computation.1 | async-start | bytes 1179648 | tf_op jit(solution)/shard_map/all_to_all | solution.py:580
  25.3 6.3 %collective-permute-done.2.refs_6_ = bf16[96,768]{1,0:T(8,128)(2,1)S(1)} collective-permute-done((bf16[96,768]{1,0:T(8,128)(2,1)S(1)}, bf16[96,768]{1,0:T(8,128)(2,1)S(1)}, u32[]{:S(2)}, u32[]{:S(2)}) %collective-permute-start.2) | collective-permute-done | bytes 147488 | tf_op jit(solution)/shard_map/ppermute | solution.py:522
  31.6 3.9 %collective-permute-done.4.refs_8_ = bf16[96,768]{1,0:T(8,128)(2,1)S(1)} collective-permute-done((bf16[96,768]{1,0:T(8,128)(2,1)S(1)}, bf16[96,768]{1,0:T(8,128)(2,1)S(1)}, u32[]{:S(2)}, u32[]{:S(2)}) %collective-permute-start.4) | collective-permute-done | bytes 147488 | tf_op jit(solution)/shard_map/ppermute | solution.py:522
  39.4 7.2 %attend.1 = (bf16[768,768]{1,0:T(8,128)(2,1)}, bf16[512,768]{1,0:T(8,128)(2,1)S(1)}, bf16[512,576]{1,0:T(8,128)(2,1)S(1)}, bf16[512,192]{1,0:T(8,128)(2,1)S(1)},...) custom-call(s32[2]{0:T(128)S(1)} %pad_add_fusion.refs_0_, ...), custom_call_target="tpu_custom_call" | custom-call | flops 805306368 | bytes 6167080 | tf_op jit(solution)/shard_map/attend/pallas_call | solution.py:75
  52.2 6.4 %collective-permute-done.11.far_ref = bf16[128,768]{1,0:T(8,128)(2,1)S(1)} collective-permute-done((bf16[128,768]{1,0:T(8,128)(2,1)S(1)}, bf16[128,768]{1,0:T(8,128)(2,1)S(1)}, u32[]{:S(2)}, u32[]{:S(2)}) %collective-permute-start.11) | collective-permute-done | bytes 196640 | tf_op jit(solution)/shard_map/ppermute | solution.py:522
  60.9 4.4 %all-to-all-start = ((bf16[8,48,896]{2,1,0:T(8,128)(2,1)}), bf16[8,48,896]{2,1,0:T(8,128)(2,1)S(1)}, u32[]{:S(2)}, u32[]{:S(2)}) async-start(bf16[8,48,896]{2,1,0:T(8,128)(2,1)} %bitcast.7), calls=%async_computation | async-start | bytes 1376256 | tf_op jit(solution)/shard_map/all_to_all | solution.py:580
  67.3 15.5 %all-to-all-done = bf16[8,48,896]{2,1,0:T(8,128)(2,1)S(1)} async-done(((bf16[8,48,896]{2,1,0:T(8,128)(2,1)}), bf16[8,48,896]{2,1,0:T(8,128)(2,1)S(1)}, u32[]{:S(2)}, u32[]{:S(2)}) %all-to-all-start) | async-done | bytes 688160 | tf_op jit(solution)/shard_map/all_to_all | solution.py:580
  82.8 4.2 %fusion.12.back_one = f32[768,768]{1,0:T(8,128)} fusion(bf16[1,768,768]{2,1,0:T(8,128)(2,1)} %param.22, bf16[384,768]{1,0:T(8,128)(2,1)S(1)} %collective-permute-done.14, bf16[384,768]{1,0:T(8,128)(2,1)} %bitcast.11), kind=kOutput, calls=%fused_computation.46 | convolution fusion | flops 908328960 | bytes 4718592 | tf_op jit(solution)/shard_map/dot_general | solution.py:29
  87.0 7.5 %collective-permute-done.15 = bf16[768,768]{1,0:T(8,128)(2,1)} collective-permute-done((bf16[768,768]{1,0:T(8,128)(2,1)}, bf16[768,768]{1,0:T(8,128)(2,1)}, u32[]{:S(2)}, u32[]{:S(2)}) %collective-permute-start.15) | collective-permute-done | bytes 1179680 | tf_op jit(solution)/shard_map/ppermute | solution.py:522
  94.5 4.0 %fusion.14.back_two = f32[768,768]{1,0:T(8,128)} fusion(bf16[768,768]{1,0:T(8,128)(2,1)} %collective-permute-done.15, bf16[384,768]{1,0:T(8,128)(2,1)S(1)} %collective-permute-done.14, bf16[384,768]{1,0:T(8,128)(2,1)} %bitcast.11), kind=kOutput, calls=%fused_computation.48 | convolution fusion | flops 908328960 | bytes 4718592 | tf_op jit(solution)/shard_map/dot_general | solution.py:29
  98.5 19.3 %collective-permute-done.13.in_two = bf16[768,768]{1,0:T(8,128)(2,1)} collective-permute-done((bf16[768,768]{1,0:T(8,128)(2,1)}, bf16[768,768]{1,0:T(8,128)(2,1)}, u32[]{:S(2)}, u32[]{:S(2)}) %collective-permute-start.13) | collective-permute-done | bytes 1179680 | tf_op jit(solution)/shard_map/ppermute | solution.py:522
  117.8 11.1 %experts.1 = (bf16[768,768]{1,0:T(8,128)(2,1)S(1)}, bf16[768,768]{1,0:T(8,128)(2,1)S(1)}, bf16[768,768]{1,0:T(8,128)(2,1)S(1)}, bf16[768,768]{1,0:T(8,128)(2,1)}...) custom-call(bf16[384,896]{1,0:T(8,128)(2,1)S(1)} %bitcast.75, bf16[384,896]{1,0:T(8,128)(2,1)S(1)} %collective-permute-done.12.mate_ref, ...), custom_call_target="tpu_custom_call" | custom-call | flops 3623878656 | bytes 16777216 | tf_op jit(solution)/shard_map/experts/pallas_call | solution.py:311
  135.7 5.7 %all-to-all-start.3 = ((bf16[8,48,896]{2,1,0:T(8,128)(2,1)}), bf16[8,48,896]{2,1,0:T(8,128)(2,1)S(1)}, u32[]{:S(2)}, u32[]{:S(2)}) async-start(bf16[8,48,896]{2,1,0:T(8,128)(2,1)} %bitcast.15), calls=%async_computation.3 | async-start | bytes 1376256 | tf_op jit(solution)/shard_map/all_to_all | solution.py:580
  148.0 3.4 %convolution_convert_fusion = bf16[768,768]{1,0:T(8,128)(2,1)} fusion(bf16[768,768]{1,0:T(8,128)(2,1)S(1)} %copy-done.28, f32[768]{0:T(1024)S(1)} %convert_reduce_fusion, bf16[384,768]{1,0:T(8,128)(2,1)S(1)} %copy-done.48, bf16[384,768]{1,0:T(8,128)(2,1)} %bitcast.11), kind=kOutput, calls=%fused_computation.4 | convolution fusion | flops 910098432 | bytes 3542016 | tf_op jit(solution)/shard_map/dot_general | solution.py:29
  152.8 6.9 %all-to-all-done.3 = bf16[8,48,896]{2,1,0:T(8,128)(2,1)S(1)} async-done(((bf16[8,48,896]{2,1,0:T(8,128)(2,1)}), bf16[8,48,896]{2,1,0:T(8,128)(2,1)S(1)}, u32[]{:S(2)}, u32[]{:S(2)}) %all-to-all-start.3) | async-done | bytes 688160 | tf_op jit(solution)/shard_map/all_to_all | solution.py:580
  161.5 3.6 %convolution_convert_fusion.1 = bf16[768,768]{1,0:T(8,128)(2,1)} fusion(bf16[768,768]{1,0:T(8,128)(2,1)} %get-tuple-element.63, bf16[384,768]{1,0:T(8,128)(2,1)S(1)} %copy-done.39, bf16[384,768]{1,0:T(8,128)(2,1)S(1)} %copy-done.37), kind=kOutput, calls=%fused_computation.5 | convolution fusion | flops 908918784 | bytes 3538944 | tf_op jit(solution)/shard_map/dot_general | solution.py:29
  166.5 18.1 %collective-permute-done.19.refs_5_ = bf16[128,768]{1,0:T(8,128)(2,1)S(1)} collective-permute-done((bf16[128,768]{1,0:T(8,128)(2,1)S(1)}, bf16[128,768]{1,0:T(8,128)(2,1)S(1)}, u32[]{:S(2)}, u32[]{:S(2)}) %collective-permute-start.19) | collective-permute-done | bytes 196640 | tf_op jit(solution)/shard_map/ppermute | solution.py:522
  186.8 6.0 %all-to-all-start.2 = ((bf16[8,48,768]{2,1,0:T(8,128)(2,1)}), bf16[8,48,768]{2,1,0:T(8,128)(2,1)S(1)}, u32[]{:S(2)}, u32[]{:S(2)}) async-start(bf16[8,48,768]{2,1,0:T(8,128)(2,1)} %bitcast.13), calls=%async_computation.2 | async-start | bytes 1179648 | tf_op jit(solution)/shard_map/all_to_all | solution.py:580
  202.9 9.6 %attend_back.1 = (f32[4,96,768]{2,1,0:T(8,128)S(1)}, bf16[4,96,768]{2,1,0:T(8,128)(2,1)S(1)}, f32[2,128,768]{2,1,0:T(8,128)S(1)}, bf16[2,128,768]{2,1,0:T(8,128)(2,1)}, f32[8,768]{1,0:T(8,128)S(1)}) custom-call(s32[2]{0:T(128)S(1)} %pad_add_fusion.refs_0_, s32[8]{0:T(128)S(1)} %xor_multiply_fusion.refs_1_, f32[32,12]{1,0:T(8,128)S(1)} %copy.33.refs_2_, ...), custom_call_target="tpu_custom_call" | custom-call | flops 2315255808 | bytes 6781480 | tf_op jit(solution)/shard_map/attend_back/pallas_call | solution.py:75
  218.0 4.2 %add_bitcast_fusion = f32[1,768,768]{2,1,0:T(8,128)} fusion(bf16[768,768]{1,0:T(8,128)(2,1)} %collective-permute-done.36, bf16[768,768]{1,0:T(8,128)(2,1)S(1)} %copy-done.22, f32[768]{0:T(1024)S(1)} %convert_reduce_fusion, bf16[384,768]{1,0:T(8,128)(2,1)S(1)} %copy-done.49, bf16[384,768]{1,0:T(8,128)(2,1)} %bitcast.11), kind=kOutput, calls=%fused_computation | convolution fusion | flops 910688256 | bytes 5901312 | tf_op jit(solution)/shard_map/dot_general | solution.py:29
  227.2 3.7 %collective-permute-start.30 = (bf16[96,768]{1,0:T(8,128)(2,1)}, bf16[96,768]{1,0:T(8,128)(2,1)}, u32[]{:S(2)}, u32[]{:S(2)}) collective-permute-start(bf16[96,768]{1,0:T(8,128)(2,1)} %get-tuple-element.86), channel_id=1, source_target_pairs={{0,24},{4,28},{8,16},{12,20},{16,8},{20,12},{24,0},{28,4},{1,25},{... | collective-permute-start | bytes 442376 | tf_op jit(solution)/shard_map/ppermute | solution.py:522
  233.1 3.8 %add_bitcast_fusion.1 = f32[1,768,768]{2,1,0:T(8,128)} fusion(bf16[768,768]{1,0:T(8,128)(2,1)} %collective-permute-done.35, bf16[768,768]{1,0:T(8,128)(2,1)S(1)} %copy-done.34, bf16[384,768]{1,0:T(8,128)(2,1)S(1)} %copy-done.40, bf16[384,768]{1,0:T(8,128)(2,1)S(1)} %copy-done.38), kind=kOutput, calls=%fused_computation.2 | convolution fusion | flops 909508608 | bytes 5898240 | tf_op jit(solution)/shard_map/dot_general | solution.py:29
  238.0 3.7 %collective-permute-done.26 = f32[24,768]{1,0:T(8,128)S(1)} collective-permute-done((f32[24,768]{1,0:T(8,128)S(1)}, f32[24,768]{1,0:T(8,128)S(1)}, u32[]{:S(2)}, u32[]{:S(2)}) %collective-permute-start.26) | collective-permute-done | bytes 73760 | tf_op jit(solution)/shard_map/ppermute | solution.py:522
  251.8 5.5 %collective-permute-done.22.far_ref = bf16[128,768]{1,0:T(8,128)(2,1)S(1)} collective-permute-done((bf16[128,768]{1,0:T(8,128)(2,1)S(1)}, bf16[128,768]{1,0:T(8,128)(2,1)S(1)}, u32[]{:S(2)}, u32[]{:S(2)}) %collective-permute-start.22) | collective-permute-done | bytes 196640 | tf_op jit(solution)/shard_map/ppermute | solution.py:522
  (215 shorter events, 88.4 us)
Async XLA Ops:
  0.7 24.2 %collective-permute-start.8 = (bf16[128,768]{1,0:T(8,128)(2,1)}, bf16[128,768]{1,0:T(8,128)(2,1)S(1)}, u32[]{:S(2)}, u32[]{:S(2)}) collective-permute-start(bf16[128,768]{1,0:T(8,128)(2,1)} %own_ref.3), channel_id=1, source_target_pairs={{0,2},{1,3},{2,0},{3,1},{4,6},{5,7},{6,4},{7,5},{8,10},{9,11},{10,... | collective-permute-start | bytes 589832 | tf_op jit(solution)/shard_map/ppermute | solution.py:522
  5.8 14.2 %collective-permute-start.1 = (bf16[96,768]{1,0:T(8,128)(2,1)S(1)}, bf16[96,768]{1,0:T(8,128)(2,1)S(1)}, u32[]{:S(2)}, u32[]{:S(2)}) collective-permute-start(bf16[96,768]{1,0:T(8,128)(2,1)S(1)} %pad_maximum_fusion.4.refs_3_), channel_id=1, source_target_pairs={{0,8},{4,12},{8,0},{12,4},{16,24},{20,28},{24,16},{28,20},{1,9},{5... | collective-permute-start | bytes 442376 | tf_op jit(solution)/shard_map/ppermute | solution.py:522
  7.4 13.9 %collective-permute-start.3 = (bf16[96,768]{1,0:T(8,128)(2,1)S(1)}, bf16[96,768]{1,0:T(8,128)(2,1)S(1)}, u32[]{:S(2)}, u32[]{:S(2)}) collective-permute-start(bf16[96,768]{1,0:T(8,128)(2,1)S(1)} %pad_maximum_fusion.4.refs_3_), channel_id=1, source_target_pairs={{0,16},{4,20},{8,24},{12,28},{16,0},{20,4},{24,8},{28,12},{1,17},{... | collective-permute-start | bytes 442376 | tf_op jit(solution)/shard_map/ppermute | solution.py:522
  10.0 12.8 %collective-permute-start.5 = (bf16[96,768]{1,0:T(8,128)(2,1)S(1)}, bf16[96,768]{1,0:T(8,128)(2,1)S(1)}, u32[]{:S(2)}, u32[]{:S(2)}) collective-permute-start(bf16[96,768]{1,0:T(8,128)(2,1)S(1)} %pad_maximum_fusion.4.refs_3_), channel_id=1, source_target_pairs={{0,24},{4,28},{8,16},{12,20},{16,8},{20,12},{24,0},{28,4},{1,25},{... | collective-permute-start | bytes 442376 | tf_op jit(solution)/shard_map/ppermute | solution.py:522
  10.2 13.1 %collective-permute-start = (bf16[96,768]{1,0:T(8,128)(2,1)S(1)}, bf16[96,768]{1,0:T(8,128)(2,1)S(1)}, u32[]{:S(2)}, u32[]{:S(2)}) collective-permute-start(bf16[96,768]{1,0:T(8,128)(2,1)S(1)} %pad_maximum_fusion.4.refs_3_), channel_id=1, source_target_pairs={{0,4},{4,0},{8,12},{12,8},{16,20},{20,16},{24,28},{28,24},{1,5},{5... | collective-permute-start | bytes 442376 | tf_op jit(solution)/shard_map/ppermute | solution.py:522
  15.1 45.8 %all-to-all-start.1 = ((bf16[8,48,768]{2,1,0:T(8,128)(2,1)}), bf16[8,48,768]{2,1,0:T(8,128)(2,1)}, u32[]{:S(2)}, u32[]{:S(2)}) async-start(bf16[8,48,768]{2,1,0:T(8,128)(2,1)} %bitcast.10), calls=%async_computation.1 | async-start | bytes 1179648 | tf_op jit(solution)/shard_map/all_to_all | solution.py:580
  23.3 14.5 %collective-permute-start.6 = (bf16[96,768]{1,0:T(8,128)(2,1)S(1)}, bf16[96,768]{1,0:T(8,128)(2,1)S(1)}, u32[]{:S(2)}, u32[]{:S(2)}) collective-permute-start(bf16[96,768]{1,0:T(8,128)(2,1)S(1)} %collective-permute-done.5.refs_9_), channel_id=1, source_target_pairs={{0,4},{4,0},{8,12},{12,8},{16,20},{20,16},{24,28},{28,24},{1,5},{5... | collective-permute-start | bytes 442376 | tf_op jit(solution)/shard_map/ppermute | solution.py:522
  24.9 13.6 %collective-permute-start.9 = (bf16[128,768]{1,0:T(8,128)(2,1)S(1)}, bf16[128,768]{1,0:T(8,128)(2,1)S(1)}, u32[]{:S(2)}, u32[]{:S(2)}) collective-permute-start(bf16[128,768]{1,0:T(8,128)(2,1)S(1)} %collective-permute-done.8.refs_13_), channel_id=1, source_target_pairs={{0,1},{1,0},{2,3},{3,2},{4,5},{5,4},{6,7},{7,6},{8,9},{9,8},{10,11... | collective-permute-start | bytes 589832 | tf_op jit(solution)/shard_map/ppermute | solution.py:522
  60.9 21.9 %all-to-all-start = ((bf16[8,48,896]{2,1,0:T(8,128)(2,1)}), bf16[8,48,896]{2,1,0:T(8,128)(2,1)S(1)}, u32[]{:S(2)}, u32[]{:S(2)}) async-start(bf16[8,48,896]{2,1,0:T(8,128)(2,1)} %bitcast.7), calls=%async_computation | async-start | bytes 1376256 | tf_op jit(solution)/shard_map/all_to_all | solution.py:580
  65.3 29.2 %collective-permute-start.15 = (bf16[768,768]{1,0:T(8,128)(2,1)}, bf16[768,768]{1,0:T(8,128)(2,1)}, u32[]{:S(2)}, u32[]{:S(2)}) collective-permute-start(bf16[768,768]{1,0:T(8,128)(2,1)} %bitcast.86), channel_id=1, source_target_pairs={{0,2},{1,3},{2,0},{3,1},{4,6},{5,7},{6,4},{7,5},{8,10},{9,11},{10,... | collective-permute-start | bytes 3538952 | tf_op jit(solution)/shard_map/ppermute | solution.py:522
  65.8 17.0 %collective-permute-start.14 = (bf16[384,768]{1,0:T(8,128)(2,1)}, bf16[384,768]{1,0:T(8,128)(2,1)S(1)}, u32[]{:S(2)}, u32[]{:S(2)}) collective-permute-start(bf16[384,768]{1,0:T(8,128)(2,1)} %bitcast.11), channel_id=1, source_target_pairs={{0,1},{1,0},{2,3},{3,2},{4,5},{5,4},{6,7},{7,6},{8,9},{9,8},{10,11... | collective-permute-start | bytes 1769480 | tf_op jit(solution)/shard_map/ppermute | solution.py:522
  65.8 52.0 %collective-permute-start.13 = (bf16[768,768]{1,0:T(8,128)(2,1)}, bf16[768,768]{1,0:T(8,128)(2,1)}, u32[]{:S(2)}, u32[]{:S(2)}) collective-permute-start(bf16[768,768]{1,0:T(8,128)(2,1)} %bitcast.84), channel_id=1, source_target_pairs={{0,2},{1,3},{2,0},{3,1},{4,6},{5,7},{6,4},{7,5},{8,10},{9,11},{10,... | collective-permute-start | bytes 3538952 | tf_op jit(solution)/shard_map/ppermute | solution.py:522
  82.8 35.0 %collective-permute-start.12 = (bf16[384,896]{1,0:T(8,128)(2,1)S(1)}, bf16[384,896]{1,0:T(8,128)(2,1)S(1)}, u32[]{:S(2)}, u32[]{:S(2)}) collective-permute-start(bf16[384,896]{1,0:T(8,128)(2,1)S(1)} %bitcast.74), channel_id=1, source_target_pairs={{0,1},{1,0},{2,3},{3,2},{4,5},{5,4},{6,7},{7,6},{8,9},{9,8},{10,11... | collective-permute-start | bytes 2064392 | tf_op jit(solution)/shard_map/ppermute | solution.py:522
  135.7 24.0 %all-to-all-start.3 = ((bf16[8,48,896]{2,1,0:T(8,128)(2,1)}), bf16[8,48,896]{2,1,0:T(8,128)(2,1)S(1)}, u32[]{:S(2)}, u32[]{:S(2)}) async-start(bf16[8,48,896]{2,1,0:T(8,128)(2,1)} %bitcast.15), calls=%async_computation.3 | async-start | bytes 1376256 | tf_op jit(solution)/shard_map/all_to_all | solution.py:580
  147.4 37.2 %collective-permute-start.16 = (bf16[384,768]{1,0:T(8,128)(2,1)}, bf16[384,768]{1,0:T(8,128)(2,1)}, u32[]{:S(2)}, u32[]{:S(2)}) collective-permute-start(bf16[384,768]{1,0:T(8,128)(2,1)} %slice.157), channel_id=1, source_target_pairs={{0,1},{1,0},{2,3},{3,2},{4,5},{5,4},{6,7},{7,6},{8,9},{9,8},{10,11... | collective-permute-start | bytes 1769480 | tf_op jit(solution)/shard_map/ppermute | solution.py:522
  151.4 66.0 %collective-permute-start.36 = (bf16[768,768]{1,0:T(8,128)(2,1)}, bf16[768,768]{1,0:T(8,128)(2,1)}, u32[]{:S(2)}, u32[]{:S(2)}) collective-permute-start(bf16[768,768]{1,0:T(8,128)(2,1)} %convolution_convert_fusion), channel_id=1, source_target_pairs={{0,2},{1,3},{2,0},{3,1},{4,6},{5,7},{6,4},{7,5},{8,10},{9,11},{10,... | collective-permute-start | bytes 3538952 | tf_op jit(solution)/shard_map/ppermute | solution.py:522
  160.8 23.8 %collective-permute-start.19 = (bf16[128,768]{1,0:T(8,128)(2,1)S(1)}, bf16[128,768]{1,0:T(8,128)(2,1)S(1)}, u32[]{:S(2)}, u32[]{:S(2)}) collective-permute-start(bf16[128,768]{1,0:T(8,128)(2,1)S(1)} %get-tuple-element.50.refs_3_), channel_id=1, source_target_pairs={{0,2},{1,3},{2,0},{3,1},{4,6},{5,7},{6,4},{7,5},{8,10},{9,11},{10,... | collective-permute-start | bytes 589832 | tf_op jit(solution)/shard_map/ppermute | solution.py:522
  165.0 67.6 %collective-permute-start.35 = (bf16[768,768]{1,0:T(8,128)(2,1)}, bf16[768,768]{1,0:T(8,128)(2,1)}, u32[]{:S(2)}, u32[]{:S(2)}) collective-permute-start(bf16[768,768]{1,0:T(8,128)(2,1)} %convolution_convert_fusion.1), channel_id=1, source_target_pairs={{0,2},{1,3},{2,0},{3,1},{4,6},{5,7},{6,4},{7,5},{8,10},{9,11},{10,... | collective-permute-start | bytes 3538952 | tf_op jit(solution)/shard_map/ppermute | solution.py:522
  166.5 26.3 %collective-permute-start.18 = (bf16[128,768]{1,0:T(8,128)(2,1)S(1)}, bf16[128,768]{1,0:T(8,128)(2,1)S(1)}, u32[]{:S(2)}, u32[]{:S(2)}) collective-permute-start(bf16[128,768]{1,0:T(8,128)(2,1)S(1)} %get-tuple-element.50.refs_3_), channel_id=1, source_target_pairs={{0,1},{1,0},{2,3},{3,2},{4,5},{5,4},{6,7},{7,6},{8,9},{9,8},{10,11... | collective-permute-start | bytes 589832 | tf_op jit(solution)/shard_map/ppermute | solution.py:522
  186.8 50.1 %all-to-all-start.2 = ((bf16[8,48,768]{2,1,0:T(8,128)(2,1)}), bf16[8,48,768]{2,1,0:T(8,128)(2,1)S(1)}, u32[]{:S(2)}, u32[]{:S(2)}) async-start(bf16[8,48,768]{2,1,0:T(8,128)(2,1)} %bitcast.13), calls=%async_computation.2 | async-start | bytes 1179648 | tf_op jit(solution)/shard_map/all_to_all | solution.py:580
  222.2 19.5 %collective-permute-start.28 = (bf16[96,768]{1,0:T(8,128)(2,1)}, bf16[96,768]{1,0:T(8,128)(2,1)}, u32[]{:S(2)}, u32[]{:S(2)}) collective-permute-start(bf16[96,768]{1,0:T(8,128)(2,1)} %get-tuple-element.93), channel_id=1, source_target_pairs={{0,4},{4,0},{8,12},{12,8},{16,20},{20,16},{24,28},{28,24},{1,5},{5... | collective-permute-start | bytes 442376 | tf_op jit(solution)/shard_map/ppermute | solution.py:522
  227.2 17.0 %collective-permute-start.30 = (bf16[96,768]{1,0:T(8,128)(2,1)}, bf16[96,768]{1,0:T(8,128)(2,1)}, u32[]{:S(2)}, u32[]{:S(2)}) collective-permute-start(bf16[96,768]{1,0:T(8,128)(2,1)} %get-tuple-element.86), channel_id=1, source_target_pairs={{0,24},{4,28},{8,16},{12,20},{16,8},{20,12},{24,0},{28,4},{1,25},{... | collective-permute-start | bytes 442376 | tf_op jit(solution)/shard_map/ppermute | solution.py:522
  230.9 13.3 %collective-permute-start.32 = (bf16[96,768]{1,0:T(8,128)(2,1)}, bf16[96,768]{1,0:T(8,128)(2,1)}, u32[]{:S(2)}, u32[]{:S(2)}) collective-permute-start(bf16[96,768]{1,0:T(8,128)(2,1)} %get-tuple-element.88), channel_id=1, source_target_pairs={{0,16},{4,20},{8,24},{12,28},{16,0},{20,4},{24,8},{28,12},{1,17},{... | collective-permute-start | bytes 442376 | tf_op jit(solution)/shard_map/ppermute | solution.py:522
  230.9 13.3 %collective-permute-start.34 = (bf16[96,768]{1,0:T(8,128)(2,1)}, bf16[96,768]{1,0:T(8,128)(2,1)}, u32[]{:S(2)}, u32[]{:S(2)}) collective-permute-start(bf16[96,768]{1,0:T(8,128)(2,1)} %get-tuple-element.87), channel_id=1, source_target_pairs={{0,8},{4,12},{8,0},{12,4},{16,24},{20,28},{24,16},{28,20},{1,9},{5... | collective-permute-start | bytes 442376 | tf_op jit(solution)/shard_map/ppermute | solution.py:522
  (67 other events, 453.5 us)

commit v2 on v1

v2 whole, which is shorter than its diff:
```python
import functools

import jax
import jax.numpy as jnp
import numpy as np
from jax import lax
from jax.experimental import pallas as pl
from jax.experimental.pallas import tpu as pltpu
from jax.sharding import PartitionSpec as P

HEADS = 12
HDIM = 64
BUCKETS = 32
ROWS = 128
GATE_LANES = 128

LIMITS = np.array([19, 21, 24, 27, 31, 35, 40, 46, 52, 59, 67, 77, 87, 99, 113], np.int32)
HIGHEST = lax.Precision.HIGHEST
F32 = jnp.float32
BF16 = jnp.bfloat16
MIB = 1024 * 1024

NN = (((1,), (0,)), ((), ()))
NT = (((1,), (1,)), ((), ()))
TN = (((0,), (0,)), ((), ()))


def dot(left, right, dims=NN, precision=None):
    return lax.dot_general(left, right, dims, preferred_element_type=F32, precision=precision)


def iota(shape, axis):
    return lax.broadcasted_iota(jnp.int32, shape, axis)


def bucket_of(distance):
    bucket = jnp.minimum(distance, 16)
    for limit in LIMITS:
        bucket = bucket + (distance >= int(limit)).astype(jnp.int32)
    return bucket


def in_three(value):
    high = value.astype(BF16)
    rest = value - high.astype(F32)
    middle = rest.astype(BF16)
    low = (rest - middle.astype(F32)).astype(BF16)
    return high, middle, low


def three_lanes(value):
    high, middle, low = in_three(value)
    lane = iota((value.shape[0], GATE_LANES), 1)
    zero = jnp.zeros((value.shape[0], GATE_LANES), F32)
    spread = jnp.where(
        lane == 0,
        high.astype(F32),
        jnp.where(lane == 1, middle.astype(F32), jnp.where(lane == 2, low.astype(F32), zero)),
    )
    return spread.astype(BF16)


def lanes_sum(lanes):
    return jnp.sum(lanes.astype(F32), axis=1, keepdims=True)


def pick(columns, at):
    return columns[:, at : at + 1]


def call(
    kernel,
    outs,
    scratch,
    args,
    smem=0,
    flops=0,
    name=None,
    after=(),
    vmem=6,
    held=(),
    kept=(),
    passed=(),
    prompt=False,
):
    n_in, n_after, n_out = len(args), len(after), len(outs)
    n_pass = len(passed)

    def run(*refs):
        ins, rest = refs[:n_in], refs[n_in + n_after + n_pass :]
        kernel(*ins, *rest[:n_out], *rest[n_out + n_pass :])

    def whole(a):
        return pl.BlockSpec(a.shape, lambda i: (0,) * len(a.shape))

    moved = sum(a.size * a.dtype.itemsize for a in list(args) + list(outs))
    args = [
        pltpu.with_memory_space_constraint(a, pltpu.HBM) if at in held else a
        for at, a in enumerate(args)
    ]
    after = [
        pltpu.with_memory_space_constraint(a, pltpu.HBM) if a.size > 1 << 18 else a for a in after
    ]
    out_shape = [
        pltpu.HBM(o.shape, o.dtype) if at in kept else jax.ShapeDtypeStruct(o.shape, o.dtype)
        for at, o in enumerate(outs)
    ]
    return pl.pallas_call(
        run,
        grid=(1,),
        out_shape=out_shape + [jax.ShapeDtypeStruct(o.shape, o.dtype) for o in passed],
        in_specs=[pl.BlockSpec(memory_space=pltpu.SMEM)] * smem
        + [whole(a) for a in args[smem:]]
        + [pl.BlockSpec(memory_space=pl.ANY)] * (n_after + n_pass),
        out_specs=[whole(o) for o in outs] + [pl.BlockSpec(memory_space=pl.ANY)] * n_pass,
        scratch_shapes=scratch,
        input_output_aliases={n_in + n_after + at: n_out + at for at in range(n_pass)},
        compiler_params=pltpu.CompilerParams(vmem_limit_bytes=vmem * MIB),
        cost_estimate=pl.CostEstimate(
            flops=1 if prompt else flops,
            bytes_accessed=1 if prompt else moved,
            transcendentals=0,
        ),
        name=name,
    )(*args, *after, *passed)


def columns_of(turned):
    filled = jnp.concatenate(
        [turned.astype(F32), jnp.zeros((8 - turned.shape[0], turned.shape[1]), F32)], axis=0
    )
    return filled.T.astype(jnp.int32)


def pack_kernel(first_ref, last_ref, out_ref):
    cols = last_ref.shape[1]
    for at in range(3):
        out_ref[:, at * cols : (at + 1) * cols] = first_ref[at]
    out_ref[:, 3 * cols :] = last_ref[...]


def struct(shape, dtype):
    return jax.ShapeDtypeStruct(shape, dtype)


def slots_kernel(capacity, routes_ref, grad_ref, slot_ref, out_ref):
    tokens = routes_ref.shape[1]
    slots = out_ref.shape[0]
    experts = slots // capacity
    routes = columns_of(routes_ref[...])
    first, second = routes[:, 0:1], routes[:, 1:2]
    lane = iota((tokens, experts), 1)
    one_first = (first == lane).astype(F32)
    one_second = (second == lane).astype(F32)
    member = (one_first + one_second).astype(BF16)
    below = (iota((tokens, tokens), 1) < iota((tokens, tokens), 0)).astype(F32).astype(BF16)
    earlier = dot(below, member)
    slot_first = first * capacity + jnp.sum(one_first * earlier, axis=1, keepdims=True).astype(
        jnp.int32
    )
    slot_second = second * capacity + jnp.sum(one_second * earlier, axis=1, keepdims=True).astype(
        jnp.int32
    )
    wide = iota((tokens, 128), 1)
    slot_ref[...] = jnp.where(wide == 0, slot_first, slot_second)
    places = iota((tokens, slots), 1)
    chosen = ((slot_first == places) | (slot_second == places)).astype(F32).astype(BF16)
    out_ref[...] = dot(chosen, grad_ref[...], TN).astype(BF16)


def bias_tiles(rel_ref, first_head, heads):
    column = iota((8, 256), 1)
    distance = (ROWS - column) & 255
    bucket = bucket_of(distance)
    tiles = []
    for head in range(heads):
        line = jnp.zeros((8, 256), F32)
        for b in range(BUCKETS):
            line = jnp.where(bucket == b, rel_ref[first_head + head, b], line)
        wide = jnp.broadcast_to(line[0:1, :], (ROWS, 256))
        tiles.append(pltpu.roll(wide, 0, 1, stride=1, stride_axis=0))
    return tiles


def masked_scores(query, keys, tile, far, second, block):
    width = (block + 1) * ROWS
    raw = dot(query, keys, NT) * HDIM**-0.5
    if block == 0:
        bias = tile[:, ROWS:]
    elif block == 1:
        bias = tile
    else:
        bias = jnp.concatenate([jnp.full((ROWS, width - 2 * ROWS), far, F32), tile], axis=1)
    column = iota((ROWS, width), 1)
    row = iota((ROWS, width), 0) + block * ROWS
    starts = jnp.where(row >= second, second, 0)
    allowed = (column <= row) & (column >= starts)
    return jnp.where(allowed, raw + bias, -1e9)


def forward_kernel(parts, pieces, heads, *refs):
    doc_ref, rel_ref = refs[:2]
    weights = refs[2 : 2 + parts]
    rows = refs[2 + parts : 2 + parts + pieces]
    gain_ref = refs[2 + parts + pieces]
    weight_out, row_out, proj_out, att_out, lse_out, keep_a, keep_b, send_out = refs[
        3 + parts + pieces :
    ]
    keep_out = (keep_a, keep_b)
    piece, mine_dp = lax.axis_index("tensor"), lax.axis_index("dp")
    second = doc_ref[doc_ref.shape[0] - 1]
    cols = heads * HDIM
    for at in range(parts):
        depth = weights[at].shape[0]
        start = (mine_dp ^ at) * depth if parts > 1 else 0
        weight_out[pl.ds(pl.multiple_of(start, 16), depth), :] = weights[at][...]
    for at in range(pieces):
        row_out[pl.ds(pl.multiple_of((piece ^ at) * ROWS, ROWS), ROWS), :] = rows[at][...]
    x = row_out[...].astype(F32)
    scale = lax.rsqrt(jnp.mean(x * x, axis=1, keepdims=True) + 1e-6)
    normed = (x * scale * gain_ref[...]).astype(BF16)
    proj_out[...] = dot(normed, weight_out[:, : 3 * cols]).astype(BF16)
    tiles = bias_tiles(rel_ref, piece * heads, heads)
    blocks = x.shape[0] // ROWS
    proj = proj_out[...]
    wide = iota((ROWS, 128), 1)
    for block in range(blocks):
        here = slice(block * ROWS, (block + 1) * ROWS)
        upto = slice(0, (block + 1) * ROWS)
        done = []
        kept = jnp.zeros((ROWS, 128), F32)
        for head in range(heads):
            at = head * HDIM
            query = proj[here, at : at + HDIM]
            keys = proj[upto, cols + at : cols + at + HDIM]
            values = proj[upto, 2 * cols + at : 2 * cols + at + HDIM]
            far = rel_ref[piece * heads + head, BUCKETS - 1]
            scores = masked_scores(query, keys, tiles[head], far, second, block)
            peak = jnp.max(scores, axis=1, keepdims=True)
            shifted = jnp.exp(scores - peak)
            total = jnp.sum(shifted, axis=1, keepdims=True)
            attention = (shifted * (1.0 / total)).astype(BF16)
            done.append(dot(attention, values).astype(BF16))
            kept = jnp.where(wide == head, peak + jnp.log(total), kept)
        att_out[here, :] = jnp.concatenate(done, axis=1)
        lse_out[here, :] = kept
    weight_last = weight_out[:, 3 * cols :]
    for at in range(pieces):
        mine = att_out[pl.ds(pl.multiple_of((piece ^ at) * ROWS, ROWS), ROWS), :]
        product = dot(mine, weight_last, NT)
        if at % 2 == 0:
            keep_out[at // 2][...] = product
        else:
            send_out[at // 2] = product.astype(BF16)


def dispatch_kernel(
    own_ref,
    part_ref,
    near_ref,
    far_ref,
    gain_ref,
    router_ref,
    routes_ref,
    slot_ref,
    mixed_ref,
    normed_ref,
    gates_ref,
    out_ref,
):
    width = own_ref.shape[1]
    tokens = own_ref.shape[0]
    slots = out_ref.shape[0]
    mixed = own_ref[...].astype(F32) + (
        part_ref[...] + near_ref[0].astype(F32) + far_ref[...].astype(F32)
    )
    mixed_ref[...] = mixed
    scale = lax.rsqrt(jnp.mean(mixed * mixed, axis=1, keepdims=True) + 1e-6)
    normed = (mixed * scale * gain_ref[...]).astype(BF16)
    normed_ref[...] = normed
    logits = dot(normed, router_ref[...], NT)
    routes = columns_of(routes_ref[...])
    lane = iota(logits.shape, 1)
    one = jnp.sum(jnp.where(routes[:, 0:1] == lane, logits, 0.0), axis=1, keepdims=True)
    two = jnp.sum(jnp.where(routes[:, 1:2] == lane, logits, 0.0), axis=1, keepdims=True)
    peak = jnp.maximum(one, two)
    one, two = jnp.exp(one - peak), jnp.exp(two - peak)
    total = one + two
    one, two = one / total, two / total
    wide = iota((tokens, 128), 1)
    gates_ref[...] = jnp.where(wide == 0, one, two)
    places = iota((tokens, slots), 1)
    slot = slot_ref[...]
    first = (slot[:, 0:1] == places).astype(F32).astype(BF16)
    second = (slot[:, 1:2] == places).astype(F32).astype(BF16)
    out_ref[:, :width] = dot(first + second, normed, TN).astype(BF16)
    gate_slots = dot(first, three_lanes(one), TN) + dot(second, three_lanes(two), TN)
    out_ref[:, width:] = gate_slots.astype(BF16)


def gelu_and_slope(x):
    inner = 0.7978845608028654 * (x + 0.044715 * (x * x * x))
    bend = jnp.tanh(inner)
    half = 0.5 * (1.0 + bend)
    slope = half + 0.5 * x * (1.0 - bend * bend) * (
        0.7978845608028654 * (1.0 + 3 * 0.044715 * (x * x))
    )
    return x * half, slope


def expert_side(source, pull, in_ref, out_ref, here, hidden_out, pre_out, total, fresh):
    width, hidden_units = in_ref.shape
    tile = 256
    slot_rows = source[:, :width]
    gate = lanes_sum(source[:, width:])
    pulls = pull[...]
    gate_sum = jnp.zeros((source.shape[0], 1), F32)
    for at in range(0, hidden_units, tile):
        there = slice(at, at + tile)
        weight = in_ref[:, there]
        pulled = dot(pulls, out_ref[there, :], NT)
        hidden, slope = gelu_and_slope(dot(slot_rows, weight))
        hidden = hidden.astype(BF16)
        pre_grad = (pulled * gate * slope).astype(BF16)
        hidden_out[here, there] = hidden
        if pre_out is not None:
            pre_out[here, there] = pre_grad
        product = dot(pre_grad, weight, NT)
        if fresh and at == 0:
            total[here, :] = product
        else:
            total[here, :] += product
        gate_sum += jnp.sum(hidden.astype(F32) * pulled, axis=1, keepdims=True)
    return gate_sum


def own_slice_kernel(
    own_ref, mate_ref, pull_own, pull_mate, in_ref, out_ref, hidden_ref, pre_ref, total_ref, sum_ref
):
    rows = own_ref.shape[0]
    for side, (source, pull) in enumerate(((own_ref, pull_own), (mate_ref, pull_mate))):
        here = slice(side * rows, (side + 1) * rows)
        gate_sum = expert_side(
            source, pull, in_ref, out_ref, here, hidden_ref, pre_ref, total_ref, True
        )
        sum_ref[here, :] = jnp.broadcast_to(gate_sum, (rows, GATE_LANES))


def far_slice_kernel(
    own_ref,
    mate_ref,
    pull_own,
    pull_mate,
    in_a_ref,
    in_b_ref,
    out_ref,
    total_ref,
    sum_ref,
    hidden_ref,
    keep_ref,
    send_ref,
    total,
    in_ref,
):
    rows = own_ref.shape[0]
    width, split = in_ref.shape[0], in_a_ref.shape[0]
    in_ref[:split, :] = in_a_ref[...]
    in_ref[split:, :] = in_b_ref[...]
    total[...] = total_ref[...]
    for side, (source, pull) in enumerate(((mate_ref, pull_mate), (own_ref, pull_own))):
        here = slice((1 - side) * rows, (2 - side) * rows)
        gate_sum = sum_ref[here, 0:1] + expert_side(
            source, pull, in_ref, out_ref, here, hidden_ref, None, total, False
        )
        if side == 0:
            send_ref[:, :width] = total[here, :].astype(BF16)
            send_ref[:, width:] = three_lanes(gate_sum)
        else:
            keep_ref[:, :width] = total[here, :]
            keep_ref[:, width:] = jnp.broadcast_to(gate_sum, (rows, GATE_LANES))


def weight_grad_kernel(
    own_ref,
    mate_ref,
    pull_own,
    pull_mate,
    far_ref,
    far_mate_ref,
    far_pull_own,
    far_pull_mate,
    in_one,
    out_one,
    hidden_one,
    pre_one,
    grad_in,
    grad_out,
    token_ref,
    rows_turned,
    pulls_all,
    hidden_far,
    pre_far,
):
    rows = own_ref.shape[0]
    width, hidden_units = in_one.shape
    tile = 256
    token_ref[...] = jnp.zeros_like(token_ref)
    for at, (source, pull) in enumerate(
        (
            (own_ref, pull_own),
            (mate_ref, pull_mate),
            (far_ref, far_pull_own),
            (far_mate_ref, far_pull_mate),
        )
    ):
        here = slice(at * rows, (at + 1) * rows)
        slot_rows = source[:, :width]
        rows_turned[:, here] = slot_rows.T
        gate = lanes_sum(source[:, width:])
        pulls_all[here, :] = (gate * pull[...].astype(F32)).astype(BF16)
        if at >= 2:
            back = slice((at - 2) * rows, (at - 1) * rows)
            for unit in range(0, hidden_units, tile):
                there = slice(unit, unit + tile)
                hidden, slope = gelu_and_slope(dot(slot_rows, in_one[:, there]))
                pulled = dot(pulls_all[here, :], out_one[there, :], NT)
                hidden_far[back, there] = hidden.astype(BF16)
                pre_far[back, there] = (pulled * slope).astype(BF16)
    for unit in range(0, hidden_units, tile):
        there = slice(unit, unit + tile)
        grad_in[:, there] = dot(rows_turned[:, : 2 * rows], pre_one[:, there]) + dot(
            rows_turned[:, 2 * rows :], pre_far[:, there]
        )
        grad_out[there, :] = dot(hidden_one[:, there], pulls_all[: 2 * rows, :], TN) + dot(
            hidden_far[:, there], pulls_all[2 * rows :, :], TN
        )


def expert_out_kernel(hidden_one, hidden_two, out_one, out_two, keep_ref, send_ref):
    rows = keep_ref.shape[0]
    product = dot(hidden_one[...], out_one[...]) + dot(hidden_two[...], out_two[...])
    keep_ref[...] = product[:rows]
    send_ref[...] = product[rows:].astype(BF16)


def merge_kernel(keep_ref, mate_ref, out_ref):
    width = keep_ref.shape[1] - GATE_LANES
    out_ref[:, :width] = (keep_ref[:, :width] + mate_ref[:, :width].astype(F32)).astype(BF16)
    gate = keep_ref[:, width : width + 1] + lanes_sum(mate_ref[:, width:])
    out_ref[:, width:] = three_lanes(gate)


def combine_kernel(
    back_ref,
    slot_ref,
    gates_ref,
    mixed_ref,
    normed_ref,
    router_ref,
    routes_ref,
    grad_ref,
    gain_ref,
    mixed_grad_ref,
    low_ref,
    sums_ref,
):
    tokens, width = grad_ref.shape
    slots = back_ref.shape[0]
    experts = router_ref.shape[0]
    places = iota((tokens, slots), 1)
    slot = slot_ref[...]
    first = (slot[:, 0:1] == places).astype(F32).astype(BF16)
    second = (slot[:, 1:2] == places).astype(F32).astype(BF16)
    lanes = back_ref[:, width:]
    pull_one = jnp.sum(dot(first, lanes), axis=1, keepdims=True)
    pull_two = jnp.sum(dot(second, lanes), axis=1, keepdims=True)
    one, two = gates_ref[:, 0:1], gates_ref[:, 1:2]
    mean_pull = one * pull_one + two * pull_two
    delta_one = one * (pull_one - mean_pull)
    delta_two = two * (pull_two - mean_pull)
    routes = columns_of(routes_ref[...])
    lane = iota((tokens, experts), 1)
    logit_grad = jnp.where(routes[:, 0:1] == lane, delta_one, 0.0) + jnp.where(
        routes[:, 1:2] == lane, delta_two, 0.0
    )
    high = logit_grad.astype(BF16)
    low = (logit_grad - high.astype(F32)).astype(BF16)
    normed = normed_ref[...]
    router = router_ref[...]
    normed_grad = dot(first + second, back_ref[:, :width]) + (
        dot(high, router) + dot(low, router)
    )
    mixed = mixed_ref[...]
    grad = grad_ref[...].astype(F32)
    scale = lax.rsqrt(jnp.mean(mixed * mixed, axis=1, keepdims=True) + 1e-6)
    scaled = normed_grad * gain_ref[...]
    cubed = scale * scale * scale
    mixed_grad = (
        grad
        + scale * scaled
        - mixed * cubed * jnp.mean(scaled * mixed, axis=1, keepdims=True)
    )
    mixed_grad_ref[...] = mixed_grad
    low_ref[...] = mixed_grad.astype(BF16)
    sums_ref[...] = jnp.zeros_like(sums_ref)
    sums_ref[:experts, :] = dot(high, normed, TN) + dot(low, normed, TN)
    sums_ref[experts : experts + 1, :] = jnp.sum(
        normed_grad * mixed * scale, axis=0, keepdims=True
    )


def result_kernel(back_ref, slot_ref, gates_ref, mixed_ref, out_ref):
    tokens = mixed_ref.shape[0]
    slots = back_ref.shape[0]
    places = iota((tokens, slots), 1)
    slot = slot_ref[...]
    first = (slot[:, 0:1] == places).astype(F32).astype(BF16)
    second = (slot[:, 1:2] == places).astype(F32).astype(BF16)
    back = back_ref[...]
    added = gates_ref[:, 0:1] * dot(first, back) + gates_ref[:, 1:2] * dot(second, back)
    out_ref[...] = (mixed_ref[...] + added).astype(BF16)


def backward_kernel(parts, pieces, heads, experts, *refs):
    doc_ref, rel_ref = refs[:2]
    lows = refs[2 : 2 + pieces]
    weight_ref, row_ref, proj_ref, att_ref, lse_ref, gain_ref, sums_ref = refs[
        2 + pieces : 9 + pieces
    ]
    outs = refs[9 + pieces :]
    n_grads = parts // 2 + 2 if parts > 1 else 1
    grad_outs = outs[:n_grads]
    keep_a, keep_b, send_out, sums_out, mixed, grad_proj, normed_grad = outs[n_grads : n_grads + 7]
    keep_out = (keep_a, keep_b)
    piece, mine_dp = lax.axis_index("tensor"), lax.axis_index("dp")
    second = doc_ref[doc_ref.shape[0] - 1]
    cols = heads * HDIM
    for at in range(pieces):
        mixed[pl.ds(pl.multiple_of((piece ^ at) * ROWS, ROWS), ROWS), :] = lows[at][...]
    weight_last = weight_ref[:, 3 * cols :]
    att_grad = dot(mixed[...], weight_last).astype(BF16)
    grad_last = dot(mixed[...], att_ref[...], TN)
    tiles = bias_tiles(rel_ref, piece * heads, heads)
    proj = proj_ref[...]
    length = proj.shape[0]
    blocks = length // ROWS
    flipped = (iota((ROWS, ROWS), 0) + iota((ROWS, ROWS), 1) == ROWS - 1).astype(F32).astype(BF16)
    line_bucket = bucket_of((ROWS - iota((256, HEADS * BUCKETS), 0)) & 255)
    target = iota((256, HEADS * BUCKETS), 1)
    target_row = iota((8, HEADS * BUCKETS), 1)
    bias_row = jnp.zeros((8, HEADS * BUCKETS), F32)
    grads_q, grads_k, grads_v = [], [], []
    for head in range(heads):
        at = head * HDIM
        far = rel_ref[piece * heads + head, BUCKETS - 1]
        key_sum = [jnp.zeros((ROWS, HDIM), F32) for _ in range(blocks)]
        value_sum = [jnp.zeros((ROWS, HDIM), F32) for _ in range(blocks)]
        near_sum = jnp.zeros((ROWS, 256), F32)
        far_sum = jnp.zeros((ROWS, ROWS), F32)
        query_done = []
        for block in range(blocks):
            here = slice(block * ROWS, (block + 1) * ROWS)
            upto = slice(0, (block + 1) * ROWS)
            query = proj[here, at : at + HDIM]
            keys = proj[upto, cols + at : cols + at + HDIM]
            values = proj[upto, 2 * cols + at : 2 * cols + at + HDIM]
            out_grad = att_grad[here, at : at + HDIM]
            scores = masked_scores(query, keys, tiles[head], far, second, block)
            again = jnp.exp(scores - lse_ref[here, head : head + 1])
            prob_grad = dot(out_grad, values, NT)
            weighted = again * prob_grad
            score_grad = weighted - again * jnp.sum(weighted, axis=1, keepdims=True)
            score_low = score_grad.astype(BF16)
            value_add = dot(again.astype(BF16), out_grad, TN)
            key_add = dot(score_low, query, TN)
            for other in range(block + 1):
                there = slice(other * ROWS, (other + 1) * ROWS)
                key_sum[other] = key_sum[other] + key_add[there, :]
                value_sum[other] = value_sum[other] + value_add[there, :]
                if other < block - 1:
                    far_sum = far_sum + score_grad[:, there]
            if block == 0:
                near_sum = near_sum + jnp.concatenate(
                    [jnp.zeros((ROWS, ROWS), F32), score_grad], axis=1
                )
            else:
                near_sum = near_sum + score_grad[:, (block - 1) * ROWS :]
            query_done.append(dot(score_low, keys) * HDIM**-0.5)
        grads_q.append(jnp.concatenate(query_done, axis=0))
        grads_k.append(jnp.concatenate(key_sum, axis=0) * HDIM**-0.5)
        grads_v.append(jnp.concatenate(value_sum, axis=0))
        first_lane = (piece * heads + head) * BUCKETS
        near_high = near_sum.astype(BF16)
        near_low = (near_sum - near_high.astype(F32)).astype(BF16)
        turned = dot(flipped, near_high) + dot(flipped, near_low)
        turned = pltpu.roll(turned, ROWS + 1, 1, stride=1, stride_axis=0)
        line = jnp.broadcast_to(jnp.sum(turned, axis=0, keepdims=True), (8, 256))
        spread = (line_bucket + first_lane == target).astype(F32)
        bias_row = bias_row + dot(line, spread, precision=HIGHEST)
        far_total = jnp.sum(jnp.sum(far_sum, axis=0, keepdims=True), axis=1, keepdims=True)
        bias_row = bias_row + jnp.where(
            target_row == first_lane + BUCKETS - 1, far_total, 0.0
        )
    grad_proj[...] = jnp.concatenate(grads_q + grads_k + grads_v, axis=1).astype(BF16)
    x = row_ref[...].astype(F32)
    scale = lax.rsqrt(jnp.mean(x * x, axis=1, keepdims=True) + 1e-6)
    unit = x * scale
    normed = (unit * gain_ref[...]).astype(BF16)
    grad_first = dot(normed, grad_proj[...], TN)
    if parts > 1:
        grads = outs[n_grads + 7]
        depth = grad_first.shape[0] // parts
        grads[:, : 3 * cols] = grad_first
        grads[:, 3 * cols :] = grad_last
        for at in range(parts):
            piece_rows = grads[pl.ds(pl.multiple_of((mine_dp ^ at) * depth, 16), depth), :]
            if at % 2 == 0:
                grad_outs[at // 2][...] = piece_rows
            else:
                at_send = parts // 2 + (0 if at > 4 else 1)
                grad_outs[at_send][0 if at % 4 == 3 else 1] = piece_rows.astype(BF16)
    else:
        grad_outs[0][:, : 3 * cols] = grad_first
        grad_outs[0][:, 3 * cols :] = grad_last
    normed_grad[...] = dot(grad_proj[...], weight_ref[:, : 3 * cols], NT)
    sums_out[...] = sums_ref[...]
    sums_out[experts + 1 : experts + 2, :] = jnp.sum(
        normed_grad[...] * unit, axis=0, keepdims=True
    )
    sums_out[experts + 2 : experts + 3, : HEADS * BUCKETS] = bias_row[0:1, :]
    for at in range(pieces):
        mine = normed_grad[pl.ds(pl.multiple_of((piece ^ at) * ROWS, ROWS), ROWS), :]
        if at % 2 == 0:
            keep_out[at // 2][...] = mine
        else:
            send_out[at // 2] = mine.astype(BF16)


def input_kernel(own_ref, gain_ref, mixed_grad_ref, part_ref, near_ref, far_ref, out_ref):
    x = own_ref[...].astype(F32)
    scale = lax.rsqrt(jnp.mean(x * x, axis=1, keepdims=True) + 1e-6)
    scaled = (
        part_ref[...] + near_ref[0].astype(F32) + far_ref[...].astype(F32)
    ) * gain_ref[...]
    cubed = scale * scale * scale
    own = scale * scaled - x * cubed * jnp.mean(scaled * x, axis=1, keepdims=True)
    out_ref[...] = (mixed_grad_ref[...] + own).astype(BF16)


def swap(value, axis, size, mask):
    return lax.ppermute(value, axis, [(i, i ^ mask) for i in range(size)])


def gather_weights(shard, senders):
    if senders != 8:
        return [lax.all_gather(shard, "dp", axis=0, tiled=True)]
    parts = {0: shard}
    parts[1] = swap(shard, "dp", senders, 1)
    for mask in (2, 4, 6):
        parts[mask] = swap(shard, "dp", senders, mask)
    for mask in (2, 4, 6):
        parts[mask + 1] = swap(parts[mask], "dp", senders, 1)
    return [parts[i] for i in range(senders)]


def fold_kernel(keep_ref, near_ref, out_ref):
    out_ref[...] = (keep_ref[...] + near_ref[...].astype(F32)).astype(BF16)


def fold(keep, near, name, after=()):
    return call(fold_kernel, [struct(near.shape, BF16)], [], [keep, near], name=name, after=after)[0]


def finish_kernel(cols, keep_ref, near_ref, one_ref, two_ref, three_ref, first_ref, last_ref):
    total = keep_ref[...] + near_ref[...].astype(F32)
    for part in (one_ref, two_ref, three_ref):
        total = total + part[...].astype(F32)
    for at in range(3):
        first_ref[at] = total[:, at * cols : (at + 1) * cols]
    last_ref[...] = total[:, 3 * cols :]


def fold_two_kernel(one_ref, two_ref, near_ref, one_out, two_out):
    one_out[...] = (one_ref[...] + near_ref[0].astype(F32)).astype(BF16)
    two_out[...] = (two_ref[...] + near_ref[1].astype(F32)).astype(BF16)


def finish_kernel(cols, keep_ref, near_ref, one_ref, two_ref, three_ref, first_ref, last_ref):
    total = keep_ref[...] + near_ref[1].astype(F32)
    for part in (one_ref, two_ref, three_ref):
        total = total + part[...].astype(F32)
    for at in range(3):
        first_ref[at] = total[:, at * cols : (at + 1) * cols]
    last_ref[...] = total[:, 3 * cols :]


def add_kernel(one_ref, two_ref, out_ref):
    out_ref[...] = one_ref[...] + two_ref[...]


def sums_kernel(experts, *refs):
    *parts, gains_ref, bias_ref, router_ref = refs
    total = parts[0][...]
    for part in parts[1:]:
        total = total + part[...]
    router_ref[...] = total[:experts]
    gains_ref[0:2, :] = total[experts : experts + 2]
    for head in range(HEADS):
        bias_ref[head : head + 1, :] = total[
            experts + 2 : experts + 3, head * BUCKETS : (head + 1) * BUCKETS
        ]


def add(one, two, after):
    return call(
        add_kernel, [struct(one.shape, F32)], [], [one, two], name="add_sums", after=after
    )[0]


def last_sums(grads, keep_a, keep_b, near, sums, senders, pieces, cols, experts):
    if senders != 8:
        part, near, far, _ = scatter_rows(keep_a, keep_b, near, pieces)
        total = lax.psum_scatter(grads[0], "dp", scatter_dimension=0, tiled=True)
        first = jnp.stack([total[:, at * cols : (at + 1) * cols] for at in range(3)])
        weight_sums = (first, total[:, 3 * cols :])
        sums = [lax.psum(sums, ("dp", "tensor"))]
    else:
        near_two = swap(grads[4], "dp", senders, 1)
        near_one = swap(grads[5], "dp", senders, 1)
        sums = add(sums, swap(sums, "tensor", pieces, 1), [near])
        got = swap(sums, "tensor", pieces, 2)
        other = call(
            lambda keep, got, out: fold_kernel(keep, got.at[1], out),
            [struct(keep_b.shape, BF16)],
            [],
            [keep_b, near],
            name="fold_rows",
            after=[sums],
        )[0]
        part, far = keep_a, swap(other, "tensor", pieces, 2)
        sums = add(sums, got, [other])
        got = swap(sums, "dp", senders, 1)
        six, four = call(
            fold_two_kernel,
            [struct(keep.shape, BF16) for keep in (grads[3], grads[2])],
            [],
            [grads[3], grads[2], near_two],
            name="fold_weights",
            after=[sums],
        )
        arrived = [swap(six, "dp", senders, 6), swap(four, "dp", senders, 4)]
        sums = add(sums, got, [six])
        two = call(
            lambda keep, got, out: fold_kernel(keep, got.at[0], out),
            [struct(grads[1].shape, BF16)],
            [],
            [grads[1], near_one],
            name="fold_weights",
            after=[sums],
        )[0]
        arrived.append(swap(two, "dp", senders, 2))
        sums = [sums] + [swap(sums, "dp", senders, mask) for mask in (6, 4, 2)]
        depth = grads[0].shape[0]
        weight_sums = call(
            functools.partial(finish_kernel, cols),
            [struct((3, depth, cols), F32), struct((depth, cols), F32)],
            [],
            [grads[0], near_one] + arrived,
            name="finish",
        )
    width = sums[0].shape[1]
    small = call(
        functools.partial(sums_kernel, experts),
        [
            struct((8, width), F32),
            struct((HEADS, BUCKETS), F32),
            struct((experts, width), F32),
        ],
        [],
        sums,
        name="sums",
    )
    return weight_sums, (part, near, far), small


def scatter_rows(keep_a, keep_b, near, pieces, after=()):
    other = call(
        lambda keep, got, out: fold_kernel(keep, got.at[1], out),
        [struct(keep_b.shape, BF16)],
        [],
        [keep_b, near],
        name="fold_rows",
        after=after,
    )[0]
    return keep_a, near, swap(other, "tensor", pieces, 2), other


def gather_rows(rows, pieces):
    far = swap(rows, "tensor", pieces, 2)
    near = swap(rows, "tensor", pieces, 1)
    last = swap(far, "tensor", pieces, 1)
    return [rows, near, far, last]


def exchange(blocks, senders, capacity):
    rows, width = blocks.shape
    return lax.all_to_all(
        blocks.reshape(senders, capacity, width), "dp", split_axis=0, concat_axis=0, tiled=True
    ).reshape(rows, width)


def body(
    tokens,
    doc_start,
    routes,
    gain_attn,
    w_qkv,
    w_out,
    rel_bias,
    gain_ffn,
    router,
    w_in,
    w_exp_out,
    out_grad,
):
    pieces = lax.axis_size("tensor")
    senders = lax.axis_size("dp")
    tok_dev, width = tokens.shape
    routes, rel_bias, router = routes.T, rel_bias.T, router.T
    length = tok_dev * pieces
    experts = router.shape[0]
    capacity = max(2, 3 * tok_dev * routes.shape[0] // (2 * experts))
    slots = experts * capacity
    heads = w_out.shape[1] // HDIM
    cols = heads * HDIM
    gain_one = gain_attn.reshape(1, width)
    gain_two = gain_ffn.reshape(1, width)

    (shard,) = call(
        pack_kernel,
        [struct((w_out.shape[0], 4 * cols), BF16)],
        [],
        [w_qkv.transpose(1, 0, 2), w_out],
        name="pack",
        held=(0, 1),
    )
    weights = gather_weights(shard, senders)
    rows = gather_rows(tokens, pieces)
    in_one, out_one = w_in[0], w_exp_out[0]
    out_two = swap(out_one, "tensor", pieces, 2)
    split = width // 3
    in_two_a = swap(in_one[:split], "tensor", pieces, 2)
    in_two_b = swap(in_one[split:], "tensor", pieces, 2)

    slot, grad_out = call(
        functools.partial(slots_kernel, capacity),
        [struct((tok_dev, 128), jnp.int32), struct((slots, width), BF16)],
        [],
        [routes, out_grad],
        flops=2 * slots * tok_dev * width,
        name="slots",
        kept=(0, 1),
    )

    (grad_out,) = call(
        lambda: None,
        [],
        [],
        [],
        name="gathered",
        after=weights[1::2],
        passed=[grad_out],
    )
    whole_weight, whole_rows, projected, attended, lse, keep_a, keep_b, send = call(
        functools.partial(forward_kernel, len(weights), pieces, heads),
        [
            struct((width, 4 * cols), BF16),
            struct((length, width), BF16),
            struct((length, 3 * cols), BF16),
            struct((length, cols), BF16),
            struct((length, 128), F32),
            struct((tok_dev, width), F32),
            struct((tok_dev, width), F32),
            struct((pieces // 2, tok_dev, width), BF16),
        ],
        [],
        [doc_start, rel_bias] + weights + rows + [gain_one],
        smem=2,
        flops=2 * length * width * 4 * cols + 4 * heads * length * length * HDIM,
        name="attend",
        held=tuple(range(2, 2 + len(weights))),
        kept=(0, 1, 2, 3, 4),
        vmem=12,
    )
    pull_own = exchange(grad_out, senders, capacity)
    pull_mate = swap(pull_own, "tensor", pieces, 1)
    far_pull_own = swap(pull_own, "tensor", pieces, 2)
    far_pull_mate = swap(far_pull_own, "tensor", pieces, 1)

    near = swap(send, "tensor", pieces, 1)
    part, near, far, _ = scatter_rows(keep_a, keep_b, near, pieces, [out_two, in_two_a])
    mixed, normed_two, gates, outgoing = call(
        dispatch_kernel,
        [
            struct((tok_dev, width), F32),
            struct((tok_dev, width), BF16),
            struct((tok_dev, 128), F32),
            struct((slots, width + GATE_LANES), BF16),
        ],
        [],
        [tokens, part, near, far, gain_two, router, routes, slot],
        flops=2 * slots * tok_dev * width,
        name="dispatch",
        after=[pull_own],
        kept=(0, 1, 2),
    )
    slot_own = exchange(outgoing, senders, capacity)
    slot_mate = swap(slot_own, "tensor", pieces, 1)
    payload = width + GATE_LANES
    units = in_one.shape[1]
    expert_flops = 12 * slots * width * units
    hidden_one, pre_one, row_total, gate_total = call(
        own_slice_kernel,
        [struct((2 * slots, units), BF16)] * 2
        + [struct((2 * slots, width), F32), struct((2 * slots, GATE_LANES), F32)],
        [],
        [slot_own, slot_mate, pull_own, pull_mate, in_one, out_one],
        flops=expert_flops,
        name="own_slice",
        prompt=True,
        held=(4, 5),
        kept=(0, 1),
        vmem=14,
    )
    hidden_two, row_keep, row_send = call(
        far_slice_kernel,
        [
            struct((2 * slots, units), BF16),
            struct((slots, payload), F32),
            struct((slots, payload), BF16),
        ],
        [pltpu.VMEM((2 * slots, width), F32), pltpu.VMEM((width, units), BF16)],
        [slot_own, slot_mate, pull_own, pull_mate, in_two_a, in_two_b, out_two, row_total, gate_total],
        flops=expert_flops,
        name="far_slice",
        prompt=True,
        after=[far_pull_own],
        held=(4, 5, 6),
        kept=(0,),
        vmem=14,
    )
    row_mate = swap(row_send, "tensor", pieces, 1)
    far_own = swap(slot_own, "tensor", pieces, 2)
    (row_out,) = call(
        merge_kernel,
        [struct((slots, payload), BF16)],
        [],
        [row_keep, row_mate],
        name="merge",
    )
    back = exchange(row_out, senders, capacity)

    far_mate = swap(far_own, "tensor", pieces, 1)
    out_keep, out_send = call(
        expert_out_kernel,
        [struct((slots, width), F32), struct((slots, width), BF16)],
        [],
        [hidden_one, hidden_two, out_one, out_two],
        flops=4 * 2 * slots * width * in_one.shape[1],
        name="expert_out",
        held=(0, 1, 2, 3),
        after=[far_own],
        vmem=10,
    )
    grad_in, grad_out_sum, graded = call(
        weight_grad_kernel,
        [struct(in_one.shape, F32), struct(out_one.shape, F32), struct((8, 128), F32)],
        [
            pltpu.VMEM((width, 4 * slots), BF16),
            pltpu.VMEM((4 * slots, width), BF16),
            pltpu.VMEM((2 * slots, in_one.shape[1]), BF16),
            pltpu.VMEM((2 * slots, in_one.shape[1]), BF16),
        ],
        [
            slot_own,
            slot_mate,
            pull_own,
            pull_mate,
            far_own,
            far_mate,
            far_pull_own,
            far_pull_mate,
            in_one,
            out_one,
            hidden_one,
            pre_one,
        ],
        flops=24 * slots * width * in_one.shape[1],
        name="weight_grads",
        held=tuple(range(12)),
        after=[out_send],
        vmem=26,
    )

    sum_rows = -(-(experts + 3) // 8) * 8
    mixed_grad, mixed_low, sums_two = call(
        combine_kernel,
        [
            struct((tok_dev, width), F32),
            struct((tok_dev, width), BF16),
            struct((sum_rows, width), F32),
        ],
        [],
        [back, slot, gates, mixed, normed_two, router, routes, out_grad, gain_two],
        flops=2 * slots * tok_dev * width,
        name="combine",
        after=[graded],
        held=(1, 2, 3, 4, 7),
    )
    expert_out = fold(out_keep, swap(out_send, "tensor", pieces, 1), "fold_out", [mixed_low])
    returned = exchange(expert_out, senders, capacity)
    (result,) = call(
        result_kernel,
        [struct((tok_dev, width), BF16)],
        [],
        [returned, slot, gates, mixed],
        flops=4 * slots * tok_dev * width,
        name="result",
        held=(1, 2, 3),
    )

    lows = gather_rows(mixed_low, pieces)
    parts = len(weights)
    if parts > 1:
        depth = width // parts
        grad_shapes = [struct((depth, 4 * cols), F32)] * (parts // 2)
        grad_shapes += [struct((2, depth, 4 * cols), BF16)] * 2
        grad_scratch = [pltpu.VMEM((width, 4 * cols), F32)]
    else:
        grad_shapes = [struct((width, 4 * cols), F32)]
        grad_scratch = []
    *weight_grads, keep_a, keep_b, send, sums = call(
        functools.partial(backward_kernel, parts, pieces, heads, experts),
        grad_shapes
        + [
            struct((tok_dev, width), F32),
            struct((tok_dev, width), F32),
            struct((pieces // 2, tok_dev, width), BF16),
            struct((sum_rows, width), F32),
        ],
        [
            pltpu.VMEM((length, width), BF16),
            pltpu.VMEM((length, 3 * cols), BF16),
            pltpu.VMEM((length, width), F32),
        ]
        + grad_scratch,
        [doc_start, rel_bias]
        + lows
        + [whole_weight, whole_rows, projected, attended, lse, gain_one, sums_two],
        smem=2,
        name="attend_back",
        prompt=True,
        held=tuple(range(2 + pieces, 7 + pieces)),
        vmem=16,
    )
    near = swap(send, "tensor", pieces, 1)
    (first_sum, last_sum), (part, near, far), (gains, bias_grad, router_grad) = last_sums(
        weight_grads, keep_a, keep_b, near, sums, senders, pieces, cols, experts
    )
    (input_grad,) = call(
        input_kernel,
        [struct((tok_dev, width), BF16)],
        [],
        [tokens, gain_one, mixed_grad, part, near, far],
        name="input_grad",
        held=(0, 2),
    )
    return (
        result,
        input_grad,
        gains[1],
        first_sum.transpose(1, 0, 2),
        last_sum,
        bias_grad.T,
        gains[0],
        router_grad.T,
        grad_in[None],
        grad_out_sum[None],
    )


def solution(mesh):
    in_specs = (
        P(("dp", "tensor"), None),
        P("dp"),
        P(("dp", "tensor"), None),
        P(),
        P("dp", None, "tensor"),
        P("dp", "tensor"),
        P(),
        P(),
        P(),
        P("dp", None, "tensor"),
        P("dp", "tensor", None),
        P(("dp", "tensor"), None),
    )
    out_specs = (
        P(("dp", "tensor"), None),
        P(("dp", "tensor"), None),
        P(),
        P("dp", None, "tensor"),
        P("dp", "tensor"),
        P(),
        P(),
        P(),
        P("dp", None, "tensor"),
        P("dp", "tensor", None),
    )
    return jax.shard_map(body, mesh=mesh, in_specs=in_specs, out_specs=out_specs, check_vma=False)
```

time: 259 us -> 200 us (0.77)
  waiting for transfers between devices: 103 us -> 67.1 us
  Pallas kernels: 35.5 us -> 64.5 us
  matrix products: 26.7 us -> 0 us
  local copies, waits for them, and re-layouts: 31.4 us -> 7.82 us
  other arithmetic: 6.32 us -> 0 us
  starting transfers between devices: 54.7 us -> 58.9 us
    pallas_call x9 -> x24, Pallas kernels: 35.5 us -> 64.5 us  [call(): pl.pallas_call(run, grid=(1,), out_shape=out_shape + [jax.ShapeDtypeStruc...]
    ppermute x37 -> x39, waiting for transfers between devices: 80.2 us -> 52.4 us  [swap(): return lax.ppermute(value, axis, [(i, i ^ mask) for i in range(size)])]
    dot_general x8 -> x0, matrix products: 26.7 us -> none  [dot(): lax.dot_general(left, right, dims, preferred_element_type=F32, precision=...]
    unnamed x106 -> x62, local copies, waits for them, and re-layouts: 23.9 us -> 5.25 us
    all_to_all x4, waiting for transfers between devices: 22.4 us -> 14.6 us  [exchange(): lax.all_to_all(blocks.reshape(senders, capacity, width), 'dp', split_axis...]
    ppermute x37 -> x39, starting transfers between devices: 33.7 us -> 38.9 us  [swap(): return lax.ppermute(value, axis, [(i, i ^ mask) for i in range(size)])]
    convert_element_type x4 -> x0, other arithmetic: 3.95 us -> none  [the longest x1 2.11 us: body(): expert_out = (partial_out[:slots] + out_mate.astype(F32)).astype(BF16)]
  transfers between devices with their start and end apart: 41 -> 43, of which waited for: 16 -> 21; matrix products, arithmetic and copies ran while one was open for 16% -> 1% of each run, Pallas kernels for 9% -> 28%
where the time goes in v2:
time: 200 us; the launch traced here: 199 us
  waiting for transfers between devices  67.1 us (34%)
  Pallas kernels  64.5 us (32%)
  starting transfers between devices  58.9 us (29%)
  local copies, waits for them, and re-layouts  7.82 us (4%)
    pallas_call x24, Pallas kernels, call(): pl.pallas_call(run, grid=(1,), out_shape=out_shape + [jax.ShapeDtypeStruc...  64.5 us
    ppermute x39, waiting for transfers between devices, swap(): return lax.ppermute(value, axis, [(i, i ^ mask) for i in range(size)])  52.4 us
    ppermute x39, starting transfers between devices, swap(): return lax.ppermute(value, axis, [(i, i ^ mask) for i in range(size)])  38.9 us
    all_to_all x4, starting transfers between devices, exchange(): lax.all_to_all(blocks.reshape(senders, capacity, width), 'dp', split_axis...  20 us
    all_to_all x4, waiting for transfers between devices, exchange(): lax.all_to_all(blocks.reshape(senders, capacity, width), 'dp', split_axis...  14.6 us
    unnamed x62, local copies, waits for them, and re-layouts  5.25 us
  transfers between devices with their start and end apart: 43, of which 21 were waited for; matrix products, arithmetic and copies ran while one was open for 1% of the time, Pallas kernels for 28%

profile of v2, /device:TPU:0, one launch (start us, length us, event | category | flops | bytes accessed | tf_op | source)
XLA Modules:
  0.0 199.2 jit_solution(8366641970161122004)
XLA Ops:
  0.6 3.0 %collective-permute-start.11 = (bf16[768,768]{1,0:T(8,128)(2,1)}, bf16[768,768]{1,0:T(8,128)(2,1)}, u32[]{:S(2)}, u32[]{:S(2)}) collective-permute-start(bf16[768,768]{1,0:T(8,128)(2,1)} %bitcast.46), channel_id=1, source_target_pairs={{0,2},{1,3},{2,0},{3,1},{4,6},{5,7},{6,4},{7,5},{8,10},{9,11},{10,... | collective-permute-start | bytes 3538952 | tf_op jit(solution)/shard_map/ppermute | solution.py:651
  6.3 2.6 %collective-permute-start.3 = (bf16[96,768]{1,0:T(8,128)(2,1)S(1)}, bf16[96,768]{1,0:T(8,128)(2,1)S(1)}, u32[]{:S(2)}, u32[]{:S(2)}) collective-permute-start(bf16[96,768]{1,0:T(8,128)(2,1)S(1)} %pack.1.refs_2_), channel_id=1, source_target_pairs={{0,16},{4,20},{8,24},{12,28},{16,0},{20,4},{24,8},{28,12},{1,17},{... | collective-permute-start | bytes 442376 | tf_op jit(solution)/shard_map/ppermute | solution.py:651
  13.4 6.8 %collective-permute-done.3.refs_6_ = bf16[96,768]{1,0:T(8,128)(2,1)S(1)} collective-permute-done((bf16[96,768]{1,0:T(8,128)(2,1)S(1)}, bf16[96,768]{1,0:T(8,128)(2,1)S(1)}, u32[]{:S(2)}, u32[]{:S(2)}) %collective-permute-start.3) | collective-permute-done | bytes 147488 | tf_op jit(solution)/shard_map/ppermute | solution.py:651
  28.9 4.5 %all-to-all-start = ((bf16[8,48,768]{2,1,0:T(8,128)(2,1)}), bf16[8,48,768]{2,1,0:T(8,128)(2,1)S(1)}, u32[]{:S(2)}, u32[]{:S(2)}) async-start(bf16[8,48,768]{2,1,0:T(8,128)(2,1)} %bitcast.35), calls=%async_computation | async-start | bytes 1179648 | tf_op jit(solution)/shard_map/all_to_all | solution.py:807
  36.9 8.2 %attend.1 = (bf16[768,768]{1,0:T(8,128)(2,1)}, bf16[512,768]{1,0:T(8,128)(2,1)}, bf16[512,576]{1,0:T(8,128)(2,1)}, bf16[512,192]{1,0:T(8,128)(2,1)}, f32[512,128...) custom-call(s32[512]{0:T(512)S(1)} %copy-done.21, ...), custom_call_target="tpu_custom_call" | custom-call | flops 805306368 | bytes 6167040 | tf_op jit(solution)/shard_map/attend/pallas_call | solution.py:108
  49.2 4.8 %collective-permute-done.13.refs_3_ = bf16[128,768]{1,0:T(8,128)(2,1)S(1)} collective-permute-done((bf16[128,768]{1,0:T(8,128)(2,1)S(1)}, bf16[128,768]{1,0:T(8,128)(2,1)S(1)}, u32[]{:S(2)}, u32[]{:S(2)}) %collective-permute-start.13) | collective-permute-done | bytes 196640 | tf_op jit(solution)/shard_map/ppermute | solution.py:651
  55.6 6.2 %all-to-all-start.1 = ((bf16[8,48,896]{2,1,0:T(8,128)(2,1)}), bf16[8,48,896]{2,1,0:T(8,128)(2,1)S(1)}, u32[]{:S(2)}, u32[]{:S(2)}) async-start(bf16[8,48,896]{2,1,0:T(8,128)(2,1)} %bitcast.8), calls=%async_computation.1 | async-start | bytes 1376256 | tf_op jit(solution)/shard_map/all_to_all | solution.py:807
  64.2 14.6 %all-to-all-done.1 = bf16[8,48,896]{2,1,0:T(8,128)(2,1)S(1)} async-done(((bf16[8,48,896]{2,1,0:T(8,128)(2,1)}), bf16[8,48,896]{2,1,0:T(8,128)(2,1)S(1)}, u32[]{:S(2)}, u32[]{:S(2)}) %all-to-all-start.1) | async-done | bytes 688160 | tf_op jit(solution)/shard_map/all_to_all | solution.py:807
  81.8 7.8 %own_slice.1 = (bf16[768,768]{1,0:T(8,128)(2,1)}, bf16[768,768]{1,0:T(8,128)(2,1)}, f32[768,768]{1,0:T(8,128)S(1)}, f32[768,128]{1,0:T(8,128)S(1)}) custom-call(bf16[384,896]{1,0:T(8,128)(2,1)S(1)} %bitcast.30, bf16[384,896]{1,0:T(8,128)(2,1)S(1)} %collective-permute-done.14.refs_1_, bf16[384,768]{1,0:T(8,128)(2,1)S(1)} %bitcast.27, ...), custom_call_target="tpu_custom_call" | custom-call | flops 1 | bytes 1 | tf_op jit(solution)/shard_map/own_slice/pallas_call | solution.py:108
  89.6 5.1 %collective-permute-done.17.refs_9_.refs_6_ = bf16[384,768]{1,0:T(8,128)(2,1)} collective-permute-done((bf16[384,768]{1,0:T(8,128)(2,1)S(1)}, bf16[384,768]{1,0:T(8,128)(2,1)}, u32[]{:S(2)}, u32[]{:S(2)}) %collective-permute-start.17) | collective-permute-done | bytes 589856 | tf_op jit(solution)/shard_map/ppermute | solution.py:651
  94.7 6.9 %far_slice.1 = (bf16[768,768]{1,0:T(8,128)(2,1)}, f32[384,896]{1,0:T(8,128)S(1)}, bf16[384,896]{1,0:T(8,128)(2,1)S(1)}) custom-call(bf16[384,896]{1,0:T(8,128)(2,1)S(1)} %bitcast.31, bf16[384,896]{1,0:T(8,128)(2,1)S(1)} %collective-permute-done.14.refs_1_, bf16[384,768]{1,0:T(8,128)(2,1)S(1)} %bitcast.28, ...), custom_call_target="tpu_custom_call" | custom-call | flops 1 | bytes 1 | tf_op jit(solution)/shard_map/far_slice/pallas_call | solution.py:108
  105.1 4.7 %all-to-all-start.2 = ((bf16[8,48,896]{2,1,0:T(8,128)(2,1)}), bf16[8,48,896]{2,1,0:T(8,128)(2,1)S(1)}, u32[]{:S(2)}, u32[]{:S(2)}) async-start(bf16[8,48,896]{2,1,0:T(8,128)(2,1)} %bitcast.12), calls=%async_computation.2 | async-start | bytes 1376256 | tf_op jit(solution)/shard_map/all_to_all | solution.py:807
  109.7 9.8 %collective-permute-done.18.refs_4_ = bf16[384,896]{1,0:T(8,128)(2,1)} collective-permute-done((bf16[384,896]{1,0:T(8,128)(2,1)S(1)}, bf16[384,896]{1,0:T(8,128)(2,1)}, u32[]{:S(2)}, u32[]{:S(2)}) %collective-permute-start.18) | collective-permute-done | bytes 688160 | tf_op jit(solution)/shard_map/ppermute | solution.py:651
  120.1 5.2 %expert_out.1 = (f32[384,768]{1,0:T(8,128)S(1)}, bf16[384,768]{1,0:T(8,128)(2,1)}) custom-call(bf16[768,768]{1,0:T(8,128)(2,1)} %get-tuple-element.62.refs_0_.refs_10_, bf16[768,768]{1,0:T(8,128)(2,1)} %get-tuple-element.65.refs_1_, bf16[768,768]{1,0:T(8,128)(2,1)} %bitcast.48, bf16[768,768]{1,0:T(8,128)(2,1)} %collective-permute-done.11.refs_2_.refs_6_.refs_3_, ...), custom_call_target="tpu_custom_call" | custom-call | flops 1811939328 | bytes 6488064 | tf_op jit(solution)/shard_map/expert_out/pallas_call | solution.py:108
  126.3 12.0 %weight_grads.1 = (f32[768,768]{1,0:T(8,128)}, f32[768,768]{1,0:T(8,128)}, f32[8,128]{1,0:T(8,128)S(1)}) custom-call(bf16[384,896]{1,0:T(8,128)(2,1)} %bitcast.33, bf16[384,896]{1,0:T(8,128)(2,1)} %copy-done.3, bf16[384,768]{1,0:T(8,128)(2,1)} %bitcast.24, bf16[384,768]{1,0:T(8,128)(2,1)} %copy-done.4, bf16[384,896]{1,0:T(8,128)(2,1)} %collective-permute-done.18.refs_4_, ...), custom_call_target="tpu_custom_call" | custom-call | flops 5435817984 | bytes 14553088 | tf_op jit(solution)/shard_map/weight_grads/pallas_call | solution.py:108
  138.3 2.4 %combine.1 = (f32[128,768]{1,0:T(8,128)S(1)}, bf16[128,768]{1,0:T(8,128)(2,1)S(1)}, f32[16,768]{1,0:T(8,128)S(1)}) custom-call(bf16[384,896]{1,0:T(8,128)(2,1)S(1)} %bitcast.34, s32[128,128]{1,0:T(8,128)} %get-tuple-element.59.refs_7_.refs_1_, f32[128,128]{1,0:T(8,128)} %get-tuple-element.70.refs_2_, f32[128,768]{1,0:T(8,128)} %get-tuple-element.71.refs_3_, ...), custom_call_target="tpu_custom_call" | custom-call | flops 75497472 | bytes 2260992 | tf_op jit(solution)/shard_map/combine/pallas_call | solution.py:108
  143.2 4.7 %all-to-all-start.3 = ((bf16[8,48,768]{2,1,0:T(8,128)(2,1)}), bf16[8,48,768]{2,1,0:T(8,128)(2,1)S(1)}, u32[]{:S(2)}, u32[]{:S(2)}) async-start(bf16[8,48,768]{2,1,0:T(8,128)(2,1)} %bitcast.14), calls=%async_computation.3 | async-start | bytes 1179648 | tf_op jit(solution)/shard_map/all_to_all | solution.py:807
  149.6 9.8 %attend_back.1 = (f32[96,768]{1,0:T(8,128)S(1)}, f32[96,768]{1,0:T(8,128)S(1)}, f32[96,768]{1,0:T(8,128)S(1)}, f32[96,768]{1,0:T(8,128)S(1)}, bf16[2,96,768]{2,1...) custom-call(s32[512]{0:T(512)S(1)} %copy-done.21, ...), custom_call_target="tpu_custom_call" | custom-call | flops 1 | bytes 1 | tf_op jit(solution)/shard_map/attend_back/pallas_call | solution.py:108
  164.4 2.7 %collective-permute-done.29.refs_1_ = f32[16,768]{1,0:T(8,128)S(1)} collective-permute-done((f32[16,768]{1,0:T(8,128)S(1)}, f32[16,768]{1,0:T(8,128)S(1)}, u32[]{:S(2)}, u32[]{:S(2)}) %collective-permute-start.29) | collective-permute-done | bytes 49184 | tf_op jit(solution)/shard_map/ppermute | solution.py:651
  170.0 6.5 %collective-permute-done.30.refs_1_ = f32[16,768]{1,0:T(8,128)S(1)} collective-permute-done((f32[16,768]{1,0:T(8,128)S(1)}, f32[16,768]{1,0:T(8,128)S(1)}, u32[]{:S(2)}, u32[]{:S(2)}) %collective-permute-start.30) | collective-permute-done | bytes 49184 | tf_op jit(solution)/shard_map/ppermute | solution.py:651
  176.5 3.6 %collective-permute-start.32 = (f32[16,768]{1,0:T(8,128)S(1)}, f32[16,768]{1,0:T(8,128)S(1)}, u32[]{:S(2)}, u32[]{:S(2)}) collective-permute-start(f32[16,768]{1,0:T(8,128)S(1)} %add_sums.5.refs_0_.refs_2_), channel_id=1, source_target_pairs={{0,24},{4,28},{8,16},{12,20},{16,8},{20,12},{24,0},{28,4},{1,25},{... | collective-permute-start | bytes 147464 | tf_op jit(solution)/shard_map/ppermute | solution.py:651
  180.9 3.5 %collective-permute-start.36 = (bf16[96,768]{1,0:T(8,128)(2,1)S(1)}, bf16[96,768]{1,0:T(8,128)(2,1)S(1)}, u32[]{:S(2)}, u32[]{:S(2)}) collective-permute-start(bf16[96,768]{1,0:T(8,128)(2,1)S(1)} %get-tuple-element.90.refs_2_), channel_id=1, source_target_pairs={{0,24},{4,28},{8,16},{12,20},{16,8},{20,12},{24,0},{28,4},{1,25},{... | collective-permute-start | bytes 442376 | tf_op jit(solution)/shard_map/ppermute | solution.py:651
  184.6 5.9 %collective-permute-done.33.refs_2_ = f32[16,768]{1,0:T(8,128)S(1)} collective-permute-done((f32[16,768]{1,0:T(8,128)S(1)}, f32[16,768]{1,0:T(8,128)S(1)}, u32[]{:S(2)}, u32[]{:S(2)}) %collective-permute-start.33) | collective-permute-done | bytes 49184 | tf_op jit(solution)/shard_map/ppermute | solution.py:651
  193.8 2.2 %result.1 = bf16[128,768]{1,0:T(8,128)(2,1)} custom-call(bf16[384,768]{1,0:T(8,128)(2,1)S(1)} %bitcast.36, s32[128,128]{1,0:T(8,128)} %get-tuple-element.59.refs_7_.refs_1_, f32[128,128]{1,0:T(8,128)} %get-tuple-element.70.refs_2_, f32[128,768]{1,0:T(8,128)} %get-tuple-element.71.refs_3_), custom_call_target="tpu_custom_call" | custom-call | flops 150994944 | bytes 1310720 | tf_op jit(solution)/shard_map/result/pallas_call | solution.py:108
  (153 shorter events, 55.0 us)
Async XLA Ops:
  0.6 46.2 %collective-permute-start.11 = (bf16[768,768]{1,0:T(8,128)(2,1)}, bf16[768,768]{1,0:T(8,128)(2,1)}, u32[]{:S(2)}, u32[]{:S(2)}) collective-permute-start(bf16[768,768]{1,0:T(8,128)(2,1)} %bitcast.46), channel_id=1, source_target_pairs={{0,2},{1,3},{2,0},{3,1},{4,6},{5,7},{6,4},{7,5},{8,10},{9,11},{10,... | collective-permute-start | bytes 3538952 | tf_op jit(solution)/shard_map/ppermute | solution.py:651
  6.3 13.9 %collective-permute-start.3 = (bf16[96,768]{1,0:T(8,128)(2,1)S(1)}, bf16[96,768]{1,0:T(8,128)(2,1)S(1)}, u32[]{:S(2)}, u32[]{:S(2)}) collective-permute-start(bf16[96,768]{1,0:T(8,128)(2,1)S(1)} %pack.1.refs_2_), channel_id=1, source_target_pairs={{0,16},{4,20},{8,24},{12,28},{16,0},{20,4},{24,8},{28,12},{1,17},{... | collective-permute-start | bytes 442376 | tf_op jit(solution)/shard_map/ppermute | solution.py:651
  8.9 12.8 %collective-permute-start.5 = (bf16[96,768]{1,0:T(8,128)(2,1)S(1)}, bf16[96,768]{1,0:T(8,128)(2,1)S(1)}, u32[]{:S(2)}, u32[]{:S(2)}) collective-permute-start(bf16[96,768]{1,0:T(8,128)(2,1)S(1)} %pack.1.refs_2_), channel_id=1, source_target_pairs={{0,24},{4,28},{8,16},{12,20},{16,8},{20,12},{24,0},{28,4},{1,25},{... | collective-permute-start | bytes 442376 | tf_op jit(solution)/shard_map/ppermute | solution.py:651
  9.1 13.1 %collective-permute-start = (bf16[96,768]{1,0:T(8,128)(2,1)S(1)}, bf16[96,768]{1,0:T(8,128)(2,1)S(1)}, u32[]{:S(2)}, u32[]{:S(2)}) collective-permute-start(bf16[96,768]{1,0:T(8,128)(2,1)S(1)} %pack.1.refs_2_), channel_id=1, source_target_pairs={{0,4},{4,0},{8,12},{12,8},{16,20},{20,16},{24,28},{28,24},{1,5},{5... | collective-permute-start | bytes 442376 | tf_op jit(solution)/shard_map/ppermute | solution.py:651
  11.9 14.2 %collective-permute-start.2 = (bf16[96,768]{1,0:T(8,128)(2,1)S(1)}, bf16[96,768]{1,0:T(8,128)(2,1)S(1)}, u32[]{:S(2)}, u32[]{:S(2)}) collective-permute-start(bf16[96,768]{1,0:T(8,128)(2,1)S(1)} %collective-permute-done.1.refs_4_), channel_id=1, source_target_pairs={{0,4},{4,0},{8,12},{12,8},{16,20},{20,16},{24,28},{28,24},{1,5},{5... | collective-permute-start | bytes 442376 | tf_op jit(solution)/shard_map/ppermute | solution.py:651
  22.2 11.8 %collective-permute-start.8 = (bf16[128,768]{1,0:T(8,128)(2,1)}, bf16[128,768]{1,0:T(8,128)(2,1)S(1)}, u32[]{:S(2)}, u32[]{:S(2)}) collective-permute-start(bf16[128,768]{1,0:T(8,128)(2,1)} %refs_0_.7), channel_id=1, source_target_pairs={{0,2},{1,3},{2,0},{3,1},{4,6},{5,7},{6,4},{7,5},{8,10},{9,11},{10,... | collective-permute-start | bytes 589832 | tf_op jit(solution)/shard_map/ppermute | solution.py:651
  28.9 20.2 %all-to-all-start = ((bf16[8,48,768]{2,1,0:T(8,128)(2,1)}), bf16[8,48,768]{2,1,0:T(8,128)(2,1)S(1)}, u32[]{:S(2)}, u32[]{:S(2)}) async-start(bf16[8,48,768]{2,1,0:T(8,128)(2,1)} %bitcast.35), calls=%async_computation | async-start | bytes 1179648 | tf_op jit(solution)/shard_map/all_to_all | solution.py:807
  35.1 11.6 %collective-permute-start.12 = (bf16[256,768]{1,0:T(8,128)(2,1)S(1)}, bf16[256,768]{1,0:T(8,128)(2,1)S(1)}, u32[]{:S(2)}, u32[]{:S(2)}) collective-permute-start(bf16[256,768]{1,0:T(8,128)(2,1)S(1)} %slice_bitcast_fusion.1), channel_id=1, source_target_pairs={{0,2},{1,3},{2,0},{3,1},{4,6},{5,7},{6,4},{7,5},{8,10},{9,11},{10,... | collective-permute-start | bytes 1179656 | tf_op jit(solution)/shard_map/ppermute | solution.py:651
  55.6 23.2 %all-to-all-start.1 = ((bf16[8,48,896]{2,1,0:T(8,128)(2,1)}), bf16[8,48,896]{2,1,0:T(8,128)(2,1)S(1)}, u32[]{:S(2)}, u32[]{:S(2)}) async-start(bf16[8,48,896]{2,1,0:T(8,128)(2,1)} %bitcast.8), calls=%async_computation.1 | async-start | bytes 1376256 | tf_op jit(solution)/shard_map/all_to_all | solution.py:807
  62.7 26.9 %collective-permute-start.16 = (bf16[512,768]{1,0:T(8,128)(2,1)}, bf16[512,768]{1,0:T(8,128)(2,1)S(1)}, u32[]{:S(2)}, u32[]{:S(2)}) collective-permute-start(bf16[512,768]{1,0:T(8,128)(2,1)} %slice_bitcast_fusion), channel_id=1, source_target_pairs={{0,2},{1,3},{2,0},{3,1},{4,6},{5,7},{6,4},{7,5},{8,10},{9,11},{10,... | collective-permute-start | bytes 2359304 | tf_op jit(solution)/shard_map/ppermute | solution.py:651
  79.3 15.4 %collective-permute-start.17 = (bf16[384,768]{1,0:T(8,128)(2,1)S(1)}, bf16[384,768]{1,0:T(8,128)(2,1)}, u32[]{:S(2)}, u32[]{:S(2)}) collective-permute-start(bf16[384,768]{1,0:T(8,128)(2,1)S(1)} %bitcast.26), channel_id=1, source_target_pairs={{0,2},{1,3},{2,0},{3,1},{4,6},{5,7},{6,4},{7,5},{8,10},{9,11},{10,... | collective-permute-start | bytes 1769480 | tf_op jit(solution)/shard_map/ppermute | solution.py:651
  101.6 18.0 %collective-permute-start.18 = (bf16[384,896]{1,0:T(8,128)(2,1)S(1)}, bf16[384,896]{1,0:T(8,128)(2,1)}, u32[]{:S(2)}, u32[]{:S(2)}) collective-permute-start(bf16[384,896]{1,0:T(8,128)(2,1)S(1)} %bitcast.32), channel_id=1, source_target_pairs={{0,2},{1,3},{2,0},{3,1},{4,6},{5,7},{6,4},{7,5},{8,10},{9,11},{10,... | collective-permute-start | bytes 2064392 | tf_op jit(solution)/shard_map/ppermute | solution.py:651
  105.1 33.2 %all-to-all-start.2 = ((bf16[8,48,896]{2,1,0:T(8,128)(2,1)}), bf16[8,48,896]{2,1,0:T(8,128)(2,1)S(1)}, u32[]{:S(2)}, u32[]{:S(2)}) async-start(bf16[8,48,896]{2,1,0:T(8,128)(2,1)} %bitcast.12), calls=%async_computation.2 | async-start | bytes 1376256 | tf_op jit(solution)/shard_map/all_to_all | solution.py:807
  125.3 17.0 %collective-permute-start.19 = (bf16[384,768]{1,0:T(8,128)(2,1)}, bf16[384,768]{1,0:T(8,128)(2,1)S(1)}, u32[]{:S(2)}, u32[]{:S(2)}) collective-permute-start(bf16[384,768]{1,0:T(8,128)(2,1)} %get-tuple-element.67.refs_12_), channel_id=1, source_target_pairs={{0,1},{1,0},{2,3},{3,2},{4,5},{5,4},{6,7},{7,6},{8,9},{9,8},{10,11... | collective-permute-start | bytes 1769480 | tf_op jit(solution)/shard_map/ppermute | solution.py:651
  143.2 50.6 %all-to-all-start.3 = ((bf16[8,48,768]{2,1,0:T(8,128)(2,1)}), bf16[8,48,768]{2,1,0:T(8,128)(2,1)S(1)}, u32[]{:S(2)}, u32[]{:S(2)}) async-start(bf16[8,48,768]{2,1,0:T(8,128)(2,1)} %bitcast.14), calls=%async_computation.3 | async-start | bytes 1179648 | tf_op jit(solution)/shard_map/all_to_all | solution.py:807
  159.6 10.3 %collective-permute-start.31 = (bf16[2,96,768]{2,1,0:T(8,128)(2,1)S(1)}, bf16[2,96,768]{2,1,0:T(8,128)(2,1)S(1)}, u32[]{:S(2)}, u32[]{:S(2)}) collective-permute-start(bf16[2,96,768]{2,1,0:T(8,128)(2,1)S(1)} %get-tuple-element.89), channel_id=1, source_target_pairs={{0,4},{4,0},{8,12},{12,8},{16,20},{20,16},{24,28},{28,24},{1,5},{5... | collective-permute-start | bytes 884744 | tf_op jit(solution)/shard_map/ppermute | solution.py:651
  161.7 19.3 %collective-permute-start.35 = (bf16[2,96,768]{2,1,0:T(8,128)(2,1)S(1)}, bf16[2,96,768]{2,1,0:T(8,128)(2,1)S(1)}, u32[]{:S(2)}, u32[]{:S(2)}) collective-permute-start(bf16[2,96,768]{2,1,0:T(8,128)(2,1)S(1)} %get-tuple-element.93), channel_id=1, source_target_pairs={{0,4},{4,0},{8,12},{12,8},{16,20},{20,16},{24,28},{28,24},{1,5},{5... | collective-permute-start | bytes 884744 | tf_op jit(solution)/shard_map/ppermute | solution.py:651
  167.1 9.4 %collective-permute-start.30 = (f32[16,768]{1,0:T(8,128)S(1)}, f32[16,768]{1,0:T(8,128)S(1)}, u32[]{:S(2)}, u32[]{:S(2)}) collective-permute-start(f32[16,768]{1,0:T(8,128)S(1)} %add_sums.4.refs_3_.refs_0_), channel_id=1, source_target_pairs={{0,4},{4,0},{8,12},{12,8},{16,20},{20,16},{24,28},{28,24},{1,5},{5... | collective-permute-start | bytes 147464 | tf_op jit(solution)/shard_map/ppermute | solution.py:651
  169.1 22.7 %collective-permute-start.28 = (bf16[128,768]{1,0:T(8,128)(2,1)S(1)}, bf16[128,768]{1,0:T(8,128)(2,1)S(1)}, u32[]{:S(2)}, u32[]{:S(2)}) collective-permute-start(bf16[128,768]{1,0:T(8,128)(2,1)S(1)} %fold_rows.3.refs_2_), channel_id=1, source_target_pairs={{0,2},{1,3},{2,0},{3,1},{4,6},{5,7},{6,4},{7,5},{8,10},{9,11},{10,... | collective-permute-start | bytes 589832 | tf_op jit(solution)/shard_map/ppermute | solution.py:651
  176.5 8.0 %collective-permute-start.32 = (f32[16,768]{1,0:T(8,128)S(1)}, f32[16,768]{1,0:T(8,128)S(1)}, u32[]{:S(2)}, u32[]{:S(2)}) collective-permute-start(f32[16,768]{1,0:T(8,128)S(1)} %add_sums.5.refs_0_.refs_2_), channel_id=1, source_target_pairs={{0,24},{4,28},{8,16},{12,20},{16,8},{20,12},{24,0},{28,4},{1,25},{... | collective-permute-start | bytes 147464 | tf_op jit(solution)/shard_map/ppermute | solution.py:651
  180.1 10.4 %collective-permute-start.33 = (f32[16,768]{1,0:T(8,128)S(1)}, f32[16,768]{1,0:T(8,128)S(1)}, u32[]{:S(2)}, u32[]{:S(2)}) collective-permute-start(f32[16,768]{1,0:T(8,128)S(1)} %add_sums.5.refs_0_.refs_2_), channel_id=1, source_target_pairs={{0,16},{4,20},{8,24},{12,28},{16,0},{20,4},{24,8},{28,12},{1,17},{... | collective-permute-start | bytes 147464 | tf_op jit(solution)/shard_map/ppermute | solution.py:651
  180.1 10.4 %collective-permute-start.34 = (f32[16,768]{1,0:T(8,128)S(1)}, f32[16,768]{1,0:T(8,128)S(1)}, u32[]{:S(2)}, u32[]{:S(2)}) collective-permute-start(f32[16,768]{1,0:T(8,128)S(1)} %add_sums.5.refs_0_.refs_2_), channel_id=1, source_target_pairs={{0,8},{4,12},{8,0},{12,4},{16,24},{20,28},{24,16},{28,20},{1,9},{5... | collective-permute-start | bytes 147464 | tf_op jit(solution)/shard_map/ppermute | solution.py:651
  180.9 15.0 %collective-permute-start.36 = (bf16[96,768]{1,0:T(8,128)(2,1)S(1)}, bf16[96,768]{1,0:T(8,128)(2,1)S(1)}, u32[]{:S(2)}, u32[]{:S(2)}) collective-permute-start(bf16[96,768]{1,0:T(8,128)(2,1)S(1)} %get-tuple-element.90.refs_2_), channel_id=1, source_target_pairs={{0,24},{4,28},{8,16},{12,20},{16,8},{20,12},{24,0},{28,4},{1,25},{... | collective-permute-start | bytes 442376 | tf_op jit(solution)/shard_map/ppermute | solution.py:651
  184.5 12.9 %collective-permute-start.37 = (bf16[96,768]{1,0:T(8,128)(2,1)S(1)}, bf16[96,768]{1,0:T(8,128)(2,1)S(1)}, u32[]{:S(2)}, u32[]{:S(2)}) collective-permute-start(bf16[96,768]{1,0:T(8,128)(2,1)S(1)} %get-tuple-element.94), channel_id=1, source_target_pairs={{0,16},{4,20},{8,24},{12,28},{16,0},{20,4},{24,8},{28,12},{1,17},{... | collective-permute-start | bytes 442376 | tf_op jit(solution)/shard_map/ppermute | solution.py:651
  (50 other events, 303.9 us)

commit v3 on v2

--- a/solution.py
+++ b/solution.py
@@ -12,6 +12,7 @@
 HDIM = 64
 BUCKETS = 32
 ROWS = 128
+BLOCK = 256
 GATE_LANES = 128
 
 LIMITS = np.array([19, 21, 24, 27, 31, 35, 40, 46, 52, 59, 67, 77, 87, 99, 113], np.int32)
@@ -82,6 +83,7 @@
     kept=(),
     passed=(),
     prompt=False,
+    parts={},
 ):
     n_in, n_after, n_out = len(args), len(after), len(outs)
     n_pass = len(passed)
@@ -91,7 +93,8 @@
         kernel(*ins, *rest[:n_out], *rest[n_out + n_pass :])
 
     def whole(a):
-        return pl.BlockSpec(a.shape, lambda i: (0,) * len(a.shape))
+        shape = getattr(a, "shape", a)
+        return pl.BlockSpec(shape, lambda i: (0,) * len(shape))
 
     moved = sum(a.size * a.dtype.itemsize for a in list(args) + list(outs))
     args = [
@@ -110,7 +113,7 @@
         grid=(1,),
         out_shape=out_shape + [jax.ShapeDtypeStruct(o.shape, o.dtype) for o in passed],
         in_specs=[pl.BlockSpec(memory_space=pltpu.SMEM)] * smem
-        + [whole(a) for a in args[smem:]]
+        + [whole(parts.get(smem + at, a)) for at, a in enumerate(args[smem:])]
         + [pl.BlockSpec(memory_space=pl.ANY)] * (n_after + n_pass),
         out_specs=[whole(o) for o in outs] + [pl.BlockSpec(memory_space=pl.ANY)] * n_pass,
         scratch_shapes=scratch,
@@ -125,6 +128,10 @@
     )(*args, *after, *passed)
 
 
+def once(value, after, name):
+    return call(lambda: None, [], [], [], name=name, after=after, passed=[value])[0]
+
+
 def columns_of(turned):
     filled = jnp.concatenate(
         [turned.astype(F32), jnp.zeros((8 - turned.shape[0], turned.shape[1]), F32)], axis=0
@@ -132,7 +139,8 @@
     return filled.T.astype(jnp.int32)
 
 
-def pack_kernel(first_ref, last_ref, out_ref):
+def pack_kernel(first_ref, last_ref, in_ref, out_ref, head_ref):
+    head_ref[...] = in_ref[...]
     cols = last_ref.shape[1]
     for at in range(3):
         out_ref[:, at * cols : (at + 1) * cols] = first_ref[at]
@@ -169,30 +177,25 @@
 
 
 def bias_tiles(rel_ref, first_head, heads):
-    column = iota((8, 256), 1)
-    distance = (ROWS - column) & 255
+    wide = 2 * BLOCK
+    distance = (BLOCK - iota((8, wide), 1)) & (wide - 1)
     bucket = bucket_of(distance)
     tiles = []
     for head in range(heads):
-        line = jnp.zeros((8, 256), F32)
+        line = jnp.zeros((8, wide), F32)
         for b in range(BUCKETS):
             line = jnp.where(bucket == b, rel_ref[first_head + head, b], line)
-        wide = jnp.broadcast_to(line[0:1, :], (ROWS, 256))
-        tiles.append(pltpu.roll(wide, 0, 1, stride=1, stride_axis=0))
+        grid = jnp.broadcast_to(line[0:1, :], (BLOCK, wide))
+        tiles.append(pltpu.roll(grid, 0, 1, stride=1, stride_axis=0))
     return tiles
 
 
-def masked_scores(query, keys, tile, far, second, block):
-    width = (block + 1) * ROWS
+def masked_scores(query, keys, tile, second, block):
+    width = (block + 1) * BLOCK
     raw = dot(query, keys, NT) * HDIM**-0.5
-    if block == 0:
-        bias = tile[:, ROWS:]
-    elif block == 1:
-        bias = tile
-    else:
-        bias = jnp.concatenate([jnp.full((ROWS, width - 2 * ROWS), far, F32), tile], axis=1)
-    column = iota((ROWS, width), 1)
-    row = iota((ROWS, width), 0) + block * ROWS
+    bias = tile[:, 2 * BLOCK - width :]
+    column = iota((BLOCK, width), 1)
+    row = iota((BLOCK, width), 0) + block * BLOCK
     starts = jnp.where(row >= second, second, 0)
     allowed = (column <= row) & (column >= starts)
     return jnp.where(allowed, raw + bias, -1e9)
@@ -221,21 +224,20 @@
     normed = (x * scale * gain_ref[...]).astype(BF16)
     proj_out[...] = dot(normed, weight_out[:, : 3 * cols]).astype(BF16)
     tiles = bias_tiles(rel_ref, piece * heads, heads)
-    blocks = x.shape[0] // ROWS
+    blocks = x.shape[0] // BLOCK
     proj = proj_out[...]
-    wide = iota((ROWS, 128), 1)
+    wide = iota((BLOCK, 128), 1)
     for block in range(blocks):
-        here = slice(block * ROWS, (block + 1) * ROWS)
-        upto = slice(0, (block + 1) * ROWS)
+        here = slice(block * BLOCK, (block + 1) * BLOCK)
+        upto = slice(0, (block + 1) * BLOCK)
         done = []
-        kept = jnp.zeros((ROWS, 128), F32)
+        kept = jnp.zeros((BLOCK, 128), F32)
         for head in range(heads):
             at = head * HDIM
             query = proj[here, at : at + HDIM]
             keys = proj[upto, cols + at : cols + at + HDIM]
             values = proj[upto, 2 * cols + at : 2 * cols + at + HDIM]
-            far = rel_ref[piece * heads + head, BUCKETS - 1]
-            scores = masked_scores(query, keys, tiles[head], far, second, block)
+            scores = masked_scores(query, keys, tiles[head], second, block)
             peak = jnp.max(scores, axis=1, keepdims=True)
             shifted = jnp.exp(scores - peak)
             total = jnp.sum(shifted, axis=1, keepdims=True)
@@ -308,42 +310,50 @@
     return x * half, slope
 
 
-def expert_side(source, pull, in_ref, out_ref, here, hidden_out, pre_out, total, fresh):
-    width, hidden_units = in_ref.shape
+def gather_sides(sources, pulls, rows_all, pulls_all):
+    rows, width = pulls[0].shape
+    gates = []
+    for at, (source, pull) in enumerate(zip(sources, pulls)):
+        here = slice(at * rows, (at + 1) * rows)
+        rows_all[here, :] = source[:, :width]
+        pulls_all[here, :] = pull[...]
+        gates.append(lanes_sum(source[:, width:]))
+    return jnp.concatenate(gates, axis=0)
+
+
+def through_slice(rows_all, pulls_all, gate, in_ref, out_ref, hidden_out, pre_out):
+    hidden_units = in_ref.shape[1]
     tile = 256
-    slot_rows = source[:, :width]
-    gate = lanes_sum(source[:, width:])
-    pulls = pull[...]
-    gate_sum = jnp.zeros((source.shape[0], 1), F32)
+    gate_wide = jnp.zeros((rows_all.shape[0], tile), F32)
     for at in range(0, hidden_units, tile):
         there = slice(at, at + tile)
-        weight = in_ref[:, there]
-        pulled = dot(pulls, out_ref[there, :], NT)
-        hidden, slope = gelu_and_slope(dot(slot_rows, weight))
+        pulled = dot(pulls_all[...], out_ref[there, :], NT)
+        hidden, slope = gelu_and_slope(dot(rows_all[...], in_ref[:, there]))
         hidden = hidden.astype(BF16)
-        pre_grad = (pulled * gate * slope).astype(BF16)
-        hidden_out[here, there] = hidden
-        if pre_out is not None:
-            pre_out[here, there] = pre_grad
-        product = dot(pre_grad, weight, NT)
-        if fresh and at == 0:
-            total[here, :] = product
-        else:
-            total[here, :] += product
-        gate_sum += jnp.sum(hidden.astype(F32) * pulled, axis=1, keepdims=True)
-    return gate_sum
+        hidden_out[:, there] = hidden
+        pre_out[:, there] = (pulled * gate * slope).astype(BF16)
+        gate_wide = gate_wide + hidden.astype(F32) * pulled
+    return jnp.sum(gate_wide, axis=1, keepdims=True)
 
 
 def own_slice_kernel(
-    own_ref, mate_ref, pull_own, pull_mate, in_ref, out_ref, hidden_ref, pre_ref, total_ref, sum_ref
+    own_ref,
+    mate_ref,
+    pull_own,
+    pull_mate,
+    in_ref,
+    out_ref,
+    hidden_ref,
+    pre_ref,
+    total_ref,
+    sum_ref,
+    rows_all,
+    pulls_all,
 ):
-    rows = own_ref.shape[0]
-    for side, (source, pull) in enumerate(((own_ref, pull_own), (mate_ref, pull_mate))):
-        here = slice(side * rows, (side + 1) * rows)
-        gate_sum = expert_side(
-            source, pull, in_ref, out_ref, here, hidden_ref, pre_ref, total_ref, True
-        )
-        sum_ref[here, :] = jnp.broadcast_to(gate_sum, (rows, GATE_LANES))
+    gate = gather_sides((own_ref, mate_ref), (pull_own, pull_mate), rows_all, pulls_all)
+    gate_sum = through_slice(rows_all, pulls_all, gate, in_ref, out_ref, hidden_ref, pre_ref)
+    sum_ref[...] = jnp.broadcast_to(gate_sum, sum_ref.shape)
+    total_ref[...] = dot(pre_ref[...], in_ref[...], NT)
 
 
 def far_slice_kernel(
@@ -359,25 +369,24 @@
     hidden_ref,
     keep_ref,
     send_ref,
-    total,
     in_ref,
+    pre_ref,
+    rows_all,
+    pulls_all,
 ):
-    rows = own_ref.shape[0]
-    width, split = in_ref.shape[0], in_a_ref.shape[0]
+    rows, width = pull_own.shape
+    split = in_a_ref.shape[0]
     in_ref[:split, :] = in_a_ref[...]
     in_ref[split:, :] = in_b_ref[...]
-    total[...] = total_ref[...]
-    for side, (source, pull) in enumerate(((mate_ref, pull_mate), (own_ref, pull_own))):
-        here = slice((1 - side) * rows, (2 - side) * rows)
-        gate_sum = sum_ref[here, 0:1] + expert_side(
-            source, pull, in_ref, out_ref, here, hidden_ref, None, total, False
-        )
-        if side == 0:
-            send_ref[:, :width] = total[here, :].astype(BF16)
-            send_ref[:, width:] = three_lanes(gate_sum)
-        else:
-            keep_ref[:, :width] = total[here, :]
-            keep_ref[:, width:] = jnp.broadcast_to(gate_sum, (rows, GATE_LANES))
+    gate = gather_sides((own_ref, mate_ref), (pull_own, pull_mate), rows_all, pulls_all)
+    gate_sum = sum_ref[:, 0:1] + through_slice(
+        rows_all, pulls_all, gate, in_ref, out_ref, hidden_ref, pre_ref
+    )
+    total = total_ref[...] + dot(pre_ref[...], in_ref[...], NT)
+    keep_ref[:, :width] = total[:rows, :]
+    keep_ref[:, width:] = jnp.broadcast_to(gate_sum[:rows], (rows, GATE_LANES))
+    send_ref[:, :width] = total[rows:, :].astype(BF16)
+    send_ref[:, width:] = three_lanes(gate_sum[rows:])
 
 
 def weight_grad_kernel(
@@ -543,29 +552,26 @@
     tiles = bias_tiles(rel_ref, piece * heads, heads)
     proj = proj_ref[...]
     length = proj.shape[0]
-    blocks = length // ROWS
-    flipped = (iota((ROWS, ROWS), 0) + iota((ROWS, ROWS), 1) == ROWS - 1).astype(F32).astype(BF16)
-    line_bucket = bucket_of((ROWS - iota((256, HEADS * BUCKETS), 0)) & 255)
-    target = iota((256, HEADS * BUCKETS), 1)
-    target_row = iota((8, HEADS * BUCKETS), 1)
-    bias_row = jnp.zeros((8, HEADS * BUCKETS), F32)
+    blocks = length // BLOCK
+    flipped = iota((BLOCK, BLOCK), 0) + iota((BLOCK, BLOCK), 1) == BLOCK - 1
+    flipped = flipped.astype(F32).astype(BF16)
+    wide = 2 * BLOCK
+    lines = []
     grads_q, grads_k, grads_v = [], [], []
     for head in range(heads):
         at = head * HDIM
-        far = rel_ref[piece * heads + head, BUCKETS - 1]
-        key_sum = [jnp.zeros((ROWS, HDIM), F32) for _ in range(blocks)]
-        value_sum = [jnp.zeros((ROWS, HDIM), F32) for _ in range(blocks)]
-        near_sum = jnp.zeros((ROWS, 256), F32)
-        far_sum = jnp.zeros((ROWS, ROWS), F32)
+        key_sum = [jnp.zeros((BLOCK, HDIM), F32) for _ in range(blocks)]
+        value_sum = [jnp.zeros((BLOCK, HDIM), F32) for _ in range(blocks)]
+        near_sum = None
         query_done = []
-        for block in range(blocks):
-            here = slice(block * ROWS, (block + 1) * ROWS)
-            upto = slice(0, (block + 1) * ROWS)
+        for block in reversed(range(blocks)):
+            here = slice(block * BLOCK, (block + 1) * BLOCK)
+            upto = slice(0, (block + 1) * BLOCK)
             query = proj[here, at : at + HDIM]
             keys = proj[upto, cols + at : cols + at + HDIM]
             values = proj[upto, 2 * cols + at : 2 * cols + at + HDIM]
             out_grad = att_grad[here, at : at + HDIM]
-            scores = masked_scores(query, keys, tiles[head], far, second, block)
+            scores = masked_scores(query, keys, tiles[head], second, block)
             again = jnp.exp(scores - lse_ref[here, head : head + 1])
             prob_grad = dot(out_grad, values, NT)
             weighted = again * prob_grad
@@ -574,33 +580,34 @@
             value_add = dot(again.astype(BF16), out_grad, TN)
             key_add = dot(score_low, query, TN)
             for other in range(block + 1):
-                there = slice(other * ROWS, (other + 1) * ROWS)
+                there = slice(other * BLOCK, (other + 1) * BLOCK)
                 key_sum[other] = key_sum[other] + key_add[there, :]
                 value_sum[other] = value_sum[other] + value_add[there, :]
-                if other < block - 1:
-                    far_sum = far_sum + score_grad[:, there]
-            if block == 0:
-                near_sum = near_sum + jnp.concatenate(
-                    [jnp.zeros((ROWS, ROWS), F32), score_grad], axis=1
+            if block == 1:
+                near_sum = score_grad
+            else:
+                near_sum = jnp.concatenate(
+                    [near_sum[:, :BLOCK], near_sum[:, BLOCK:] + score_grad], axis=1
                 )
-            else:
-                near_sum = near_sum + score_grad[:, (block - 1) * ROWS :]
-            query_done.append(dot(score_low, keys) * HDIM**-0.5)
+            query_done.insert(0, dot(score_low, keys) * HDIM**-0.5)
         grads_q.append(jnp.concatenate(query_done, axis=0))
         grads_k.append(jnp.concatenate(key_sum, axis=0) * HDIM**-0.5)
         grads_v.append(jnp.concatenate(value_sum, axis=0))
-        first_lane = (piece * heads + head) * BUCKETS
         near_high = near_sum.astype(BF16)
         near_low = (near_sum - near_high.astype(F32)).astype(BF16)
         turned = dot(flipped, near_high) + dot(flipped, near_low)
-        turned = pltpu.roll(turned, ROWS + 1, 1, stride=1, stride_axis=0)
-        line = jnp.broadcast_to(jnp.sum(turned, axis=0, keepdims=True), (8, 256))
-        spread = (line_bucket + first_lane == target).astype(F32)
-        bias_row = bias_row + dot(line, spread, precision=HIGHEST)
-        far_total = jnp.sum(jnp.sum(far_sum, axis=0, keepdims=True), axis=1, keepdims=True)
-        bias_row = bias_row + jnp.where(
-            target_row == first_lane + BUCKETS - 1, far_total, 0.0
-        )
+        turned = pltpu.roll(turned, BLOCK + 1, 1, stride=1, stride_axis=0)
+        lines.append(jnp.sum(turned, axis=0, keepdims=True))
+    lines = jnp.concatenate(lines + [jnp.zeros((8 - heads, wide), F32)], axis=0)
+    line_bucket = bucket_of((BLOCK - iota((wide, 128), 0)) & (wide - 1))
+    spread = (line_bucket == iota((wide, 128), 1)).astype(F32)
+    by_bucket = jnp.concatenate(
+        [dot(lines, spread, precision=HIGHEST), jnp.zeros((8, HEADS * BUCKETS - 128), F32)], axis=1
+    )
+    bias_row = jnp.zeros((1, HEADS * BUCKETS), F32)
+    for head in range(heads):
+        placed = pltpu.roll(by_bucket, (piece * heads + head) * BUCKETS, 1)
+        bias_row = bias_row + placed[head : head + 1, :]
     grad_proj[...] = jnp.concatenate(grads_q + grads_k + grads_v, axis=1).astype(BF16)
     x = row_ref[...].astype(F32)
     scale = lax.rsqrt(jnp.mean(x * x, axis=1, keepdims=True) + 1e-6)
@@ -627,7 +634,7 @@
     sums_out[experts + 1 : experts + 2, :] = jnp.sum(
         normed_grad[...] * unit, axis=0, keepdims=True
     )
-    sums_out[experts + 2 : experts + 3, : HEADS * BUCKETS] = bias_row[0:1, :]
+    sums_out[experts + 2 : experts + 3, : HEADS * BUCKETS] = bias_row
     for at in range(pieces):
         mine = normed_grad[pl.ds(pl.multiple_of((piece ^ at) * ROWS, ROWS), ROWS), :]
         if at % 2 == 0:
@@ -713,7 +720,7 @@
 
 def add(one, two, after):
     return call(
-        add_kernel, [struct(one.shape, F32)], [], [one, two], name="add_sums", after=after
+        add_kernel, [struct(one.shape, F32)], [], [one, two], name="add_sums", prompt=True, after=after
     )[0]
 
 
@@ -734,7 +741,7 @@
             [struct(keep_b.shape, BF16)],
             [],
             [keep_b, near],
-            name="fold_rows",
+            name="fold_rows", prompt=True,
             after=[sums],
         )[0]
         part, far = keep_a, swap(other, "tensor", pieces, 2)
@@ -745,7 +752,7 @@
             [struct(keep.shape, BF16) for keep in (grads[3], grads[2])],
             [],
             [grads[3], grads[2], near_two],
-            name="fold_weights",
+            name="fold_weights", prompt=True,
             after=[sums],
         )
         arrived = [swap(six, "dp", senders, 6), swap(four, "dp", senders, 4)]
@@ -755,7 +762,7 @@
             [struct(grads[1].shape, BF16)],
             [],
             [grads[1], near_one],
-            name="fold_weights",
+            name="fold_weights", prompt=True,
             after=[sums],
         )[0]
         arrived.append(swap(two, "dp", senders, 2))
@@ -766,7 +773,7 @@
             [struct((3, depth, cols), F32), struct((depth, cols), F32)],
             [],
             [grads[0], near_one] + arrived,
-            name="finish",
+            name="finish", prompt=True,
         )
     width = sums[0].shape[1]
     small = call(
@@ -778,7 +785,7 @@
         ],
         [],
         sums,
-        name="sums",
+        name="sums", prompt=True,
     )
     return weight_sums, (part, near, far), small
 
@@ -789,7 +796,7 @@
         [struct(keep_b.shape, BF16)],
         [],
         [keep_b, near],
-        name="fold_rows",
+        name="fold_rows", prompt=True,
         after=after,
     )[0]
     return keep_a, near, swap(other, "tensor", pieces, 2), other
@@ -836,21 +843,25 @@
     gain_one = gain_attn.reshape(1, width)
     gain_two = gain_ffn.reshape(1, width)
 
-    (shard,) = call(
+    shard, in_head = call(
         pack_kernel,
-        [struct((w_out.shape[0], 4 * cols), BF16)],
+        [
+            struct((w_out.shape[0], 4 * cols), BF16),
+            struct((width // 3, w_in.shape[2]), BF16),
+        ],
         [],
-        [w_qkv.transpose(1, 0, 2), w_out],
+        [w_qkv.transpose(1, 0, 2), w_out, w_in[0]],
         name="pack",
-        held=(0, 1),
+        held=(0, 1, 2),
+        parts={2: (width // 3, w_in.shape[2])},
     )
     weights = gather_weights(shard, senders)
     rows = gather_rows(tokens, pieces)
-    in_one, out_one = w_in[0], w_exp_out[0]
+    out_one = w_exp_out[0]
+    in_one = w_in[0]
     out_two = swap(out_one, "tensor", pieces, 2)
-    split = width // 3
-    in_two_a = swap(in_one[:split], "tensor", pieces, 2)
-    in_two_b = swap(in_one[split:], "tensor", pieces, 2)
+    in_two_a = swap(in_head, "tensor", pieces, 2)
+    in_two_b = swap(in_one[in_head.shape[0] :], "tensor", pieces, 2)
 
     slot, grad_out = call(
         functools.partial(slots_kernel, capacity),
@@ -859,18 +870,11 @@
         [routes, out_grad],
         flops=2 * slots * tok_dev * width,
         name="slots",
+        held=(1,),
         kept=(0, 1),
     )
 
-    (grad_out,) = call(
-        lambda: None,
-        [],
-        [],
-        [],
-        name="gathered",
-        after=weights[1::2],
-        passed=[grad_out],
-    )
+    grad_out = once(grad_out, weights[1::2], "gathered")
     whole_weight, whole_rows, projected, attended, lse, keep_a, keep_b, send = call(
         functools.partial(forward_kernel, len(weights), pieces, heads),
         [
@@ -895,7 +899,6 @@
     pull_own = exchange(grad_out, senders, capacity)
     pull_mate = swap(pull_own, "tensor", pieces, 1)
     far_pull_own = swap(pull_own, "tensor", pieces, 2)
-    far_pull_mate = swap(far_pull_own, "tensor", pieces, 1)
 
     near = swap(send, "tensor", pieces, 1)
     part, near, far, _ = scatter_rows(keep_a, keep_b, near, pieces, [out_two, in_two_a])
@@ -923,14 +926,14 @@
         own_slice_kernel,
         [struct((2 * slots, units), BF16)] * 2
         + [struct((2 * slots, width), F32), struct((2 * slots, GATE_LANES), F32)],
-        [],
+        [pltpu.VMEM((2 * slots, width), BF16)] * 2,
         [slot_own, slot_mate, pull_own, pull_mate, in_one, out_one],
         flops=expert_flops,
         name="own_slice",
         prompt=True,
         held=(4, 5),
         kept=(0, 1),
-        vmem=14,
+        vmem=18,
     )
     hidden_two, row_keep, row_send = call(
         far_slice_kernel,
@@ -939,15 +942,15 @@
             struct((slots, payload), F32),
             struct((slots, payload), BF16),
         ],
-        [pltpu.VMEM((2 * slots, width), F32), pltpu.VMEM((width, units), BF16)],
+        [pltpu.VMEM((width, units), BF16), pltpu.VMEM((2 * slots, units), BF16)]
+        + [pltpu.VMEM((2 * slots, width), BF16)] * 2,
         [slot_own, slot_mate, pull_own, pull_mate, in_two_a, in_two_b, out_two, row_total, gate_total],
         flops=expert_flops,
         name="far_slice",
         prompt=True,
-        after=[far_pull_own],
         held=(4, 5, 6),
         kept=(0,),
-        vmem=14,
+        vmem=20,
     )
     row_mate = swap(row_send, "tensor", pieces, 1)
     far_own = swap(slot_own, "tensor", pieces, 2)
@@ -972,6 +975,8 @@
         after=[far_own],
         vmem=10,
     )
+    far_pull_own = once(far_pull_own, [out_send], "pulled")
+    far_pull_mate = swap(far_pull_own, "tensor", pieces, 1)
     grad_in, grad_out_sum, graded = call(
         weight_grad_kernel,
         [struct(in_one.shape, F32), struct(out_one.shape, F32), struct((8, 128), F32)],
@@ -1025,7 +1030,7 @@
         [],
         [returned, slot, gates, mixed],
         flops=4 * slots * tok_dev * width,
-        name="result",
+        name="result", prompt=True,
         held=(1, 2, 3),
     )
 
@@ -1072,7 +1077,7 @@
         [struct((tok_dev, width), BF16)],
         [],
         [tokens, gain_one, mixed_grad, part, near, far],
-        name="input_grad",
+        name="input_grad", prompt=True,
         held=(0, 2),
     )
     return (

time: 200 us -> 186 us (0.930)
  waiting for transfers between devices: 67.1 us -> 58.3 us
  Pallas kernels: 64.5 us -> 60.4 us
  starting transfers between devices: 58.9 us -> 55.9 us
    ppermute x39, waiting for transfers between devices: 52.4 us -> 43.7 us  [swap(): return lax.ppermute(value, axis, [(i, i ^ mask) for i in range(size)])]
    pallas_call x24 -> x25, Pallas kernels: 64.5 us -> 60.4 us  [call(): pl.pallas_call(run, grid=(1,), out_shape=out_shape + [jax.ShapeDtypeStruc...]
    unnamed x62 -> x66, local copies, waits for them, and re-layouts: 5.25 us -> 8.08 us
  transfers between devices with their start and end apart: 43 -> 43, of which waited for: 21 -> 20; matrix products, arithmetic and copies ran while one was open for 1% -> 1% of each run, Pallas kernels for 28% -> 31%
where the time goes in v3:
time: 186 us; the launch traced here: 185 us
  Pallas kernels  60.4 us (32%)
  waiting for transfers between devices  58.3 us (31%)
  starting transfers between devices  55.9 us (30%)
  local copies, waits for them, and re-layouts  9.63 us (5%)
    pallas_call x25, Pallas kernels, call(): pl.pallas_call(run, grid=(1,), out_shape=out_shape + [jax.ShapeDtypeStruc...  60.4 us
    ppermute x39, waiting for transfers between devices, swap(): return lax.ppermute(value, axis, [(i, i ^ mask) for i in range(size)])  43.7 us
    ppermute x39, starting transfers between devices, swap(): return lax.ppermute(value, axis, [(i, i ^ mask) for i in range(size)])  37.2 us
    all_to_all x4, starting transfers between devices, exchange(): lax.all_to_all(blocks.reshape(senders, capacity, width), 'dp', split_axis...  18.7 us
    all_to_all x4, waiting for transfers between devices, exchange(): lax.all_to_all(blocks.reshape(senders, capacity, width), 'dp', split_axis...  14.6 us
    unnamed x66, local copies, waits for them, and re-layouts  8.08 us
  transfers between devices with their start and end apart: 43, of which 20 were waited for; matrix products, arithmetic and copies ran while one was open for 1% of the time, Pallas kernels for 31%

profile of v3, /device:TPU:0, one launch (start us, length us, event | category | flops | bytes accessed | tf_op | source)
XLA Modules:
  0.0 185.2 jit_solution(15285444574394672362)
XLA Ops:
  0.7 3.0 %collective-permute-start.11 = (bf16[768,768]{1,0:T(8,128)(2,1)}, bf16[768,768]{1,0:T(8,128)(2,1)}, u32[]{:S(2)}, u32[]{:S(2)}) collective-permute-start(bf16[768,768]{1,0:T(8,128)(2,1)} %bitcast.45), channel_id=1, source_target_pairs={{0,2},{1,3},{2,0},{3,1},{4,6},{5,7},{6,4},{7,5},{8,10},{9,11},{10,... | collective-permute-start | bytes 3538952 | tf_op jit(solution)/shard_map/ppermute | solution.py:658
  6.5 2.6 %collective-permute-start.3 = (bf16[96,768]{1,0:T(8,128)(2,1)S(1)}, bf16[96,768]{1,0:T(8,128)(2,1)S(1)}, u32[]{:S(2)}, u32[]{:S(2)}) collective-permute-start(bf16[96,768]{1,0:T(8,128)(2,1)S(1)} %get-tuple-element.58.refs_2_), channel_id=1, source_target_pairs={{0,16},{4,20},{8,24},{12,28},{16,0},{20,4},{24,8},{28,12},{1,17},{... | collective-permute-start | bytes 442376 | tf_op jit(solution)/shard_map/ppermute | solution.py:658
  13.6 6.8 %collective-permute-done.3.refs_6_ = bf16[96,768]{1,0:T(8,128)(2,1)S(1)} collective-permute-done((bf16[96,768]{1,0:T(8,128)(2,1)S(1)}, bf16[96,768]{1,0:T(8,128)(2,1)S(1)}, u32[]{:S(2)}, u32[]{:S(2)}) %collective-permute-start.3) | collective-permute-done | bytes 147488 | tf_op jit(solution)/shard_map/ppermute | solution.py:658
  23.1 2.6 %slots.1 = (s32[128,128]{1,0:T(8,128)}, bf16[384,768]{1,0:T(8,128)(2,1)}) custom-call(s32[2,128]{1,0:T(2,128)S(1)} %bitcast.39, bf16[128,768]{1,0:T(8,128)(2,1)} %refs_7_.1), custom_call_target="tpu_custom_call" | custom-call | flops 75497472 | bytes 852992 | tf_op jit(solution)/shard_map/slots/pallas_call | solution.py:111
  29.1 4.5 %all-to-all-start = ((bf16[8,48,768]{2,1,0:T(8,128)(2,1)}), bf16[8,48,768]{2,1,0:T(8,128)(2,1)S(1)}, u32[]{:S(2)}, u32[]{:S(2)}) async-start(bf16[8,48,768]{2,1,0:T(8,128)(2,1)} %bitcast.33), calls=%async_computation | async-start | bytes 1179648 | tf_op jit(solution)/shard_map/all_to_all | solution.py:814
  37.5 6.5 %attend.1 = (bf16[768,768]{1,0:T(8,128)(2,1)}, bf16[512,768]{1,0:T(8,128)(2,1)}, bf16[512,576]{1,0:T(8,128)(2,1)}, bf16[512,192]{1,0:T(8,128)(2,1)}, f32[512,128...) custom-call(s32[512]{0:T(512)S(1)} %copy-done.21, ...), custom_call_target="tpu_custom_call" | custom-call | flops 805306368 | bytes 6167040 | tf_op jit(solution)/shard_map/attend/pallas_call | solution.py:111
  48.8 4.8 %collective-permute-done.13.refs_3_ = bf16[128,768]{1,0:T(8,128)(2,1)S(1)} collective-permute-done((bf16[128,768]{1,0:T(8,128)(2,1)S(1)}, bf16[128,768]{1,0:T(8,128)(2,1)S(1)}, u32[]{:S(2)}, u32[]{:S(2)}) %collective-permute-start.13) | collective-permute-done | bytes 196640 | tf_op jit(solution)/shard_map/ppermute | solution.py:658
  55.2 6.2 %all-to-all-start.1 = ((bf16[8,48,896]{2,1,0:T(8,128)(2,1)}), bf16[8,48,896]{2,1,0:T(8,128)(2,1)S(1)}, u32[]{:S(2)}, u32[]{:S(2)}) async-start(bf16[8,48,896]{2,1,0:T(8,128)(2,1)} %bitcast.8), calls=%async_computation.1 | async-start | bytes 1376256 | tf_op jit(solution)/shard_map/all_to_all | solution.py:814
  63.8 14.6 %all-to-all-done.1 = bf16[8,48,896]{2,1,0:T(8,128)(2,1)S(1)} async-done(((bf16[8,48,896]{2,1,0:T(8,128)(2,1)}), bf16[8,48,896]{2,1,0:T(8,128)(2,1)S(1)}, u32[]{:S(2)}, u32[]{:S(2)}) %all-to-all-start.1) | async-done | bytes 688160 | tf_op jit(solution)/shard_map/all_to_all | solution.py:814
  81.4 6.8 %own_slice.1 = (bf16[768,768]{1,0:T(8,128)(2,1)}, bf16[768,768]{1,0:T(8,128)(2,1)}, f32[768,768]{1,0:T(8,128)S(1)}, f32[768,128]{1,0:T(8,128)S(1)}) custom-call(bf16[384,896]{1,0:T(8,128)(2,1)S(1)} %bitcast.29, bf16[384,896]{1,0:T(8,128)(2,1)S(1)} %collective-permute-done.14.refs_1_, bf16[384,768]{1,0:T(8,128)(2,1)S(1)} %bitcast.24, ...), custom_call_target="tpu_custom_call" | custom-call | flops 1 | bytes 1 | tf_op jit(solution)/shard_map/own_slice/pallas_call | solution.py:111
  89.1 5.7 %far_slice.1 = (bf16[768,768]{1,0:T(8,128)(2,1)}, f32[384,896]{1,0:T(8,128)S(1)}, bf16[384,896]{1,0:T(8,128)(2,1)S(1)}) custom-call(bf16[384,896]{1,0:T(8,128)(2,1)S(1)} %bitcast.30, bf16[384,896]{1,0:T(8,128)(2,1)S(1)} %collective-permute-done.14.refs_1_, bf16[384,768]{1,0:T(8,128)(2,1)S(1)} %bitcast.25, ...), custom_call_target="tpu_custom_call" | custom-call | flops 1 | bytes 1 | tf_op jit(solution)/shard_map/far_slice/pallas_call | solution.py:111
  98.3 4.1 %all-to-all-start.2 = ((bf16[8,48,896]{2,1,0:T(8,128)(2,1)}), bf16[8,48,896]{2,1,0:T(8,128)(2,1)S(1)}, u32[]{:S(2)}, u32[]{:S(2)}) async-start(bf16[8,48,896]{2,1,0:T(8,128)(2,1)} %bitcast.11), calls=%async_computation.2 | async-start | bytes 1376256 | tf_op jit(solution)/shard_map/all_to_all | solution.py:814
  102.4 4.3 %expert_out.1 = (f32[384,768]{1,0:T(8,128)S(1)}, bf16[384,768]{1,0:T(8,128)(2,1)S(1)}) custom-call(bf16[768,768]{1,0:T(8,128)(2,1)} %get-tuple-element.66.refs_0_.refs_10_, bf16[768,768]{1,0:T(8,128)(2,1)} %get-tuple-element.69.refs_1_, bf16[768,768]{1,0:T(8,128)(2,1)} %bitcast.47, bf16[768,768]{1,0:T(8,128)(2,1)} %collective-permute-done.11.refs_2_.refs_6_.refs_3_, ...), custom_call_target="tpu_custom_call" | custom-call | flops 1811939328 | bytes 6488064 | tf_op jit(solution)/shard_map/expert_out/pallas_call | solution.py:111
  107.6 3.0 %collective-permute-done.21.refs_1_ = bf16[384,768]{1,0:T(8,128)(2,1)S(1)} collective-permute-done((bf16[384,768]{1,0:T(8,128)(2,1)S(1)}, bf16[384,768]{1,0:T(8,128)(2,1)S(1)}, u32[]{:S(2)}, u32[]{:S(2)}) %collective-permute-start.21) | collective-permute-done | bytes 589856 | tf_op jit(solution)/shard_map/ppermute | solution.py:658
  113.4 12.0 %weight_grads.1 = (f32[768,768]{1,0:T(8,128)}, f32[768,768]{1,0:T(8,128)}, f32[8,128]{1,0:T(8,128)S(1)}) custom-call(bf16[384,896]{1,0:T(8,128)(2,1)} %bitcast.31, bf16[384,896]{1,0:T(8,128)(2,1)} %copy-done.3, bf16[384,768]{1,0:T(8,128)(2,1)} %bitcast.22, bf16[384,768]{1,0:T(8,128)(2,1)} %copy-done.6, bf16[384,896]{1,0:T(8,128)(2,1)} %collective-permute-done.17.refs_4_, ...), custom_call_target="tpu_custom_call" | custom-call | flops 5435817984 | bytes 14553088 | tf_op jit(solution)/shard_map/weight_grads/pallas_call | solution.py:111
  125.4 2.3 %combine.1 = (f32[128,768]{1,0:T(8,128)S(1)}, bf16[128,768]{1,0:T(8,128)(2,1)S(1)}, f32[16,768]{1,0:T(8,128)S(1)}) custom-call(bf16[384,896]{1,0:T(8,128)(2,1)S(1)} %bitcast.32, s32[128,128]{1,0:T(8,128)} %get-tuple-element.63.refs_7_.refs_1_, f32[128,128]{1,0:T(8,128)} %get-tuple-element.74.refs_2_, f32[128,768]{1,0:T(8,128)} %get-tuple-element.75.refs_3_, ...), custom_call_target="tpu_custom_call" | custom-call | flops 75497472 | bytes 2260992 | tf_op jit(solution)/shard_map/combine/pallas_call | solution.py:111
  131.3 3.8 %all-to-all-start.3 = ((bf16[8,48,768]{2,1,0:T(8,128)(2,1)}), bf16[8,48,768]{2,1,0:T(8,128)(2,1)S(1)}, u32[]{:S(2)}, u32[]{:S(2)}) async-start(bf16[8,48,768]{2,1,0:T(8,128)(2,1)} %bitcast.13), calls=%async_computation.3 | async-start | bytes 1179648 | tf_op jit(solution)/shard_map/all_to_all | solution.py:814
  136.9 8.2 %attend_back.1 = (f32[96,768]{1,0:T(8,128)S(1)}, f32[96,768]{1,0:T(8,128)S(1)}, f32[96,768]{1,0:T(8,128)S(1)}, f32[96,768]{1,0:T(8,128)S(1)}, bf16[2,96,768]{2,1...) custom-call(s32[512]{0:T(512)S(1)} %copy-done.21, ...), custom_call_target="tpu_custom_call" | custom-call | flops 1 | bytes 1 | tf_op jit(solution)/shard_map/attend_back/pallas_call | solution.py:111
  149.5 3.3 %collective-permute-done.29.refs_1_ = f32[16,768]{1,0:T(8,128)S(1)} collective-permute-done((f32[16,768]{1,0:T(8,128)S(1)}, f32[16,768]{1,0:T(8,128)S(1)}, u32[]{:S(2)}, u32[]{:S(2)}) %collective-permute-start.29) | collective-permute-done | bytes 49184 | tf_op jit(solution)/shard_map/ppermute | solution.py:658
  155.3 7.2 %collective-permute-done.30.refs_1_ = f32[16,768]{1,0:T(8,128)S(1)} collective-permute-done((f32[16,768]{1,0:T(8,128)S(1)}, f32[16,768]{1,0:T(8,128)S(1)}, u32[]{:S(2)}, u32[]{:S(2)}) %collective-permute-start.30) | collective-permute-done | bytes 49184 | tf_op jit(solution)/shard_map/ppermute | solution.py:658
  162.6 3.1 %collective-permute-start.32 = (f32[16,768]{1,0:T(8,128)S(1)}, f32[16,768]{1,0:T(8,128)S(1)}, u32[]{:S(2)}, u32[]{:S(2)}) collective-permute-start(f32[16,768]{1,0:T(8,128)S(1)} %add_sums.5.refs_0_.refs_2_), channel_id=1, source_target_pairs={{0,24},{4,28},{8,16},{12,20},{16,8},{20,12},{24,0},{28,4},{1,25},{... | collective-permute-start | bytes 147464 | tf_op jit(solution)/shard_map/ppermute | solution.py:658
  167.0 3.0 %collective-permute-start.36 = (bf16[96,768]{1,0:T(8,128)(2,1)S(1)}, bf16[96,768]{1,0:T(8,128)(2,1)S(1)}, u32[]{:S(2)}, u32[]{:S(2)}) collective-permute-start(bf16[96,768]{1,0:T(8,128)(2,1)S(1)} %get-tuple-element.94.refs_2_), channel_id=1, source_target_pairs={{0,24},{4,28},{8,16},{12,20},{16,8},{20,12},{24,0},{28,4},{1,25},{... | collective-permute-start | bytes 442376 | tf_op jit(solution)/shard_map/ppermute | solution.py:658
  170.1 5.9 %collective-permute-done.33.refs_2_ = f32[16,768]{1,0:T(8,128)S(1)} collective-permute-done((f32[16,768]{1,0:T(8,128)S(1)}, f32[16,768]{1,0:T(8,128)S(1)}, u32[]{:S(2)}, u32[]{:S(2)}) %collective-permute-start.33) | collective-permute-done | bytes 49184 | tf_op jit(solution)/shard_map/ppermute | solution.py:658
  179.3 2.2 %result.1 = bf16[128,768]{1,0:T(8,128)(2,1)} custom-call(bf16[384,768]{1,0:T(8,128)(2,1)S(1)} %bitcast.34, s32[128,128]{1,0:T(8,128)} %get-tuple-element.63.refs_7_.refs_1_, f32[128,128]{1,0:T(8,128)} %get-tuple-element.74.refs_2_, f32[128,768]{1,0:T(8,128)} %get-tuple-element.75.refs_3_), custom_call_target="tpu_custom_call" | custom-call | flops 1 | bytes 1 | tf_op jit(solution)/shard_map/result/pallas_call | solution.py:111
  (157 shorter events, 57.7 us)
Async XLA Ops:
  0.7 45.6 %collective-permute-start.11 = (bf16[768,768]{1,0:T(8,128)(2,1)}, bf16[768,768]{1,0:T(8,128)(2,1)}, u32[]{:S(2)}, u32[]{:S(2)}) collective-permute-start(bf16[768,768]{1,0:T(8,128)(2,1)} %bitcast.45), channel_id=1, source_target_pairs={{0,2},{1,3},{2,0},{3,1},{4,6},{5,7},{6,4},{7,5},{8,10},{9,11},{10,... | collective-permute-start | bytes 3538952 | tf_op jit(solution)/shard_map/ppermute | solution.py:658
  6.5 13.9 %collective-permute-start.3 = (bf16[96,768]{1,0:T(8,128)(2,1)S(1)}, bf16[96,768]{1,0:T(8,128)(2,1)S(1)}, u32[]{:S(2)}, u32[]{:S(2)}) collective-permute-start(bf16[96,768]{1,0:T(8,128)(2,1)S(1)} %get-tuple-element.58.refs_2_), channel_id=1, source_target_pairs={{0,16},{4,20},{8,24},{12,28},{16,0},{20,4},{24,8},{28,12},{1,17},{... | collective-permute-start | bytes 442376 | tf_op jit(solution)/shard_map/ppermute | solution.py:658
  9.1 12.8 %collective-permute-start.5 = (bf16[96,768]{1,0:T(8,128)(2,1)S(1)}, bf16[96,768]{1,0:T(8,128)(2,1)S(1)}, u32[]{:S(2)}, u32[]{:S(2)}) collective-permute-start(bf16[96,768]{1,0:T(8,128)(2,1)S(1)} %get-tuple-element.58.refs_2_), channel_id=1, source_target_pairs={{0,24},{4,28},{8,16},{12,20},{16,8},{20,12},{24,0},{28,4},{1,25},{... | collective-permute-start | bytes 442376 | tf_op jit(solution)/shard_map/ppermute | solution.py:658
  9.4 13.1 %collective-permute-start = (bf16[96,768]{1,0:T(8,128)(2,1)S(1)}, bf16[96,768]{1,0:T(8,128)(2,1)S(1)}, u32[]{:S(2)}, u32[]{:S(2)}) collective-permute-start(bf16[96,768]{1,0:T(8,128)(2,1)S(1)} %get-tuple-element.58.refs_2_), channel_id=1, source_target_pairs={{0,4},{4,0},{8,12},{12,8},{16,20},{20,16},{24,28},{28,24},{1,5},{5... | collective-permute-start | bytes 442376 | tf_op jit(solution)/shard_map/ppermute | solution.py:658
  12.1 13.6 %collective-permute-start.2 = (bf16[96,768]{1,0:T(8,128)(2,1)S(1)}, bf16[96,768]{1,0:T(8,128)(2,1)S(1)}, u32[]{:S(2)}, u32[]{:S(2)}) collective-permute-start(bf16[96,768]{1,0:T(8,128)(2,1)S(1)} %collective-permute-done.1.refs_4_), channel_id=1, source_target_pairs={{0,4},{4,0},{8,12},{12,8},{16,20},{20,16},{24,28},{28,24},{1,5},{5... | collective-permute-start | bytes 442376 | tf_op jit(solution)/shard_map/ppermute | solution.py:658
  22.5 11.6 %collective-permute-start.8 = (bf16[128,768]{1,0:T(8,128)(2,1)S(1)}, bf16[128,768]{1,0:T(8,128)(2,1)S(1)}, u32[]{:S(2)}, u32[]{:S(2)}) collective-permute-start(bf16[128,768]{1,0:T(8,128)(2,1)S(1)} %copy-done.8), channel_id=1, source_target_pairs={{0,2},{1,3},{2,0},{3,1},{4,6},{5,7},{6,4},{7,5},{8,10},{9,11},{10,... | collective-permute-start | bytes 589832 | tf_op jit(solution)/shard_map/ppermute | solution.py:658
  29.1 19.7 %all-to-all-start = ((bf16[8,48,768]{2,1,0:T(8,128)(2,1)}), bf16[8,48,768]{2,1,0:T(8,128)(2,1)S(1)}, u32[]{:S(2)}, u32[]{:S(2)}) async-start(bf16[8,48,768]{2,1,0:T(8,128)(2,1)} %bitcast.33), calls=%async_computation | async-start | bytes 1179648 | tf_op jit(solution)/shard_map/all_to_all | solution.py:814
  34.8 11.5 %collective-permute-start.12 = (bf16[256,768]{1,0:T(8,128)(2,1)S(1)}, bf16[256,768]{1,0:T(8,128)(2,1)S(1)}, u32[]{:S(2)}, u32[]{:S(2)}) collective-permute-start(bf16[256,768]{1,0:T(8,128)(2,1)S(1)} %get-tuple-element.62), channel_id=1, source_target_pairs={{0,2},{1,3},{2,0},{3,1},{4,6},{5,7},{6,4},{7,5},{8,10},{9,11},{10,... | collective-permute-start | bytes 1179656 | tf_op jit(solution)/shard_map/ppermute | solution.py:658
  55.2 23.2 %all-to-all-start.1 = ((bf16[8,48,896]{2,1,0:T(8,128)(2,1)}), bf16[8,48,896]{2,1,0:T(8,128)(2,1)S(1)}, u32[]{:S(2)}, u32[]{:S(2)}) async-start(bf16[8,48,896]{2,1,0:T(8,128)(2,1)} %bitcast.8), calls=%async_computation.1 | async-start | bytes 1376256 | tf_op jit(solution)/shard_map/all_to_all | solution.py:814
  62.3 25.9 %collective-permute-start.16 = (bf16[512,768]{1,0:T(8,128)(2,1)}, bf16[512,768]{1,0:T(8,128)(2,1)S(1)}, u32[]{:S(2)}, u32[]{:S(2)}) collective-permute-start(bf16[512,768]{1,0:T(8,128)(2,1)} %slice_bitcast_fusion), channel_id=1, source_target_pairs={{0,2},{1,3},{2,0},{3,1},{4,6},{5,7},{6,4},{7,5},{8,10},{9,11},{10,... | collective-permute-start | bytes 2359304 | tf_op jit(solution)/shard_map/ppermute | solution.py:658
  78.9 17.5 %collective-permute-start.17 = (bf16[384,896]{1,0:T(8,128)(2,1)S(1)}, bf16[384,896]{1,0:T(8,128)(2,1)}, u32[]{:S(2)}, u32[]{:S(2)}) collective-permute-start(bf16[384,896]{1,0:T(8,128)(2,1)S(1)} %bitcast.28), channel_id=1, source_target_pairs={{0,2},{1,3},{2,0},{3,1},{4,6},{5,7},{6,4},{7,5},{8,10},{9,11},{10,... | collective-permute-start | bytes 2064392 | tf_op jit(solution)/shard_map/ppermute | solution.py:658
  95.0 15.6 %collective-permute-start.21 = (bf16[384,768]{1,0:T(8,128)(2,1)S(1)}, bf16[384,768]{1,0:T(8,128)(2,1)S(1)}, u32[]{:S(2)}, u32[]{:S(2)}) collective-permute-start(bf16[384,768]{1,0:T(8,128)(2,1)S(1)} %bitcast.26), channel_id=1, source_target_pairs={{0,2},{1,3},{2,0},{3,1},{4,6},{5,7},{6,4},{7,5},{8,10},{9,11},{10,... | collective-permute-start | bytes 1769480 | tf_op jit(solution)/shard_map/ppermute | solution.py:658
  96.5 16.1 %collective-permute-start.20 = (bf16[384,896]{1,0:T(8,128)(2,1)}, bf16[384,896]{1,0:T(8,128)(2,1)}, u32[]{:S(2)}, u32[]{:S(2)}) collective-permute-start(bf16[384,896]{1,0:T(8,128)(2,1)} %collective-permute-done.17.refs_4_), channel_id=1, source_target_pairs={{0,1},{1,0},{2,3},{3,2},{4,5},{5,4},{6,7},{7,6},{8,9},{9,8},{10,11... | collective-permute-start | bytes 2064392 | tf_op jit(solution)/shard_map/ppermute | solution.py:658
  98.3 27.1 %all-to-all-start.2 = ((bf16[8,48,896]{2,1,0:T(8,128)(2,1)}), bf16[8,48,896]{2,1,0:T(8,128)(2,1)S(1)}, u32[]{:S(2)}, u32[]{:S(2)}) async-start(bf16[8,48,896]{2,1,0:T(8,128)(2,1)} %bitcast.11), calls=%async_computation.2 | async-start | bytes 1376256 | tf_op jit(solution)/shard_map/all_to_all | solution.py:814
  111.8 17.5 %collective-permute-start.18 = (bf16[384,768]{1,0:T(8,128)(2,1)S(1)}, bf16[384,768]{1,0:T(8,128)(2,1)}, u32[]{:S(2)}, u32[]{:S(2)}) collective-permute-start(bf16[384,768]{1,0:T(8,128)(2,1)S(1)} %copy-done.10), channel_id=1, source_target_pairs={{0,1},{1,0},{2,3},{3,2},{4,5},{5,4},{6,7},{7,6},{8,9},{9,8},{10,11... | collective-permute-start | bytes 1769480 | tf_op jit(solution)/shard_map/ppermute | solution.py:658
  131.3 48.0 %all-to-all-start.3 = ((bf16[8,48,768]{2,1,0:T(8,128)(2,1)}), bf16[8,48,768]{2,1,0:T(8,128)(2,1)S(1)}, u32[]{:S(2)}, u32[]{:S(2)}) async-start(bf16[8,48,768]{2,1,0:T(8,128)(2,1)} %bitcast.13), calls=%async_computation.3 | async-start | bytes 1179648 | tf_op jit(solution)/shard_map/all_to_all | solution.py:814
  145.4 9.9 %collective-permute-start.31 = (bf16[2,96,768]{2,1,0:T(8,128)(2,1)S(1)}, bf16[2,96,768]{2,1,0:T(8,128)(2,1)S(1)}, u32[]{:S(2)}, u32[]{:S(2)}) collective-permute-start(bf16[2,96,768]{2,1,0:T(8,128)(2,1)S(1)} %get-tuple-element.93), channel_id=1, source_target_pairs={{0,4},{4,0},{8,12},{12,8},{16,20},{20,16},{24,28},{28,24},{1,5},{5... | collective-permute-start | bytes 884744 | tf_op jit(solution)/shard_map/ppermute | solution.py:658
  147.2 19.8 %collective-permute-start.35 = (bf16[2,96,768]{2,1,0:T(8,128)(2,1)S(1)}, bf16[2,96,768]{2,1,0:T(8,128)(2,1)S(1)}, u32[]{:S(2)}, u32[]{:S(2)}) collective-permute-start(bf16[2,96,768]{2,1,0:T(8,128)(2,1)S(1)} %get-tuple-element.97), channel_id=1, source_target_pairs={{0,4},{4,0},{8,12},{12,8},{16,20},{20,16},{24,28},{28,24},{1,5},{5... | collective-permute-start | bytes 884744 | tf_op jit(solution)/shard_map/ppermute | solution.py:658
  152.8 9.8 %collective-permute-start.30 = (f32[16,768]{1,0:T(8,128)S(1)}, f32[16,768]{1,0:T(8,128)S(1)}, u32[]{:S(2)}, u32[]{:S(2)}) collective-permute-start(f32[16,768]{1,0:T(8,128)S(1)} %add_sums.4.refs_3_.refs_0_), channel_id=1, source_target_pairs={{0,4},{4,0},{8,12},{12,8},{16,20},{20,16},{24,28},{28,24},{1,5},{5... | collective-permute-start | bytes 147464 | tf_op jit(solution)/shard_map/ppermute | solution.py:658
  154.7 22.7 %collective-permute-start.28 = (bf16[128,768]{1,0:T(8,128)(2,1)S(1)}, bf16[128,768]{1,0:T(8,128)(2,1)S(1)}, u32[]{:S(2)}, u32[]{:S(2)}) collective-permute-start(bf16[128,768]{1,0:T(8,128)(2,1)S(1)} %fold_rows.3.refs_2_), channel_id=1, source_target_pairs={{0,2},{1,3},{2,0},{3,1},{4,6},{5,7},{6,4},{7,5},{8,10},{9,11},{10,... | collective-permute-start | bytes 589832 | tf_op jit(solution)/shard_map/ppermute | solution.py:658
  165.6 10.4 %collective-permute-start.33 = (f32[16,768]{1,0:T(8,128)S(1)}, f32[16,768]{1,0:T(8,128)S(1)}, u32[]{:S(2)}, u32[]{:S(2)}) collective-permute-start(f32[16,768]{1,0:T(8,128)S(1)} %add_sums.5.refs_0_.refs_2_), channel_id=1, source_target_pairs={{0,16},{4,20},{8,24},{12,28},{16,0},{20,4},{24,8},{28,12},{1,17},{... | collective-permute-start | bytes 147464 | tf_op jit(solution)/shard_map/ppermute | solution.py:658
  166.1 10.0 %collective-permute-start.34 = (f32[16,768]{1,0:T(8,128)S(1)}, f32[16,768]{1,0:T(8,128)S(1)}, u32[]{:S(2)}, u32[]{:S(2)}) collective-permute-start(f32[16,768]{1,0:T(8,128)S(1)} %add_sums.5.refs_0_.refs_2_), channel_id=1, source_target_pairs={{0,8},{4,12},{8,0},{12,4},{16,24},{20,28},{24,16},{28,20},{1,9},{5... | collective-permute-start | bytes 147464 | tf_op jit(solution)/shard_map/ppermute | solution.py:658
  167.0 14.5 %collective-permute-start.36 = (bf16[96,768]{1,0:T(8,128)(2,1)S(1)}, bf16[96,768]{1,0:T(8,128)(2,1)S(1)}, u32[]{:S(2)}, u32[]{:S(2)}) collective-permute-start(bf16[96,768]{1,0:T(8,128)(2,1)S(1)} %get-tuple-element.94.refs_2_), channel_id=1, source_target_pairs={{0,24},{4,28},{8,16},{12,20},{16,8},{20,12},{24,0},{28,4},{1,25},{... | collective-permute-start | bytes 442376 | tf_op jit(solution)/shard_map/ppermute | solution.py:658
  170.1 13.4 %collective-permute-start.37 = (bf16[96,768]{1,0:T(8,128)(2,1)S(1)}, bf16[96,768]{1,0:T(8,128)(2,1)S(1)}, u32[]{:S(2)}, u32[]{:S(2)}) collective-permute-start(bf16[96,768]{1,0:T(8,128)(2,1)S(1)} %get-tuple-element.98), channel_id=1, source_target_pairs={{0,16},{4,20},{8,24},{12,28},{16,0},{20,4},{24,8},{28,12},{1,17},{... | collective-permute-start | bytes 442376 | tf_op jit(solution)/shard_map/ppermute | solution.py:658
  (52 other events, 298.6 us)

commit v4 on v3

--- a/solution.py
+++ b/solution.py
@@ -389,60 +389,65 @@
     send_ref[:, width:] = three_lanes(gate_sum[rows:])
 
 
-def weight_grad_kernel(
+def turn_slots(sources, pulls, rows_turned, pulls_all, rows_all=None):
+    rows, width = pulls[0].shape
+    for at, (source, pull) in enumerate(zip(sources, pulls)):
+        here = slice(at * rows, (at + 1) * rows)
+        rows_turned[:, here] = source[:, :width].T
+        gate = lanes_sum(source[:, width:])
+        pulls_all[here, :] = (gate * pull[...].astype(F32)).astype(BF16)
+        if rows_all is not None:
+            rows_all[here, :] = source[:, :width]
+
+
+def own_grads_kernel(
     own_ref,
     mate_ref,
     pull_own,
     pull_mate,
-    far_ref,
-    far_mate_ref,
-    far_pull_own,
-    far_pull_mate,
-    in_one,
-    out_one,
-    hidden_one,
-    pre_one,
+    hidden_ref,
+    pre_ref,
     grad_in,
     grad_out,
     token_ref,
     rows_turned,
     pulls_all,
-    hidden_far,
-    pre_far,
 ):
-    rows = own_ref.shape[0]
-    width, hidden_units = in_one.shape
+    token_ref[...] = jnp.zeros_like(token_ref)
+    turn_slots((own_ref, mate_ref), (pull_own, pull_mate), rows_turned, pulls_all)
     tile = 256
+    for unit in range(0, hidden_ref.shape[1], tile):
+        there = slice(unit, unit + tile)
+        grad_in[:, there] = dot(rows_turned[...], pre_ref[:, there])
+        grad_out[there, :] = dot(hidden_ref[:, there], pulls_all[...], TN)
+
+
+def far_grads_kernel(
+    own_ref,
+    mate_ref,
+    pull_own,
+    pull_mate,
+    in_ref,
+    out_ref,
+    own_in,
+    own_out,
+    grad_in,
+    grad_out,
+    token_ref,
+    rows_turned,
+    pulls_all,
+    rows_all,
+):
     token_ref[...] = jnp.zeros_like(token_ref)
-    for at, (source, pull) in enumerate(
-        (
-            (own_ref, pull_own),
-            (mate_ref, pull_mate),
-            (far_ref, far_pull_own),
-            (far_mate_ref, far_pull_mate),
-        )
-    ):
-        here = slice(at * rows, (at + 1) * rows)
-        slot_rows = source[:, :width]
-        rows_turned[:, here] = slot_rows.T
-        gate = lanes_sum(source[:, width:])
-        pulls_all[here, :] = (gate * pull[...].astype(F32)).astype(BF16)
-        if at >= 2:
-            back = slice((at - 2) * rows, (at - 1) * rows)
-            for unit in range(0, hidden_units, tile):
-                there = slice(unit, unit + tile)
-                hidden, slope = gelu_and_slope(dot(slot_rows, in_one[:, there]))
-                pulled = dot(pulls_all[here, :], out_one[there, :], NT)
-                hidden_far[back, there] = hidden.astype(BF16)
-                pre_far[back, there] = (pulled * slope).astype(BF16)
-    for unit in range(0, hidden_units, tile):
+    turn_slots((own_ref, mate_ref), (pull_own, pull_mate), rows_turned, pulls_all, rows_all)
+    tile = 256
+    for unit in range(0, in_ref.shape[1], tile):
         there = slice(unit, unit + tile)
-        grad_in[:, there] = dot(rows_turned[:, : 2 * rows], pre_one[:, there]) + dot(
-            rows_turned[:, 2 * rows :], pre_far[:, there]
-        )
-        grad_out[there, :] = dot(hidden_one[:, there], pulls_all[: 2 * rows, :], TN) + dot(
-            hidden_far[:, there], pulls_all[2 * rows :, :], TN
-        )
+        hidden, slope = gelu_and_slope(dot(rows_all[...], in_ref[:, there]))
+        pulled = dot(pulls_all[...], out_ref[there, :], NT)
+        pre_grad = (pulled * slope).astype(BF16)
+        grad_in[:, there] = own_in[:, there] + dot(rows_turned[...], pre_grad)
+        grad_out[there, :] = own_out[there, :] + dot(hidden.astype(BF16), pulls_all[...], TN)
 
 
 def expert_out_kernel(hidden_one, hidden_two, out_one, out_two, keep_ref, send_ref):
@@ -624,8 +629,7 @@
             if at % 2 == 0:
                 grad_outs[at // 2][...] = piece_rows
             else:
-                at_send = parts // 2 + (0 if at > 4 else 1)
-                grad_outs[at_send][0 if at % 4 == 3 else 1] = piece_rows.astype(BF16)
+                grad_outs[parts // 2 + (at == 1)][max(at // 2 - 1, 0)] = piece_rows.astype(BF16)
     else:
         grad_outs[0][:, : 3 * cols] = grad_first
         grad_outs[0][:, 3 * cols :] = grad_last
@@ -640,14 +644,40 @@
         if at % 2 == 0:
             keep_out[at // 2][...] = mine
         else:
-            send_out[at // 2] = mine.astype(BF16)
+            send_out[at // 2 * ROWS : (at // 2 + 1) * ROWS, :] = mine.astype(BF16)
+    put_sums(send_out, pieces // 2 * ROWS, sums_out[...])
+
+
+def put_sums(out, start, sums):
+    count = sums.shape[0]
+    high = sums.astype(BF16)
+    out[start : start + count, :] = high
+    out[start + count : start + 2 * count, :] = (sums - high.astype(F32)).astype(BF16)
+
+
+def get_sums(rows, start, count):
+    return rows[start : start + count, :].astype(F32) + rows[
+        start + count : start + 2 * count, :
+    ].astype(F32)
+
+
+def fold_back_kernel(keep_ref, near_ref, sums_ref, out_ref, sums_out):
+    count = sums_ref.shape[0]
+    out_ref[:ROWS, :] = (keep_ref[...] + near_ref[ROWS : 2 * ROWS, :].astype(F32)).astype(BF16)
+    sums = sums_ref[...] + get_sums(near_ref, 2 * ROWS, count)
+    sums_out[...] = sums
+    put_sums(out_ref, ROWS, sums)
+
+
+def join_kernel(sums_ref, far_ref, out_ref):
+    out_ref[...] = sums_ref[...] + get_sums(far_ref, ROWS, sums_ref.shape[0])
 
 
 def input_kernel(own_ref, gain_ref, mixed_grad_ref, part_ref, near_ref, far_ref, out_ref):
     x = own_ref[...].astype(F32)
     scale = lax.rsqrt(jnp.mean(x * x, axis=1, keepdims=True) + 1e-6)
     scaled = (
-        part_ref[...] + near_ref[0].astype(F32) + far_ref[...].astype(F32)
+        part_ref[...] + near_ref[:ROWS, :].astype(F32) + far_ref[:ROWS, :].astype(F32)
     ) * gain_ref[...]
     cubed = scale * scale * scale
     own = scale * scaled - x * cubed * jnp.mean(scaled * x, axis=1, keepdims=True)
@@ -687,13 +717,13 @@
     last_ref[...] = total[:, 3 * cols :]
 
 
-def fold_two_kernel(one_ref, two_ref, near_ref, one_out, two_out):
-    one_out[...] = (one_ref[...] + near_ref[0].astype(F32)).astype(BF16)
-    two_out[...] = (two_ref[...] + near_ref[1].astype(F32)).astype(BF16)
+def fold_three_kernel(one_ref, two_ref, three_ref, near_ref, *outs):
+    for at, (keep, out) in enumerate(zip((one_ref, two_ref, three_ref), outs)):
+        out[...] = (keep[...] + near_ref[at].astype(F32)).astype(BF16)
 
 
 def finish_kernel(cols, keep_ref, near_ref, one_ref, two_ref, three_ref, first_ref, last_ref):
-    total = keep_ref[...] + near_ref[1].astype(F32)
+    total = keep_ref[...] + near_ref[...].astype(F32)
     for part in (one_ref, two_ref, three_ref):
         total = total + part[...].astype(F32)
     for at in range(3):
@@ -701,15 +731,31 @@
     last_ref[...] = total[:, 3 * cols :]
 
 
-def add_kernel(one_ref, two_ref, out_ref):
-    out_ref[...] = one_ref[...] + two_ref[...]
+def fold_two_kernel(one_ref, two_ref, near_ref, one_out, two_out):
+    one_out[...] = (one_ref[...] + near_ref[0].astype(F32)).astype(BF16)
+    two_out[...] = (two_ref[...] + near_ref[1].astype(F32)).astype(BF16)
+
+
+def finish_kernel(cols, keep_ref, near_ref, one_ref, two_ref, three_ref, first_ref, last_ref):
+    total = keep_ref[...] + near_ref[0].astype(F32)
+    for part in (one_ref, two_ref, three_ref):
+        total = total + part[...].astype(F32)
+    for at in range(3):
+        first_ref[at] = total[:, at * cols : (at + 1) * cols]
+    last_ref[...] = total[:, 3 * cols :]
+
+
+def add_kernel(one_ref, two_ref, out_ref, low_ref):
+    total = one_ref[...] + two_ref[...]
+    out_ref[...] = total
+    low_ref[...] = total.astype(BF16)
 
 
 def sums_kernel(experts, *refs):
     *parts, gains_ref, bias_ref, router_ref = refs
     total = parts[0][...]
     for part in parts[1:]:
-        total = total + part[...]
+        total = total + part[...].astype(F32)
     router_ref[...] = total[:experts]
     gains_ref[0:2, :] = total[experts : experts + 2]
     for head in range(HEADS):
@@ -720,60 +766,60 @@
 
 def add(one, two, after):
     return call(
-        add_kernel, [struct(one.shape, F32)], [], [one, two], name="add_sums", prompt=True, after=after
-    )[0]
+        add_kernel,
+        [struct(one.shape, F32), struct(one.shape, BF16)],
+        [],
+        [one, two],
+        name="add_sums",
+        prompt=True,
+        after=after,
+    )
 
 
 def last_sums(grads, keep_a, keep_b, near, sums, senders, pieces, cols, experts):
+    count, width = sums.shape
+    if senders == 8:
+        near_grads = swap(grads[4], "dp", senders, 1)
+        near_last = swap(grads[5], "dp", senders, 1)
+    other, sums = call(
+        fold_back_kernel,
+        [struct((ROWS + 2 * count, width), BF16), struct((count, width), F32)],
+        [],
+        [keep_b, near, sums],
+        name="fold_rows",
+        prompt=True,
+    )
+    far = swap(other, "tensor", pieces, 2)
+    (sums,) = call(
+        join_kernel, [struct((count, width), F32)], [], [sums, far], name="join", prompt=True
+    )
     if senders != 8:
-        part, near, far, _ = scatter_rows(keep_a, keep_b, near, pieces)
         total = lax.psum_scatter(grads[0], "dp", scatter_dimension=0, tiled=True)
         first = jnp.stack([total[:, at * cols : (at + 1) * cols] for at in range(3)])
         weight_sums = (first, total[:, 3 * cols :])
-        sums = [lax.psum(sums, ("dp", "tensor"))]
+        sums = [lax.psum(sums, "dp")]
     else:
-        near_two = swap(grads[4], "dp", senders, 1)
-        near_one = swap(grads[5], "dp", senders, 1)
-        sums = add(sums, swap(sums, "tensor", pieces, 1), [near])
-        got = swap(sums, "tensor", pieces, 2)
-        other = call(
-            lambda keep, got, out: fold_kernel(keep, got.at[1], out),
-            [struct(keep_b.shape, BF16)],
+        got = swap(sums, "dp", senders, 1)
+        folded = call(
+            fold_three_kernel,
+            [struct(grads[0].shape, BF16)] * 3,
             [],
-            [keep_b, near],
-            name="fold_rows", prompt=True,
-            after=[sums],
-        )[0]
-        part, far = keep_a, swap(other, "tensor", pieces, 2)
-        sums = add(sums, got, [other])
-        got = swap(sums, "dp", senders, 1)
-        six, four = call(
-            fold_two_kernel,
-            [struct(keep.shape, BF16) for keep in (grads[3], grads[2])],
-            [],
-            [grads[3], grads[2], near_two],
-            name="fold_weights", prompt=True,
+            [grads[1], grads[2], grads[3], near_grads],
+            name="fold_weights",
+            prompt=True,
             after=[sums],
         )
-        arrived = [swap(six, "dp", senders, 6), swap(four, "dp", senders, 4)]
-        sums = add(sums, got, [six])
-        two = call(
-            lambda keep, got, out: fold_kernel(keep, got.at[0], out),
-            [struct(grads[1].shape, BF16)],
-            [],
-            [grads[1], near_one],
-            name="fold_weights", prompt=True,
-            after=[sums],
-        )[0]
-        arrived.append(swap(two, "dp", senders, 2))
-        sums = [sums] + [swap(sums, "dp", senders, mask) for mask in (6, 4, 2)]
+        arrived = [swap(folded[at], "dp", senders, 2 * at + 2) for at in (2, 1, 0)]
+        sums, low = add(sums, got, [folded[0]])
+        sums = [sums] + [swap(low, "dp", senders, mask) for mask in (6, 4, 2)]
         depth = grads[0].shape[0]
         weight_sums = call(
             functools.partial(finish_kernel, cols),
             [struct((3, depth, cols), F32), struct((depth, cols), F32)],
             [],
-            [grads[0], near_one] + arrived,
-            name="finish", prompt=True,
+            [grads[0], near_last] + arrived,
+            name="finish",
+            prompt=True,
         )
     width = sums[0].shape[1]
     small = call(
@@ -787,7 +833,7 @@
         sums,
         name="sums", prompt=True,
     )
-    return weight_sums, (part, near, far), small
+    return weight_sums, (keep_a, near, far), small
 
 
 def scatter_rows(keep_a, keep_b, near, pieces, after=()):
@@ -975,36 +1021,30 @@
         after=[far_own],
         vmem=10,
     )
-    far_pull_own = once(far_pull_own, [out_send], "pulled")
+    turned = [pltpu.VMEM((width, 2 * slots), BF16), pltpu.VMEM((2 * slots, width), BF16)]
+    grads_both = [struct(in_one.shape, F32), struct(out_one.shape, F32), struct((8, 128), F32)]
+    own_in, own_out, own_graded = call(
+        own_grads_kernel,
+        grads_both,
+        turned,
+        [slot_own, slot_mate, pull_own, pull_mate, hidden_one, pre_one],
+        flops=8 * slots * width * units,
+        name="own_grads",
+        after=[out_send],
+        held=(0, 1, 2, 3, 4, 5),
+        vmem=24,
+    )
+    far_pull_own = once(far_pull_own, [own_graded], "pulled")
     far_pull_mate = swap(far_pull_own, "tensor", pieces, 1)
     grad_in, grad_out_sum, graded = call(
-        weight_grad_kernel,
-        [struct(in_one.shape, F32), struct(out_one.shape, F32), struct((8, 128), F32)],
-        [
-            pltpu.VMEM((width, 4 * slots), BF16),
-            pltpu.VMEM((4 * slots, width), BF16),
-            pltpu.VMEM((2 * slots, in_one.shape[1]), BF16),
-            pltpu.VMEM((2 * slots, in_one.shape[1]), BF16),
-        ],
-        [
-            slot_own,
-            slot_mate,
-            pull_own,
-            pull_mate,
-            far_own,
-            far_mate,
-            far_pull_own,
-            far_pull_mate,
-            in_one,
-            out_one,
-            hidden_one,
-            pre_one,
-        ],
-        flops=24 * slots * width * in_one.shape[1],
-        name="weight_grads",
-        held=tuple(range(12)),
-        after=[out_send],
-        vmem=26,
+        far_grads_kernel,
+        grads_both,
+        turned + [pltpu.VMEM((2 * slots, width), BF16)],
+        [far_own, far_mate, far_pull_own, far_pull_mate, in_one, out_one, own_in, own_out],
+        flops=16 * slots * width * units,
+        name="far_grads",
+        held=(4, 5),
+        vmem=30,
     )
 
     sum_rows = -(-(experts + 3) // 8) * 8
@@ -1039,7 +1079,7 @@
     if parts > 1:
         depth = width // parts
         grad_shapes = [struct((depth, 4 * cols), F32)] * (parts // 2)
-        grad_shapes += [struct((2, depth, 4 * cols), BF16)] * 2
+        grad_shapes += [struct((n, depth, 4 * cols), BF16) for n in (parts // 2 - 1, 1)]
         grad_scratch = [pltpu.VMEM((width, 4 * cols), F32)]
     else:
         grad_shapes = [struct((width, 4 * cols), F32)]
@@ -1050,7 +1090,7 @@
         + [
             struct((tok_dev, width), F32),
             struct((tok_dev, width), F32),
-            struct((pieces // 2, tok_dev, width), BF16),
+            struct((pieces // 2 * tok_dev + 2 * sum_rows, width), BF16),
             struct((sum_rows, width), F32),
         ],
         [

time: 186 us -> 180 us (0.968)
  waiting for transfers between devices: 58.3 us -> 50.4 us
  starting transfers between devices: 55.9 us -> 59.9 us
  local copies, waits for them, and re-layouts: 9.63 us -> 6.72 us
    ppermute x39 -> x37, waiting for transfers between devices: 43.7 us -> 35.8 us  [swap(): return lax.ppermute(value, axis, [(i, i ^ mask) for i in range(size)])]
    unnamed x66 -> x58, local copies, waits for them, and re-layouts: 8.08 us -> 5.17 us
    all_to_all x4, starting transfers between devices: 18.7 us -> 20.9 us  [exchange(): lax.all_to_all(blocks.reshape(senders, capacity, width), 'dp', split_axis...]
    ppermute x39 -> x37, starting transfers between devices: 37.2 us -> 39 us  [swap(): return lax.ppermute(value, axis, [(i, i ^ mask) for i in range(size)])]
    pallas_call x25 -> x24, Pallas kernels: 60.4 us -> 61.6 us  [call(): pl.pallas_call(run, grid=(1,), out_shape=out_shape + [jax.ShapeDtypeStruc...]
  transfers between devices with their start and end apart: 43 -> 41, of which waited for: 20 -> 17; matrix products, arithmetic and copies ran while one was open for 1% -> 1% of each run, Pallas kernels for 31% -> 33%
where the time goes in v4:
time: 180 us
  Pallas kernels  61.6 us (34%)
  starting transfers between devices  59.9 us (33%)
  waiting for transfers between devices  50.4 us (28%)
  local copies, waits for them, and re-layouts  6.72 us (4%)
    pallas_call x24, Pallas kernels, call(): pl.pallas_call(run, grid=(1,), out_shape=out_shape + [jax.ShapeDtypeStruc...  61.6 us
    ppermute x37, starting transfers between devices, swap(): return lax.ppermute(value, axis, [(i, i ^ mask) for i in range(size)])  39 us
    ppermute x37, waiting for transfers between devices, swap(): return lax.ppermute(value, axis, [(i, i ^ mask) for i in range(size)])  35.8 us
    all_to_all x4, starting transfers between devices, exchange(): lax.all_to_all(blocks.reshape(senders, capacity, width), 'dp', split_axis...  20.9 us
    all_to_all x4, waiting for transfers between devices, exchange(): lax.all_to_all(blocks.reshape(senders, capacity, width), 'dp', split_axis...  14.6 us
    unnamed x58, local copies, waits for them, and re-layouts  5.17 us
  transfers between devices with their start and end apart: 41, of which 17 were waited for; matrix products, arithmetic and copies ran while one was open for 1% of the time, Pallas kernels for 33%

profile of v4, /device:TPU:0, one launch (start us, length us, event | category | flops | bytes accessed | tf_op | source)
XLA Modules:
  0.0 179.6 jit_solution(14497785767762913668)
XLA Ops:
  0.7 3.0 %collective-permute-start.11 = (bf16[768,768]{1,0:T(8,128)(2,1)}, bf16[768,768]{1,0:T(8,128)(2,1)}, u32[]{:S(2)}, u32[]{:S(2)}) collective-permute-start(bf16[768,768]{1,0:T(8,128)(2,1)} %bitcast.45), channel_id=1, source_target_pairs={{0,2},{1,3},{2,0},{3,1},{4,6},{5,7},{6,4},{7,5},{8,10},{9,11},{10,... | collective-permute-start | bytes 3538952 | tf_op jit(solution)/shard_map/ppermute | solution.py:688
  6.5 2.6 %collective-permute-start.3 = (bf16[96,768]{1,0:T(8,128)(2,1)S(1)}, bf16[96,768]{1,0:T(8,128)(2,1)S(1)}, u32[]{:S(2)}, u32[]{:S(2)}) collective-permute-start(bf16[96,768]{1,0:T(8,128)(2,1)S(1)} %get-tuple-element.66.refs_2_), channel_id=1, source_target_pairs={{0,16},{4,20},{8,24},{12,28},{16,0},{20,4},{24,8},{28,12},{1,17},{... | collective-permute-start | bytes 442376 | tf_op jit(solution)/shard_map/ppermute | solution.py:688
  13.6 6.8 %collective-permute-done.3.refs_6_ = bf16[96,768]{1,0:T(8,128)(2,1)S(1)} collective-permute-done((bf16[96,768]{1,0:T(8,128)(2,1)S(1)}, bf16[96,768]{1,0:T(8,128)(2,1)S(1)}, u32[]{:S(2)}, u32[]{:S(2)}) %collective-permute-start.3) | collective-permute-done | bytes 147488 | tf_op jit(solution)/shard_map/ppermute | solution.py:688
  23.1 2.6 %slots.1 = (s32[128,128]{1,0:T(8,128)}, bf16[384,768]{1,0:T(8,128)(2,1)}) custom-call(s32[2,128]{1,0:T(2,128)S(1)} %bitcast.39, bf16[128,768]{1,0:T(8,128)(2,1)} %refs_7_.1), custom_call_target="tpu_custom_call" | custom-call | flops 75497472 | bytes 852992 | tf_op jit(solution)/shard_map/slots/pallas_call | solution.py:111
  29.1 4.5 %all-to-all-start = ((bf16[8,48,768]{2,1,0:T(8,128)(2,1)}), bf16[8,48,768]{2,1,0:T(8,128)(2,1)S(1)}, u32[]{:S(2)}, u32[]{:S(2)}) async-start(bf16[8,48,768]{2,1,0:T(8,128)(2,1)} %bitcast.33), calls=%async_computation | async-start | bytes 1179648 | tf_op jit(solution)/shard_map/all_to_all | solution.py:860
  37.5 6.5 %attend.1 = (bf16[768,768]{1,0:T(8,128)(2,1)}, bf16[512,768]{1,0:T(8,128)(2,1)}, bf16[512,576]{1,0:T(8,128)(2,1)}, bf16[512,192]{1,0:T(8,128)(2,1)}, f32[512,128...) custom-call(s32[512]{0:T(512)S(1)} %copy-done.18, ...), custom_call_target="tpu_custom_call" | custom-call | flops 805306368 | bytes 6167040 | tf_op jit(solution)/shard_map/attend/pallas_call | solution.py:111
  44.2 2.1 %collective-permute-done.12.refs_3_.refs_4_ = bf16[256,768]{1,0:T(8,128)(2,1)S(1)} collective-permute-done((bf16[256,768]{1,0:T(8,128)(2,1)S(1)}, bf16[256,768]{1,0:T(8,128)(2,1)S(1)}, u32[]{:S(2)}, u32[]{:S(2)}) %collective-permute-start.12) | collective-permute-done | bytes 393248 | tf_op jit(solution)/shard_map/ppermute | solution.py:688
  48.8 4.8 %collective-permute-done.13.refs_3_ = bf16[128,768]{1,0:T(8,128)(2,1)S(1)} collective-permute-done((bf16[128,768]{1,0:T(8,128)(2,1)S(1)}, bf16[128,768]{1,0:T(8,128)(2,1)S(1)}, u32[]{:S(2)}, u32[]{:S(2)}) %collective-permute-start.13) | collective-permute-done | bytes 196640 | tf_op jit(solution)/shard_map/ppermute | solution.py:688
  55.2 6.2 %all-to-all-start.1 = ((bf16[8,48,896]{2,1,0:T(8,128)(2,1)}), bf16[8,48,896]{2,1,0:T(8,128)(2,1)S(1)}, u32[]{:S(2)}, u32[]{:S(2)}) async-start(bf16[8,48,896]{2,1,0:T(8,128)(2,1)} %bitcast.8), calls=%async_computation.1 | async-start | bytes 1376256 | tf_op jit(solution)/shard_map/all_to_all | solution.py:860
  63.8 14.6 %all-to-all-done.1 = bf16[8,48,896]{2,1,0:T(8,128)(2,1)S(1)} async-done(((bf16[8,48,896]{2,1,0:T(8,128)(2,1)}), bf16[8,48,896]{2,1,0:T(8,128)(2,1)S(1)}, u32[]{:S(2)}, u32[]{:S(2)}) %all-to-all-start.1) | async-done | bytes 688160 | tf_op jit(solution)/shard_map/all_to_all | solution.py:860
  81.4 6.8 %own_slice.1 = (bf16[768,768]{1,0:T(8,128)(2,1)}, bf16[768,768]{1,0:T(8,128)(2,1)}, f32[768,768]{1,0:T(8,128)S(1)}, f32[768,128]{1,0:T(8,128)S(1)}) custom-call(bf16[384,896]{1,0:T(8,128)(2,1)S(1)} %bitcast.29, bf16[384,896]{1,0:T(8,128)(2,1)S(1)} %collective-permute-done.14.refs_1_, bf16[384,768]{1,0:T(8,128)(2,1)S(1)} %bitcast.24, ...), custom_call_target="tpu_custom_call" | custom-call | flops 1 | bytes 1 | tf_op jit(solution)/shard_map/own_slice/pallas_call | solution.py:111
  89.1 5.7 %far_slice.1 = (bf16[768,768]{1,0:T(8,128)(2,1)}, f32[384,896]{1,0:T(8,128)S(1)}, bf16[384,896]{1,0:T(8,128)(2,1)S(1)}) custom-call(bf16[384,896]{1,0:T(8,128)(2,1)S(1)} %bitcast.30, bf16[384,896]{1,0:T(8,128)(2,1)S(1)} %collective-permute-done.14.refs_1_, bf16[384,768]{1,0:T(8,128)(2,1)S(1)} %bitcast.25, ...), custom_call_target="tpu_custom_call" | custom-call | flops 1 | bytes 1 | tf_op jit(solution)/shard_map/far_slice/pallas_call | solution.py:111
  98.3 4.1 %all-to-all-start.2 = ((bf16[8,48,896]{2,1,0:T(8,128)(2,1)}), bf16[8,48,896]{2,1,0:T(8,128)(2,1)S(1)}, u32[]{:S(2)}, u32[]{:S(2)}) async-start(bf16[8,48,896]{2,1,0:T(8,128)(2,1)} %bitcast.11), calls=%async_computation.2 | async-start | bytes 1376256 | tf_op jit(solution)/shard_map/all_to_all | solution.py:860
  102.4 5.2 %expert_out.1 = (f32[384,768]{1,0:T(8,128)S(1)}, bf16[384,768]{1,0:T(8,128)(2,1)}) custom-call(bf16[768,768]{1,0:T(8,128)(2,1)} %get-tuple-element.74.refs_0_.refs_4_, bf16[768,768]{1,0:T(8,128)(2,1)} %get-tuple-element.77.refs_1_, bf16[768,768]{1,0:T(8,128)(2,1)} %bitcast.47, bf16[768,768]{1,0:T(8,128)(2,1)} %collective-permute-done.11.refs_2_.refs_6_.refs_3_, ...), custom_call_target="tpu_custom_call" | custom-call | flops 1811939328 | bytes 6488064 | tf_op jit(solution)/shard_map/expert_out/pallas_call | solution.py:111
  107.6 4.6 %own_grads.1 = (f32[768,768]{1,0:T(8,128)S(1)}, f32[768,768]{1,0:T(8,128)S(1)}, f32[8,128]{1,0:T(8,128)S(1)}) custom-call(bf16[384,896]{1,0:T(8,128)(2,1)} %bitcast.31, bf16[384,896]{1,0:T(8,128)(2,1)} %copy-done.3, bf16[384,768]{1,0:T(8,128)(2,1)} %bitcast.22, bf16[384,768]{1,0:T(8,128)(2,1)} %copy-done.6, ...), custom_call_target="tpu_custom_call" | custom-call | flops 1811939328 | bytes 9637888 | tf_op jit(solution)/shard_map/own_grads/pallas_call | solution.py:111
  114.3 8.8 %far_grads.1 = (f32[768,768]{1,0:T(8,128)}, f32[768,768]{1,0:T(8,128)}, f32[8,128]{1,0:T(8,128)S(1)}) custom-call(bf16[384,896]{1,0:T(8,128)(2,1)} %collective-permute-done.17.refs_4_.refs_0_, bf16[384,896]{1,0:T(8,128)(2,1)} %collective-permute-done.20.refs_1_, bf16[384,768]{1,0:T(8,128)(2,1)S(1)} %pulled.1.refs_2_, ...), custom_call_target="tpu_custom_call" | custom-call | flops 3623878656 | bytes 14356480 | tf_op jit(solution)/shard_map/far_grads/pallas_call | solution.py:111
  123.1 2.3 %combine.1 = (f32[128,768]{1,0:T(8,128)S(1)}, bf16[128,768]{1,0:T(8,128)(2,1)S(1)}, f32[16,768]{1,0:T(8,128)S(1)}) custom-call(bf16[384,896]{1,0:T(8,128)(2,1)S(1)} %bitcast.32, s32[128,128]{1,0:T(8,128)} %get-tuple-element.71.refs_7_.refs_1_, f32[128,128]{1,0:T(8,128)} %get-tuple-element.82.refs_2_, f32[128,768]{1,0:T(8,128)} %get-tuple-element.83.refs_3_, ...), custom_call_target="tpu_custom_call" | custom-call | flops 75497472 | bytes 2260992 | tf_op jit(solution)/shard_map/combine/pallas_call | solution.py:111
  128.0 6.0 %all-to-all-start.3 = ((bf16[8,48,768]{2,1,0:T(8,128)(2,1)}), bf16[8,48,768]{2,1,0:T(8,128)(2,1)S(1)}, u32[]{:S(2)}, u32[]{:S(2)}) async-start(bf16[8,48,768]{2,1,0:T(8,128)(2,1)} %bitcast.13), calls=%async_computation.3 | async-start | bytes 1179648 | tf_op jit(solution)/shard_map/all_to_all | solution.py:860
  135.7 8.2 %attend_back.1 = (f32[96,768]{1,0:T(8,128)S(1)}, f32[96,768]{1,0:T(8,128)S(1)}, f32[96,768]{1,0:T(8,128)S(1)}, f32[96,768]{1,0:T(8,128)S(1)}, bf16[3,96,768]{2,1...) custom-call(s32[512]{0:T(512)S(1)} %copy-done.18, ...), custom_call_target="tpu_custom_call" | custom-call | flops 1 | bytes 1 | tf_op jit(solution)/shard_map/attend_back/pallas_call | solution.py:111
  146.9 7.3 %collective-permute-done.27.refs_5_.refs_1_ = bf16[160,768]{1,0:T(8,128)(2,1)S(1)} collective-permute-done((bf16[160,768]{1,0:T(8,128)(2,1)S(1)}, bf16[160,768]{1,0:T(8,128)(2,1)S(1)}, u32[]{:S(2)}, u32[]{:S(2)}) %collective-permute-start.27) | collective-permute-done | bytes 245792 | tf_op jit(solution)/shard_map/ppermute | solution.py:688
  158.4 3.6 %collective-permute-start.30 = (bf16[16,768]{1,0:T(8,128)(2,1)S(1)}, bf16[16,768]{1,0:T(8,128)(2,1)S(1)}, u32[]{:S(2)}, u32[]{:S(2)}) collective-permute-start(bf16[16,768]{1,0:T(8,128)(2,1)S(1)} %get-tuple-element.110), channel_id=1, source_target_pairs={{0,24},{4,28},{8,16},{12,20},{16,8},{20,12},{24,0},{28,4},{1,25},{... | collective-permute-start | bytes 73736 | tf_op jit(solution)/shard_map/ppermute | solution.py:688
  167.9 3.1 %collective-permute-done.31.refs_2_ = bf16[16,768]{1,0:T(8,128)(2,1)S(1)} collective-permute-done((bf16[16,768]{1,0:T(8,128)(2,1)S(1)}, bf16[16,768]{1,0:T(8,128)(2,1)S(1)}, u32[]{:S(2)}, u32[]{:S(2)}) %collective-permute-start.31) | collective-permute-done | bytes 24608 | tf_op jit(solution)/shard_map/ppermute | solution.py:688
  171.0 2.2 %result.1 = bf16[128,768]{1,0:T(8,128)(2,1)} custom-call(bf16[384,768]{1,0:T(8,128)(2,1)S(1)} %bitcast.34, s32[128,128]{1,0:T(8,128)} %get-tuple-element.71.refs_7_.refs_1_, f32[128,128]{1,0:T(8,128)} %get-tuple-element.82.refs_2_, f32[128,768]{1,0:T(8,128)} %get-tuple-element.83.refs_3_), custom_call_target="tpu_custom_call" | custom-call | flops 1 | bytes 1 | tf_op jit(solution)/shard_map/result/pallas_call | solution.py:111
  176.5 2.3 %collective-permute-done.35.refs_3_ = bf16[96,768]{1,0:T(8,128)(2,1)S(1)} collective-permute-done((bf16[96,768]{1,0:T(8,128)(2,1)S(1)}, bf16[96,768]{1,0:T(8,128)(2,1)S(1)}, u32[]{:S(2)}, u32[]{:S(2)}) %collective-permute-start.35) | collective-permute-done | bytes 147488 | tf_op jit(solution)/shard_map/ppermute | solution.py:688
  (144 shorter events, 54.7 us)
Async XLA Ops:
  0.7 45.6 %collective-permute-start.11 = (bf16[768,768]{1,0:T(8,128)(2,1)}, bf16[768,768]{1,0:T(8,128)(2,1)}, u32[]{:S(2)}, u32[]{:S(2)}) collective-permute-start(bf16[768,768]{1,0:T(8,128)(2,1)} %bitcast.45), channel_id=1, source_target_pairs={{0,2},{1,3},{2,0},{3,1},{4,6},{5,7},{6,4},{7,5},{8,10},{9,11},{10,... | collective-permute-start | bytes 3538952 | tf_op jit(solution)/shard_map/ppermute | solution.py:688
  6.5 13.9 %collective-permute-start.3 = (bf16[96,768]{1,0:T(8,128)(2,1)S(1)}, bf16[96,768]{1,0:T(8,128)(2,1)S(1)}, u32[]{:S(2)}, u32[]{:S(2)}) collective-permute-start(bf16[96,768]{1,0:T(8,128)(2,1)S(1)} %get-tuple-element.66.refs_2_), channel_id=1, source_target_pairs={{0,16},{4,20},{8,24},{12,28},{16,0},{20,4},{24,8},{28,12},{1,17},{... | collective-permute-start | bytes 442376 | tf_op jit(solution)/shard_map/ppermute | solution.py:688
  9.1 12.8 %collective-permute-start.5 = (bf16[96,768]{1,0:T(8,128)(2,1)S(1)}, bf16[96,768]{1,0:T(8,128)(2,1)S(1)}, u32[]{:S(2)}, u32[]{:S(2)}) collective-permute-start(bf16[96,768]{1,0:T(8,128)(2,1)S(1)} %get-tuple-element.66.refs_2_), channel_id=1, source_target_pairs={{0,24},{4,28},{8,16},{12,20},{16,8},{20,12},{24,0},{28,4},{1,25},{... | collective-permute-start | bytes 442376 | tf_op jit(solution)/shard_map/ppermute | solution.py:688
  9.4 13.1 %collective-permute-start = (bf16[96,768]{1,0:T(8,128)(2,1)S(1)}, bf16[96,768]{1,0:T(8,128)(2,1)S(1)}, u32[]{:S(2)}, u32[]{:S(2)}) collective-permute-start(bf16[96,768]{1,0:T(8,128)(2,1)S(1)} %get-tuple-element.66.refs_2_), channel_id=1, source_target_pairs={{0,4},{4,0},{8,12},{12,8},{16,20},{20,16},{24,28},{28,24},{1,5},{5... | collective-permute-start | bytes 442376 | tf_op jit(solution)/shard_map/ppermute | solution.py:688
  12.1 13.6 %collective-permute-start.2 = (bf16[96,768]{1,0:T(8,128)(2,1)S(1)}, bf16[96,768]{1,0:T(8,128)(2,1)S(1)}, u32[]{:S(2)}, u32[]{:S(2)}) collective-permute-start(bf16[96,768]{1,0:T(8,128)(2,1)S(1)} %collective-permute-done.1.refs_4_), channel_id=1, source_target_pairs={{0,4},{4,0},{8,12},{12,8},{16,20},{20,16},{24,28},{28,24},{1,5},{5... | collective-permute-start | bytes 442376 | tf_op jit(solution)/shard_map/ppermute | solution.py:688
  22.5 11.6 %collective-permute-start.8 = (bf16[128,768]{1,0:T(8,128)(2,1)S(1)}, bf16[128,768]{1,0:T(8,128)(2,1)S(1)}, u32[]{:S(2)}, u32[]{:S(2)}) collective-permute-start(bf16[128,768]{1,0:T(8,128)(2,1)S(1)} %copy-done.8), channel_id=1, source_target_pairs={{0,2},{1,3},{2,0},{3,1},{4,6},{5,7},{6,4},{7,5},{8,10},{9,11},{10,... | collective-permute-start | bytes 589832 | tf_op jit(solution)/shard_map/ppermute | solution.py:688
  29.1 19.7 %all-to-all-start = ((bf16[8,48,768]{2,1,0:T(8,128)(2,1)}), bf16[8,48,768]{2,1,0:T(8,128)(2,1)S(1)}, u32[]{:S(2)}, u32[]{:S(2)}) async-start(bf16[8,48,768]{2,1,0:T(8,128)(2,1)} %bitcast.33), calls=%async_computation | async-start | bytes 1179648 | tf_op jit(solution)/shard_map/all_to_all | solution.py:860
  34.8 11.5 %collective-permute-start.12 = (bf16[256,768]{1,0:T(8,128)(2,1)S(1)}, bf16[256,768]{1,0:T(8,128)(2,1)S(1)}, u32[]{:S(2)}, u32[]{:S(2)}) collective-permute-start(bf16[256,768]{1,0:T(8,128)(2,1)S(1)} %get-tuple-element.70), channel_id=1, source_target_pairs={{0,2},{1,3},{2,0},{3,1},{4,6},{5,7},{6,4},{7,5},{8,10},{9,11},{10,... | collective-permute-start | bytes 1179656 | tf_op jit(solution)/shard_map/ppermute | solution.py:688
  55.2 23.2 %all-to-all-start.1 = ((bf16[8,48,896]{2,1,0:T(8,128)(2,1)}), bf16[8,48,896]{2,1,0:T(8,128)(2,1)S(1)}, u32[]{:S(2)}, u32[]{:S(2)}) async-start(bf16[8,48,896]{2,1,0:T(8,128)(2,1)} %bitcast.8), calls=%async_computation.1 | async-start | bytes 1376256 | tf_op jit(solution)/shard_map/all_to_all | solution.py:860
  62.3 25.9 %collective-permute-start.16 = (bf16[512,768]{1,0:T(8,128)(2,1)}, bf16[512,768]{1,0:T(8,128)(2,1)S(1)}, u32[]{:S(2)}, u32[]{:S(2)}) collective-permute-start(bf16[512,768]{1,0:T(8,128)(2,1)} %slice_bitcast_fusion), channel_id=1, source_target_pairs={{0,2},{1,3},{2,0},{3,1},{4,6},{5,7},{6,4},{7,5},{8,10},{9,11},{10,... | collective-permute-start | bytes 2359304 | tf_op jit(solution)/shard_map/ppermute | solution.py:688
  79.0 17.5 %collective-permute-start.17 = (bf16[384,896]{1,0:T(8,128)(2,1)S(1)}, bf16[384,896]{1,0:T(8,128)(2,1)}, u32[]{:S(2)}, u32[]{:S(2)}) collective-permute-start(bf16[384,896]{1,0:T(8,128)(2,1)S(1)} %bitcast.28), channel_id=1, source_target_pairs={{0,2},{1,3},{2,0},{3,1},{4,6},{5,7},{6,4},{7,5},{8,10},{9,11},{10,... | collective-permute-start | bytes 2064392 | tf_op jit(solution)/shard_map/ppermute | solution.py:688
  95.0 17.2 %collective-permute-start.21 = (bf16[384,768]{1,0:T(8,128)(2,1)S(1)}, bf16[384,768]{1,0:T(8,128)(2,1)S(1)}, u32[]{:S(2)}, u32[]{:S(2)}) collective-permute-start(bf16[384,768]{1,0:T(8,128)(2,1)S(1)} %bitcast.26), channel_id=1, source_target_pairs={{0,2},{1,3},{2,0},{3,1},{4,6},{5,7},{6,4},{7,5},{8,10},{9,11},{10,... | collective-permute-start | bytes 1769480 | tf_op jit(solution)/shard_map/ppermute | solution.py:688
  96.5 17.8 %collective-permute-start.20 = (bf16[384,896]{1,0:T(8,128)(2,1)}, bf16[384,896]{1,0:T(8,128)(2,1)}, u32[]{:S(2)}, u32[]{:S(2)}) collective-permute-start(bf16[384,896]{1,0:T(8,128)(2,1)} %collective-permute-done.17.refs_4_.refs_0_), channel_id=1, source_target_pairs={{0,1},{1,0},{2,3},{3,2},{4,5},{5,4},{6,7},{7,6},{8,9},{9,8},{10,11... | collective-permute-start | bytes 2064392 | tf_op jit(solution)/shard_map/ppermute | solution.py:688
  98.3 24.8 %all-to-all-start.2 = ((bf16[8,48,896]{2,1,0:T(8,128)(2,1)}), bf16[8,48,896]{2,1,0:T(8,128)(2,1)S(1)}, u32[]{:S(2)}, u32[]{:S(2)}) async-start(bf16[8,48,896]{2,1,0:T(8,128)(2,1)} %bitcast.11), calls=%async_computation.2 | async-start | bytes 1376256 | tf_op jit(solution)/shard_map/all_to_all | solution.py:860
  112.5 14.5 %collective-permute-start.18 = (bf16[384,768]{1,0:T(8,128)(2,1)}, bf16[384,768]{1,0:T(8,128)(2,1)S(1)}, u32[]{:S(2)}, u32[]{:S(2)}) collective-permute-start(bf16[384,768]{1,0:T(8,128)(2,1)} %get-tuple-element.79.refs_6_), channel_id=1, source_target_pairs={{0,1},{1,0},{2,3},{3,2},{4,5},{5,4},{6,7},{7,6},{8,9},{9,8},{10,11... | collective-permute-start | bytes 1769480 | tf_op jit(solution)/shard_map/ppermute | solution.py:688
  125.5 8.6 %collective-permute-start.24 = (bf16[128,768]{1,0:T(8,128)(2,1)S(1)}, bf16[128,768]{1,0:T(8,128)(2,1)S(1)}, u32[]{:S(2)}, u32[]{:S(2)}) collective-permute-start(bf16[128,768]{1,0:T(8,128)(2,1)S(1)} %get-tuple-element.90.refs_2_), channel_id=1, source_target_pairs={{0,2},{1,3},{2,0},{3,1},{4,6},{5,7},{6,4},{7,5},{8,10},{9,11},{10,... | collective-permute-start | bytes 589832 | tf_op jit(solution)/shard_map/ppermute | solution.py:688
  128.0 43.1 %all-to-all-start.3 = ((bf16[8,48,768]{2,1,0:T(8,128)(2,1)}), bf16[8,48,768]{2,1,0:T(8,128)(2,1)S(1)}, u32[]{:S(2)}, u32[]{:S(2)}) async-start(bf16[8,48,768]{2,1,0:T(8,128)(2,1)} %bitcast.13), calls=%async_computation.3 | async-start | bytes 1179648 | tf_op jit(solution)/shard_map/all_to_all | solution.py:860
  144.2 13.2 %collective-permute-start.29 = (bf16[3,96,768]{2,1,0:T(8,128)(2,1)S(1)}, bf16[3,96,768]{2,1,0:T(8,128)(2,1)S(1)}, u32[]{:S(2)}, u32[]{:S(2)}) collective-permute-start(bf16[3,96,768]{2,1,0:T(8,128)(2,1)S(1)} %get-tuple-element.107), channel_id=1, source_target_pairs={{0,4},{4,0},{8,12},{12,8},{16,20},{20,16},{24,28},{28,24},{1,5},{5... | collective-permute-start | bytes 1327112 | tf_op jit(solution)/shard_map/ppermute | solution.py:688
  158.4 8.0 %collective-permute-start.30 = (bf16[16,768]{1,0:T(8,128)(2,1)S(1)}, bf16[16,768]{1,0:T(8,128)(2,1)S(1)}, u32[]{:S(2)}, u32[]{:S(2)}) collective-permute-start(bf16[16,768]{1,0:T(8,128)(2,1)S(1)} %get-tuple-element.110), channel_id=1, source_target_pairs={{0,24},{4,28},{8,16},{12,20},{16,8},{20,12},{24,0},{28,4},{1,25},{... | collective-permute-start | bytes 73736 | tf_op jit(solution)/shard_map/ppermute | solution.py:688
  162.1 9.0 %collective-permute-start.31 = (bf16[16,768]{1,0:T(8,128)(2,1)S(1)}, bf16[16,768]{1,0:T(8,128)(2,1)S(1)}, u32[]{:S(2)}, u32[]{:S(2)}) collective-permute-start(bf16[16,768]{1,0:T(8,128)(2,1)S(1)} %get-tuple-element.110), channel_id=1, source_target_pairs={{0,16},{4,20},{8,24},{12,28},{16,0},{20,4},{24,8},{28,12},{1,17},{... | collective-permute-start | bytes 73736 | tf_op jit(solution)/shard_map/ppermute | solution.py:688
  162.1 14.4 %collective-permute-start.33 = (bf16[1,96,768]{2,1,0:T(8,128)(2,1)S(1)}, bf16[1,96,768]{2,1,0:T(8,128)(2,1)S(1)}, u32[]{:S(2)}, u32[]{:S(2)}) collective-permute-start(bf16[1,96,768]{2,1,0:T(8,128)(2,1)S(1)} %get-tuple-element.113), channel_id=1, source_target_pairs={{0,4},{4,0},{8,12},{12,8},{16,20},{20,16},{24,28},{28,24},{1,5},{5... | collective-permute-start | bytes 442376 | tf_op jit(solution)/shard_map/ppermute | solution.py:688
  163.5 13.0 %collective-permute-start.34 = (bf16[96,768]{1,0:T(8,128)(2,1)S(1)}, bf16[96,768]{1,0:T(8,128)(2,1)S(1)}, u32[]{:S(2)}, u32[]{:S(2)}) collective-permute-start(bf16[96,768]{1,0:T(8,128)(2,1)S(1)} %get-tuple-element.114), channel_id=1, source_target_pairs={{0,24},{4,28},{8,16},{12,20},{16,8},{20,12},{24,0},{28,4},{1,25},{... | collective-permute-start | bytes 442376 | tf_op jit(solution)/shard_map/ppermute | solution.py:688
  165.5 13.2 %collective-permute-start.35 = (bf16[96,768]{1,0:T(8,128)(2,1)S(1)}, bf16[96,768]{1,0:T(8,128)(2,1)S(1)}, u32[]{:S(2)}, u32[]{:S(2)}) collective-permute-start(bf16[96,768]{1,0:T(8,128)(2,1)S(1)} %get-tuple-element.115), channel_id=1, source_target_pairs={{0,16},{4,20},{8,24},{12,28},{16,0},{20,4},{24,8},{28,12},{1,17},{... | collective-permute-start | bytes 442376 | tf_op jit(solution)/shard_map/ppermute | solution.py:688
  166.5 12.3 %collective-permute-start.36 = (bf16[96,768]{1,0:T(8,128)(2,1)S(1)}, bf16[96,768]{1,0:T(8,128)(2,1)S(1)}, u32[]{:S(2)}, u32[]{:S(2)}) collective-permute-start(bf16[96,768]{1,0:T(8,128)(2,1)S(1)} %get-tuple-element.108.refs_2_), channel_id=1, source_target_pairs={{0,8},{4,12},{8,0},{12,4},{16,24},{20,28},{24,16},{28,20},{1,9},{5... | collective-permute-start | bytes 442376 | tf_op jit(solution)/shard_map/ppermute | solution.py:688
  (46 other events, 281.1 us)

commit v5 on v4

--- a/solution.py
+++ b/solution.py
@@ -523,7 +523,8 @@
     )
 
 
-def result_kernel(back_ref, slot_ref, gates_ref, mixed_ref, out_ref):
+def result_kernel(back_ref, slot_ref, gates_ref, mixed_ref, out_ref, token_ref):
+    token_ref[...] = jnp.zeros_like(token_ref)
     tokens = mixed_ref.shape[0]
     slots = back_ref.shape[0]
     places = iota((tokens, slots), 1)
@@ -645,32 +646,20 @@
             keep_out[at // 2][...] = mine
         else:
             send_out[at // 2 * ROWS : (at // 2 + 1) * ROWS, :] = mine.astype(BF16)
-    put_sums(send_out, pieces // 2 * ROWS, sums_out[...])
-
-
-def put_sums(out, start, sums):
-    count = sums.shape[0]
-    high = sums.astype(BF16)
-    out[start : start + count, :] = high
-    out[start + count : start + 2 * count, :] = (sums - high.astype(F32)).astype(BF16)
-
-
-def get_sums(rows, start, count):
-    return rows[start : start + count, :].astype(F32) + rows[
-        start + count : start + 2 * count, :
-    ].astype(F32)
+    send_out[pieces // 2 * ROWS :, :] = sums_out[...].astype(BF16)
 
 
 def fold_back_kernel(keep_ref, near_ref, sums_ref, out_ref, sums_out):
-    count = sums_ref.shape[0]
     out_ref[:ROWS, :] = (keep_ref[...] + near_ref[ROWS : 2 * ROWS, :].astype(F32)).astype(BF16)
-    sums = sums_ref[...] + get_sums(near_ref, 2 * ROWS, count)
+    sums = sums_ref[...] + near_ref[2 * ROWS :, :].astype(F32)
     sums_out[...] = sums
-    put_sums(out_ref, ROWS, sums)
-
-
-def join_kernel(sums_ref, far_ref, out_ref):
-    out_ref[...] = sums_ref[...] + get_sums(far_ref, ROWS, sums_ref.shape[0])
+    out_ref[ROWS:, :] = sums.astype(BF16)
+
+
+def join_kernel(sums_ref, far_ref, out_ref, low_ref):
+    sums = sums_ref[...] + far_ref[ROWS:, :].astype(F32)
+    out_ref[...] = sums
+    low_ref[...] = sums.astype(BF16)
 
 
 def input_kernel(own_ref, gain_ref, mixed_grad_ref, part_ref, near_ref, far_ref, out_ref):
@@ -717,45 +706,17 @@
     last_ref[...] = total[:, 3 * cols :]
 
 
-def fold_three_kernel(one_ref, two_ref, three_ref, near_ref, *outs):
-    for at, (keep, out) in enumerate(zip((one_ref, two_ref, three_ref), outs)):
-        out[...] = (keep[...] + near_ref[at].astype(F32)).astype(BF16)
-
-
-def finish_kernel(cols, keep_ref, near_ref, one_ref, two_ref, three_ref, first_ref, last_ref):
-    total = keep_ref[...] + near_ref[...].astype(F32)
-    for part in (one_ref, two_ref, three_ref):
-        total = total + part[...].astype(F32)
-    for at in range(3):
-        first_ref[at] = total[:, at * cols : (at + 1) * cols]
-    last_ref[...] = total[:, 3 * cols :]
-
-
-def fold_two_kernel(one_ref, two_ref, near_ref, one_out, two_out):
-    one_out[...] = (one_ref[...] + near_ref[0].astype(F32)).astype(BF16)
-    two_out[...] = (two_ref[...] + near_ref[1].astype(F32)).astype(BF16)
-
-
-def finish_kernel(cols, keep_ref, near_ref, one_ref, two_ref, three_ref, first_ref, last_ref):
-    total = keep_ref[...] + near_ref[0].astype(F32)
-    for part in (one_ref, two_ref, three_ref):
-        total = total + part[...].astype(F32)
-    for at in range(3):
-        first_ref[at] = total[:, at * cols : (at + 1) * cols]
-    last_ref[...] = total[:, 3 * cols :]
-
-
-def add_kernel(one_ref, two_ref, out_ref, low_ref):
-    total = one_ref[...] + two_ref[...]
-    out_ref[...] = total
-    low_ref[...] = total.astype(BF16)
-
-
-def sums_kernel(experts, *refs):
-    *parts, gains_ref, bias_ref, router_ref = refs
-    total = parts[0][...]
-    for part in parts[1:]:
-        total = total + part[...].astype(F32)
+def fold_three_kernel(one_ref, two_ref, three_ref, near_ref, sums_ref, got_ref, *outs):
+    *chunks, sums_out = outs
+    sums = sums_ref[...] + got_ref[...].astype(F32)
+    sums_out[...] = sums
+    for at, (keep, out) in enumerate(zip((one_ref, two_ref, three_ref), chunks)):
+        depth = keep.shape[0]
+        out[:depth, :] = (keep[...] + near_ref[at].astype(F32)).astype(BF16)
+        out[depth:, :] = sums.astype(BF16)
+
+
+def put_small(total, experts, gains_ref, bias_ref, router_ref):
     router_ref[...] = total[:experts]
     gains_ref[0:2, :] = total[experts : experts + 2]
     for head in range(HEADS):
@@ -764,75 +725,80 @@
         ]
 
 
-def add(one, two, after):
-    return call(
-        add_kernel,
-        [struct(one.shape, F32), struct(one.shape, BF16)],
-        [],
-        [one, two],
-        name="add_sums",
-        prompt=True,
-        after=after,
-    )
-
-
-def last_sums(grads, keep_a, keep_b, near, sums, senders, pieces, cols, experts):
+def finish_kernel(cols, experts, keep_ref, near_ref, sums_ref, *refs):
+    *parts, first_ref, last_ref, gains_ref, bias_ref, router_ref = refs
+    depth = keep_ref.shape[0]
+    total = keep_ref[...] + near_ref[0].astype(F32)
+    small = sums_ref[...]
+    for part in parts:
+        total = total + part[:depth, :].astype(F32)
+        small = small + part[depth:, :].astype(F32)
+    for at in range(3):
+        first_ref[at] = total[:, at * cols : (at + 1) * cols]
+    last_ref[...] = total[:, 3 * cols :]
+    put_small(small, experts, gains_ref, bias_ref, router_ref)
+
+
+def sums_kernel(experts, sums_ref, gains_ref, bias_ref, router_ref):
+    put_small(sums_ref[...], experts, gains_ref, bias_ref, router_ref)
+
+
+def last_sums(grads, keep_a, keep_b, near, sums, senders, pieces, cols, experts, before):
     count, width = sums.shape
     if senders == 8:
         near_grads = swap(grads[4], "dp", senders, 1)
         near_last = swap(grads[5], "dp", senders, 1)
     other, sums = call(
         fold_back_kernel,
-        [struct((ROWS + 2 * count, width), BF16), struct((count, width), F32)],
+        [struct((ROWS + count, width), BF16), struct((count, width), F32)],
         [],
         [keep_b, near, sums],
         name="fold_rows",
         prompt=True,
     )
     far = swap(other, "tensor", pieces, 2)
-    (sums,) = call(
-        join_kernel, [struct((count, width), F32)], [], [sums, far], name="join", prompt=True
-    )
+    sums, low = call(
+        join_kernel,
+        [struct((count, width), F32), struct((count, width), BF16)],
+        [],
+        [sums, far],
+        name="join",
+        prompt=True,
+    )
+    small = [
+        struct((8, width), F32),
+        struct((HEADS, BUCKETS), F32),
+        struct((experts, width), F32),
+    ]
     if senders != 8:
         total = lax.psum_scatter(grads[0], "dp", scatter_dimension=0, tiled=True)
         first = jnp.stack([total[:, at * cols : (at + 1) * cols] for at in range(3)])
         weight_sums = (first, total[:, 3 * cols :])
-        sums = [lax.psum(sums, "dp")]
+        small = call(
+            functools.partial(sums_kernel, experts), small, [], [lax.psum(sums, "dp")], name="sums"
+        )
     else:
-        got = swap(sums, "dp", senders, 1)
-        folded = call(
+        depth = grads[0].shape[0]
+        got = swap(low, "dp", senders, 1)
+        *folded, sums = call(
             fold_three_kernel,
-            [struct(grads[0].shape, BF16)] * 3,
+            [struct((depth + count, width), BF16)] * 3 + [struct((count, width), F32)],
             [],
-            [grads[1], grads[2], grads[3], near_grads],
+            [grads[1], grads[2], grads[3], near_grads, sums, got],
             name="fold_weights",
             prompt=True,
-            after=[sums],
+            after=before,
         )
         arrived = [swap(folded[at], "dp", senders, 2 * at + 2) for at in (2, 1, 0)]
-        sums, low = add(sums, got, [folded[0]])
-        sums = [sums] + [swap(low, "dp", senders, mask) for mask in (6, 4, 2)]
-        depth = grads[0].shape[0]
-        weight_sums = call(
-            functools.partial(finish_kernel, cols),
-            [struct((3, depth, cols), F32), struct((depth, cols), F32)],
+        first, last, *small = call(
+            functools.partial(finish_kernel, cols, experts),
+            [struct((3, depth, cols), F32), struct((depth, cols), F32)] + small,
             [],
-            [grads[0], near_last] + arrived,
+            [grads[0], near_last, sums] + arrived,
             name="finish",
             prompt=True,
         )
-    width = sums[0].shape[1]
-    small = call(
-        functools.partial(sums_kernel, experts),
-        [
-            struct((8, width), F32),
-            struct((HEADS, BUCKETS), F32),
-            struct((experts, width), F32),
-        ],
-        [],
-        sums,
-        name="sums", prompt=True,
-    )
+        weight_sums = (first, last)
     return weight_sums, (keep_a, near, far), small
 
 
@@ -1064,9 +1030,9 @@
     )
     expert_out = fold(out_keep, swap(out_send, "tensor", pieces, 1), "fold_out", [mixed_low])
     returned = exchange(expert_out, senders, capacity)
-    (result,) = call(
+    result, given = call(
         result_kernel,
-        [struct((tok_dev, width), BF16)],
+        [struct((tok_dev, width), BF16), struct((8, 128), F32)],
         [],
         [returned, slot, gates, mixed],
         flops=4 * slots * tok_dev * width,
@@ -1090,7 +1056,7 @@
         + [
             struct((tok_dev, width), F32),
             struct((tok_dev, width), F32),
-            struct((pieces // 2 * tok_dev + 2 * sum_rows, width), BF16),
+            struct((pieces // 2 * tok_dev + sum_rows, width), BF16),
             struct((sum_rows, width), F32),
         ],
         [
@@ -1110,7 +1076,7 @@
     )
     near = swap(send, "tensor", pieces, 1)
     (first_sum, last_sum), (part, near, far), (gains, bias_grad, router_grad) = last_sums(
-        weight_grads, keep_a, keep_b, near, sums, senders, pieces, cols, experts
+        weight_grads, keep_a, keep_b, near, sums, senders, pieces, cols, experts, [given]
     )
     (input_grad,) = call(
         input_kernel,

time: 180 us -> 180 us (level)
  starting transfers between devices: 59.9 us -> 57.1 us
  waiting for transfers between devices: 50.4 us -> 52.3 us
    ppermute x37 -> x34, starting transfers between devices: 39 us -> 36.1 us  [swap(): return lax.ppermute(value, axis, [(i, i ^ mask) for i in range(size)])]
    ppermute x37 -> x34, waiting for transfers between devices: 35.8 us -> 37.7 us  [swap(): return lax.ppermute(value, axis, [(i, i ^ mask) for i in range(size)])]
    pallas_call x24 -> x22, Pallas kernels: 61.6 us -> 61.7 us  [call(): pl.pallas_call(run, grid=(1,), out_shape=out_shape + [jax.ShapeDtypeStruc...]
    unnamed x58 -> x66, local copies, waits for them, and re-layouts: 5.17 us -> 5.18 us
  transfers between devices with their start and end apart: 41 -> 38, of which waited for: 17 -> 15; matrix products, arithmetic and copies ran while one was open for 1% -> 1% of each run, Pallas kernels for 33% -> 33%
where the time goes in v5:
time: 180 us; the launch traced here: 179 us
  Pallas kernels  61.7 us (34%)
  starting transfers between devices  57.1 us (32%)
  waiting for transfers between devices  52.3 us (29%)
  local copies, waits for them, and re-layouts  6.73 us (4%)
    pallas_call x22, Pallas kernels, call(): pl.pallas_call(run, grid=(1,), out_shape=out_shape + [jax.ShapeDtypeStruc...  61.7 us
    ppermute x34, waiting for transfers between devices, swap(): return lax.ppermute(value, axis, [(i, i ^ mask) for i in range(size)])  37.7 us
    ppermute x34, starting transfers between devices, swap(): return lax.ppermute(value, axis, [(i, i ^ mask) for i in range(size)])  36.1 us
    all_to_all x4, starting transfers between devices, exchange(): lax.all_to_all(blocks.reshape(senders, capacity, width), 'dp', split_axis...  21.1 us
    all_to_all x4, waiting for transfers between devices, exchange(): lax.all_to_all(blocks.reshape(senders, capacity, width), 'dp', split_axis...  14.6 us
    unnamed x66, local copies, waits for them, and re-layouts  5.18 us
  transfers between devices with their start and end apart: 38, of which 15 were waited for; matrix products, arithmetic and copies ran while one was open for 1% of the time, Pallas kernels for 33%

profile of v5, /device:TPU:0, one launch (start us, length us, event | category | flops | bytes accessed | tf_op | source)
XLA Modules:
  0.0 178.8 jit_solution(2457754673399988376)
XLA Ops:
  0.7 3.0 %collective-permute-start.11 = (bf16[768,768]{1,0:T(8,128)(2,1)}, bf16[768,768]{1,0:T(8,128)(2,1)}, u32[]{:S(2)}, u32[]{:S(2)}) collective-permute-start(bf16[768,768]{1,0:T(8,128)(2,1)} %bitcast.45), channel_id=1, source_target_pairs={{0,2},{1,3},{2,0},{3,1},{4,6},{5,7},{6,4},{7,5},{8,10},{9,11},{10,... | collective-permute-start | bytes 3538952 | tf_op jit(solution)/shard_map/ppermute | solution.py:677
  6.5 2.6 %collective-permute-start.3 = (bf16[96,768]{1,0:T(8,128)(2,1)S(1)}, bf16[96,768]{1,0:T(8,128)(2,1)S(1)}, u32[]{:S(2)}, u32[]{:S(2)}) collective-permute-start(bf16[96,768]{1,0:T(8,128)(2,1)S(1)} %get-tuple-element.69.refs_2_), channel_id=1, source_target_pairs={{0,16},{4,20},{8,24},{12,28},{16,0},{20,4},{24,8},{28,12},{1,17},{... | collective-permute-start | bytes 442376 | tf_op jit(solution)/shard_map/ppermute | solution.py:677
  13.6 6.8 %collective-permute-done.3.refs_6_ = bf16[96,768]{1,0:T(8,128)(2,1)S(1)} collective-permute-done((bf16[96,768]{1,0:T(8,128)(2,1)S(1)}, bf16[96,768]{1,0:T(8,128)(2,1)S(1)}, u32[]{:S(2)}, u32[]{:S(2)}) %collective-permute-start.3) | collective-permute-done | bytes 147488 | tf_op jit(solution)/shard_map/ppermute | solution.py:677
  23.1 2.6 %slots.1 = (s32[128,128]{1,0:T(8,128)}, bf16[384,768]{1,0:T(8,128)(2,1)}) custom-call(s32[2,128]{1,0:T(2,128)S(1)} %bitcast.39, bf16[128,768]{1,0:T(8,128)(2,1)} %refs_7_.1), custom_call_target="tpu_custom_call" | custom-call | flops 75497472 | bytes 852992 | tf_op jit(solution)/shard_map/slots/pallas_call | solution.py:111
  29.1 4.5 %all-to-all-start = ((bf16[8,48,768]{2,1,0:T(8,128)(2,1)}), bf16[8,48,768]{2,1,0:T(8,128)(2,1)S(1)}, u32[]{:S(2)}, u32[]{:S(2)}) async-start(bf16[8,48,768]{2,1,0:T(8,128)(2,1)} %bitcast.33), calls=%async_computation | async-start | bytes 1179648 | tf_op jit(solution)/shard_map/all_to_all | solution.py:826
  37.5 6.5 %attend.1 = (bf16[768,768]{1,0:T(8,128)(2,1)}, bf16[512,768]{1,0:T(8,128)(2,1)}, bf16[512,576]{1,0:T(8,128)(2,1)}, bf16[512,192]{1,0:T(8,128)(2,1)}, f32[512,128...) custom-call(s32[512]{0:T(512)S(1)} %copy-done.20, ...), custom_call_target="tpu_custom_call" | custom-call | flops 805306368 | bytes 6167040 | tf_op jit(solution)/shard_map/attend/pallas_call | solution.py:111
  44.2 2.1 %collective-permute-done.12.refs_3_.refs_4_ = bf16[256,768]{1,0:T(8,128)(2,1)S(1)} collective-permute-done((bf16[256,768]{1,0:T(8,128)(2,1)S(1)}, bf16[256,768]{1,0:T(8,128)(2,1)S(1)}, u32[]{:S(2)}, u32[]{:S(2)}) %collective-permute-start.12) | collective-permute-done | bytes 393248 | tf_op jit(solution)/shard_map/ppermute | solution.py:677
  48.8 4.8 %collective-permute-done.13.refs_3_ = bf16[128,768]{1,0:T(8,128)(2,1)S(1)} collective-permute-done((bf16[128,768]{1,0:T(8,128)(2,1)S(1)}, bf16[128,768]{1,0:T(8,128)(2,1)S(1)}, u32[]{:S(2)}, u32[]{:S(2)}) %collective-permute-start.13) | collective-permute-done | bytes 196640 | tf_op jit(solution)/shard_map/ppermute | solution.py:677
  55.2 6.2 %all-to-all-start.1 = ((bf16[8,48,896]{2,1,0:T(8,128)(2,1)}), bf16[8,48,896]{2,1,0:T(8,128)(2,1)S(1)}, u32[]{:S(2)}, u32[]{:S(2)}) async-start(bf16[8,48,896]{2,1,0:T(8,128)(2,1)} %bitcast.8), calls=%async_computation.1 | async-start | bytes 1376256 | tf_op jit(solution)/shard_map/all_to_all | solution.py:826
  63.8 14.6 %all-to-all-done.1 = bf16[8,48,896]{2,1,0:T(8,128)(2,1)S(1)} async-done(((bf16[8,48,896]{2,1,0:T(8,128)(2,1)}), bf16[8,48,896]{2,1,0:T(8,128)(2,1)S(1)}, u32[]{:S(2)}, u32[]{:S(2)}) %all-to-all-start.1) | async-done | bytes 688160 | tf_op jit(solution)/shard_map/all_to_all | solution.py:826
  81.4 6.8 %own_slice.1 = (bf16[768,768]{1,0:T(8,128)(2,1)}, bf16[768,768]{1,0:T(8,128)(2,1)}, f32[768,768]{1,0:T(8,128)S(1)}, f32[768,128]{1,0:T(8,128)S(1)}) custom-call(bf16[384,896]{1,0:T(8,128)(2,1)S(1)} %bitcast.29, bf16[384,896]{1,0:T(8,128)(2,1)S(1)} %collective-permute-done.14.refs_1_, bf16[384,768]{1,0:T(8,128)(2,1)S(1)} %bitcast.24, ...), custom_call_target="tpu_custom_call" | custom-call | flops 1 | bytes 1 | tf_op jit(solution)/shard_map/own_slice/pallas_call | solution.py:111
  89.1 5.7 %far_slice.1 = (bf16[768,768]{1,0:T(8,128)(2,1)}, f32[384,896]{1,0:T(8,128)S(1)}, bf16[384,896]{1,0:T(8,128)(2,1)S(1)}) custom-call(bf16[384,896]{1,0:T(8,128)(2,1)S(1)} %bitcast.30, bf16[384,896]{1,0:T(8,128)(2,1)S(1)} %collective-permute-done.14.refs_1_, bf16[384,768]{1,0:T(8,128)(2,1)S(1)} %bitcast.25, ...), custom_call_target="tpu_custom_call" | custom-call | flops 1 | bytes 1 | tf_op jit(solution)/shard_map/far_slice/pallas_call | solution.py:111
  98.3 4.1 %all-to-all-start.2 = ((bf16[8,48,896]{2,1,0:T(8,128)(2,1)}), bf16[8,48,896]{2,1,0:T(8,128)(2,1)S(1)}, u32[]{:S(2)}, u32[]{:S(2)}) async-start(bf16[8,48,896]{2,1,0:T(8,128)(2,1)} %bitcast.11), calls=%async_computation.2 | async-start | bytes 1376256 | tf_op jit(solution)/shard_map/all_to_all | solution.py:826
  102.4 5.2 %expert_out.1 = (f32[384,768]{1,0:T(8,128)S(1)}, bf16[384,768]{1,0:T(8,128)(2,1)}) custom-call(bf16[768,768]{1,0:T(8,128)(2,1)} %get-tuple-element.77.refs_0_.refs_4_, bf16[768,768]{1,0:T(8,128)(2,1)} %get-tuple-element.80.refs_1_, bf16[768,768]{1,0:T(8,128)(2,1)} %bitcast.47, bf16[768,768]{1,0:T(8,128)(2,1)} %collective-permute-done.11.refs_2_.refs_6_.refs_3_, ...), custom_call_target="tpu_custom_call" | custom-call | flops 1811939328 | bytes 6488064 | tf_op jit(solution)/shard_map/expert_out/pallas_call | solution.py:111
  107.6 4.6 %own_grads.1 = (f32[768,768]{1,0:T(8,128)S(1)}, f32[768,768]{1,0:T(8,128)S(1)}, f32[8,128]{1,0:T(8,128)S(1)}) custom-call(bf16[384,896]{1,0:T(8,128)(2,1)} %bitcast.31, bf16[384,896]{1,0:T(8,128)(2,1)} %copy-done.3, bf16[384,768]{1,0:T(8,128)(2,1)} %bitcast.22, bf16[384,768]{1,0:T(8,128)(2,1)} %copy-done.6, ...), custom_call_target="tpu_custom_call" | custom-call | flops 1811939328 | bytes 9637888 | tf_op jit(solution)/shard_map/own_grads/pallas_call | solution.py:111
  114.3 8.8 %far_grads.1 = (f32[768,768]{1,0:T(8,128)}, f32[768,768]{1,0:T(8,128)}, f32[8,128]{1,0:T(8,128)S(1)}) custom-call(bf16[384,896]{1,0:T(8,128)(2,1)} %collective-permute-done.17.refs_4_.refs_0_, bf16[384,896]{1,0:T(8,128)(2,1)} %collective-permute-done.20.refs_1_, bf16[384,768]{1,0:T(8,128)(2,1)S(1)} %pulled.1.refs_2_, ...), custom_call_target="tpu_custom_call" | custom-call | flops 3623878656 | bytes 14356480 | tf_op jit(solution)/shard_map/far_grads/pallas_call | solution.py:111
  123.1 2.3 %combine.1 = (f32[128,768]{1,0:T(8,128)S(1)}, bf16[128,768]{1,0:T(8,128)(2,1)S(1)}, f32[16,768]{1,0:T(8,128)S(1)}) custom-call(bf16[384,896]{1,0:T(8,128)(2,1)S(1)} %bitcast.32, s32[128,128]{1,0:T(8,128)} %get-tuple-element.74.refs_7_.refs_1_, f32[128,128]{1,0:T(8,128)} %get-tuple-element.85.refs_2_, f32[128,768]{1,0:T(8,128)} %get-tuple-element.86.refs_3_, ...), custom_call_target="tpu_custom_call" | custom-call | flops 75497472 | bytes 2260992 | tf_op jit(solution)/shard_map/combine/pallas_call | solution.py:111
  128.0 6.2 %all-to-all-start.3 = ((bf16[8,48,768]{2,1,0:T(8,128)(2,1)}), bf16[8,48,768]{2,1,0:T(8,128)(2,1)S(1)}, u32[]{:S(2)}, u32[]{:S(2)}) async-start(bf16[8,48,768]{2,1,0:T(8,128)(2,1)} %bitcast.13), calls=%async_computation.3 | async-start | bytes 1179648 | tf_op jit(solution)/shard_map/all_to_all | solution.py:826
  135.9 8.8 %attend_back.1 = (f32[96,768]{1,0:T(8,128)S(1)}, f32[96,768]{1,0:T(8,128)S(1)}, f32[96,768]{1,0:T(8,128)S(1)}, f32[96,768]{1,0:T(8,128)S(1)}, bf16[3,96,768]{2,1...) custom-call(s32[512]{0:T(512)S(1)} %copy-done.20, ...), custom_call_target="tpu_custom_call" | custom-call | flops 1 | bytes 1 | tf_op jit(solution)/shard_map/attend_back/pallas_call | solution.py:111
  147.6 6.8 %collective-permute-done.27.refs_5_.refs_1_ = bf16[144,768]{1,0:T(8,128)(2,1)S(1)} collective-permute-done((bf16[144,768]{1,0:T(8,128)(2,1)S(1)}, bf16[144,768]{1,0:T(8,128)(2,1)S(1)}, u32[]{:S(2)}, u32[]{:S(2)}) %collective-permute-start.27) | collective-permute-done | bytes 221216 | tf_op jit(solution)/shard_map/ppermute | solution.py:677
  156.3 2.2 %result.1 = (bf16[128,768]{1,0:T(8,128)(2,1)}, f32[8,128]{1,0:T(8,128)S(1)}) custom-call(bf16[384,768]{1,0:T(8,128)(2,1)S(1)} %bitcast.34, s32[128,128]{1,0:T(8,128)} %get-tuple-element.74.refs_7_.refs_1_, f32[128,128]{1,0:T(8,128)} %get-tuple-element.85.refs_2_, f32[128,768]{1,0:T(8,128)} %get-tuple-element.86.refs_3_), custom_call_target="tpu_custom_call" | custom-call | flops 1 | bytes 1 | tf_op jit(solution)/shard_map/result/pallas_call | solution.py:111
  158.6 3.5 %collective-permute-start.31 = (bf16[112,768]{1,0:T(8,128)(2,1)S(1)}, bf16[112,768]{1,0:T(8,128)(2,1)S(1)}, u32[]{:S(2)}, u32[]{:S(2)}) collective-permute-start(bf16[112,768]{1,0:T(8,128)(2,1)S(1)} %get-tuple-element.118), channel_id=1, source_target_pairs={{0,24},{4,28},{8,16},{12,20},{16,8},{20,12},{24,0},{28,4},{1,25},{... | collective-permute-start | bytes 516104 | tf_op jit(solution)/shard_map/ppermute | solution.py:677
  163.0 2.3 %collective-permute-start.28 = (bf16[1,96,768]{2,1,0:T(8,128)(2,1)S(1)}, bf16[1,96,768]{2,1,0:T(8,128)(2,1)S(1)}, u32[]{:S(2)}, u32[]{:S(2)}) collective-permute-start(bf16[1,96,768]{2,1,0:T(8,128)(2,1)S(1)} %copy-done.24), channel_id=1, source_target_pairs={{0,4},{4,0},{8,12},{12,8},{16,20},{20,16},{24,28},{28,24},{1,5},{5... | collective-permute-start | bytes 442376 | tf_op jit(solution)/shard_map/ppermute | solution.py:677
  168.4 8.8 %collective-permute-done.32.refs_4_ = bf16[112,768]{1,0:T(8,128)(2,1)S(1)} collective-permute-done((bf16[112,768]{1,0:T(8,128)(2,1)S(1)}, bf16[112,768]{1,0:T(8,128)(2,1)S(1)}, u32[]{:S(2)}, u32[]{:S(2)}) %collective-permute-start.32) | collective-permute-done | bytes 172064 | tf_op jit(solution)/shard_map/ppermute | solution.py:677
  (144 shorter events, 48.0 us)
Async XLA Ops:
  0.7 45.6 %collective-permute-start.11 = (bf16[768,768]{1,0:T(8,128)(2,1)}, bf16[768,768]{1,0:T(8,128)(2,1)}, u32[]{:S(2)}, u32[]{:S(2)}) collective-permute-start(bf16[768,768]{1,0:T(8,128)(2,1)} %bitcast.45), channel_id=1, source_target_pairs={{0,2},{1,3},{2,0},{3,1},{4,6},{5,7},{6,4},{7,5},{8,10},{9,11},{10,... | collective-permute-start | bytes 3538952 | tf_op jit(solution)/shard_map/ppermute | solution.py:677
  4.9 7.2 %collective-permute-start.1 = (bf16[96,768]{1,0:T(8,128)(2,1)S(1)}, bf16[96,768]{1,0:T(8,128)(2,1)S(1)}, u32[]{:S(2)}, u32[]{:S(2)}) collective-permute-start(bf16[96,768]{1,0:T(8,128)(2,1)S(1)} %get-tuple-element.69.refs_2_), channel_id=1, source_target_pairs={{0,8},{4,12},{8,0},{12,4},{16,24},{20,28},{24,16},{28,20},{1,9},{5... | collective-permute-start | bytes 442376 | tf_op jit(solution)/shard_map/ppermute | solution.py:677
  6.5 13.9 %collective-permute-start.3 = (bf16[96,768]{1,0:T(8,128)(2,1)S(1)}, bf16[96,768]{1,0:T(8,128)(2,1)S(1)}, u32[]{:S(2)}, u32[]{:S(2)}) collective-permute-start(bf16[96,768]{1,0:T(8,128)(2,1)S(1)} %get-tuple-element.69.refs_2_), channel_id=1, source_target_pairs={{0,16},{4,20},{8,24},{12,28},{16,0},{20,4},{24,8},{28,12},{1,17},{... | collective-permute-start | bytes 442376 | tf_op jit(solution)/shard_map/ppermute | solution.py:677
  9.1 12.8 %collective-permute-start.5 = (bf16[96,768]{1,0:T(8,128)(2,1)S(1)}, bf16[96,768]{1,0:T(8,128)(2,1)S(1)}, u32[]{:S(2)}, u32[]{:S(2)}) collective-permute-start(bf16[96,768]{1,0:T(8,128)(2,1)S(1)} %get-tuple-element.69.refs_2_), channel_id=1, source_target_pairs={{0,24},{4,28},{8,16},{12,20},{16,8},{20,12},{24,0},{28,4},{1,25},{... | collective-permute-start | bytes 442376 | tf_op jit(solution)/shard_map/ppermute | solution.py:677
  9.4 13.1 %collective-permute-start = (bf16[96,768]{1,0:T(8,128)(2,1)S(1)}, bf16[96,768]{1,0:T(8,128)(2,1)S(1)}, u32[]{:S(2)}, u32[]{:S(2)}) collective-permute-start(bf16[96,768]{1,0:T(8,128)(2,1)S(1)} %get-tuple-element.69.refs_2_), channel_id=1, source_target_pairs={{0,4},{4,0},{8,12},{12,8},{16,20},{20,16},{24,28},{28,24},{1,5},{5... | collective-permute-start | bytes 442376 | tf_op jit(solution)/shard_map/ppermute | solution.py:677
  12.1 13.6 %collective-permute-start.2 = (bf16[96,768]{1,0:T(8,128)(2,1)S(1)}, bf16[96,768]{1,0:T(8,128)(2,1)S(1)}, u32[]{:S(2)}, u32[]{:S(2)}) collective-permute-start(bf16[96,768]{1,0:T(8,128)(2,1)S(1)} %collective-permute-done.1.refs_4_), channel_id=1, source_target_pairs={{0,4},{4,0},{8,12},{12,8},{16,20},{20,16},{24,28},{28,24},{1,5},{5... | collective-permute-start | bytes 442376 | tf_op jit(solution)/shard_map/ppermute | solution.py:677
  22.5 11.6 %collective-permute-start.8 = (bf16[128,768]{1,0:T(8,128)(2,1)S(1)}, bf16[128,768]{1,0:T(8,128)(2,1)S(1)}, u32[]{:S(2)}, u32[]{:S(2)}) collective-permute-start(bf16[128,768]{1,0:T(8,128)(2,1)S(1)} %copy-done.8), channel_id=1, source_target_pairs={{0,2},{1,3},{2,0},{3,1},{4,6},{5,7},{6,4},{7,5},{8,10},{9,11},{10,... | collective-permute-start | bytes 589832 | tf_op jit(solution)/shard_map/ppermute | solution.py:677
  29.1 19.7 %all-to-all-start = ((bf16[8,48,768]{2,1,0:T(8,128)(2,1)}), bf16[8,48,768]{2,1,0:T(8,128)(2,1)S(1)}, u32[]{:S(2)}, u32[]{:S(2)}) async-start(bf16[8,48,768]{2,1,0:T(8,128)(2,1)} %bitcast.33), calls=%async_computation | async-start | bytes 1179648 | tf_op jit(solution)/shard_map/all_to_all | solution.py:826
  34.8 11.5 %collective-permute-start.12 = (bf16[256,768]{1,0:T(8,128)(2,1)S(1)}, bf16[256,768]{1,0:T(8,128)(2,1)S(1)}, u32[]{:S(2)}, u32[]{:S(2)}) collective-permute-start(bf16[256,768]{1,0:T(8,128)(2,1)S(1)} %get-tuple-element.73), channel_id=1, source_target_pairs={{0,2},{1,3},{2,0},{3,1},{4,6},{5,7},{6,4},{7,5},{8,10},{9,11},{10,... | collective-permute-start | bytes 1179656 | tf_op jit(solution)/shard_map/ppermute | solution.py:677
  47.1 6.5 %collective-permute-start.13 = (bf16[128,768]{1,0:T(8,128)(2,1)S(1)}, bf16[128,768]{1,0:T(8,128)(2,1)S(1)}, u32[]{:S(2)}, u32[]{:S(2)}) collective-permute-start(bf16[128,768]{1,0:T(8,128)(2,1)S(1)} %fold_rows.2), channel_id=1, source_target_pairs={{0,2},{1,3},{2,0},{3,1},{4,6},{5,7},{6,4},{7,5},{8,10},{9,11},{10,... | collective-permute-start | bytes 589832 | tf_op jit(solution)/shard_map/ppermute | solution.py:677
  55.2 23.2 %all-to-all-start.1 = ((bf16[8,48,896]{2,1,0:T(8,128)(2,1)}), bf16[8,48,896]{2,1,0:T(8,128)(2,1)S(1)}, u32[]{:S(2)}, u32[]{:S(2)}) async-start(bf16[8,48,896]{2,1,0:T(8,128)(2,1)} %bitcast.8), calls=%async_computation.1 | async-start | bytes 1376256 | tf_op jit(solution)/shard_map/all_to_all | solution.py:826
  62.3 25.9 %collective-permute-start.16 = (bf16[512,768]{1,0:T(8,128)(2,1)}, bf16[512,768]{1,0:T(8,128)(2,1)S(1)}, u32[]{:S(2)}, u32[]{:S(2)}) collective-permute-start(bf16[512,768]{1,0:T(8,128)(2,1)} %slice_bitcast_fusion), channel_id=1, source_target_pairs={{0,2},{1,3},{2,0},{3,1},{4,6},{5,7},{6,4},{7,5},{8,10},{9,11},{10,... | collective-permute-start | bytes 2359304 | tf_op jit(solution)/shard_map/ppermute | solution.py:677
  78.9 17.5 %collective-permute-start.17 = (bf16[384,896]{1,0:T(8,128)(2,1)S(1)}, bf16[384,896]{1,0:T(8,128)(2,1)}, u32[]{:S(2)}, u32[]{:S(2)}) collective-permute-start(bf16[384,896]{1,0:T(8,128)(2,1)S(1)} %bitcast.28), channel_id=1, source_target_pairs={{0,2},{1,3},{2,0},{3,1},{4,6},{5,7},{6,4},{7,5},{8,10},{9,11},{10,... | collective-permute-start | bytes 2064392 | tf_op jit(solution)/shard_map/ppermute | solution.py:677
  95.0 17.2 %collective-permute-start.21 = (bf16[384,768]{1,0:T(8,128)(2,1)S(1)}, bf16[384,768]{1,0:T(8,128)(2,1)S(1)}, u32[]{:S(2)}, u32[]{:S(2)}) collective-permute-start(bf16[384,768]{1,0:T(8,128)(2,1)S(1)} %bitcast.26), channel_id=1, source_target_pairs={{0,2},{1,3},{2,0},{3,1},{4,6},{5,7},{6,4},{7,5},{8,10},{9,11},{10,... | collective-permute-start | bytes 1769480 | tf_op jit(solution)/shard_map/ppermute | solution.py:677
  96.5 17.8 %collective-permute-start.20 = (bf16[384,896]{1,0:T(8,128)(2,1)}, bf16[384,896]{1,0:T(8,128)(2,1)}, u32[]{:S(2)}, u32[]{:S(2)}) collective-permute-start(bf16[384,896]{1,0:T(8,128)(2,1)} %collective-permute-done.17.refs_4_.refs_0_), channel_id=1, source_target_pairs={{0,1},{1,0},{2,3},{3,2},{4,5},{5,4},{6,7},{7,6},{8,9},{9,8},{10,11... | collective-permute-start | bytes 2064392 | tf_op jit(solution)/shard_map/ppermute | solution.py:677
  98.3 24.8 %all-to-all-start.2 = ((bf16[8,48,896]{2,1,0:T(8,128)(2,1)}), bf16[8,48,896]{2,1,0:T(8,128)(2,1)S(1)}, u32[]{:S(2)}, u32[]{:S(2)}) async-start(bf16[8,48,896]{2,1,0:T(8,128)(2,1)} %bitcast.11), calls=%async_computation.2 | async-start | bytes 1376256 | tf_op jit(solution)/shard_map/all_to_all | solution.py:826
  112.5 14.5 %collective-permute-start.18 = (bf16[384,768]{1,0:T(8,128)(2,1)}, bf16[384,768]{1,0:T(8,128)(2,1)S(1)}, u32[]{:S(2)}, u32[]{:S(2)}) collective-permute-start(bf16[384,768]{1,0:T(8,128)(2,1)} %get-tuple-element.82.refs_6_), channel_id=1, source_target_pairs={{0,1},{1,0},{2,3},{3,2},{4,5},{5,4},{6,7},{7,6},{8,9},{9,8},{10,11... | collective-permute-start | bytes 1769480 | tf_op jit(solution)/shard_map/ppermute | solution.py:677
  125.5 8.7 %collective-permute-start.24 = (bf16[128,768]{1,0:T(8,128)(2,1)S(1)}, bf16[128,768]{1,0:T(8,128)(2,1)S(1)}, u32[]{:S(2)}, u32[]{:S(2)}) collective-permute-start(bf16[128,768]{1,0:T(8,128)(2,1)S(1)} %get-tuple-element.93.refs_2_), channel_id=1, source_target_pairs={{0,2},{1,3},{2,0},{3,1},{4,6},{5,7},{6,4},{7,5},{8,10},{9,11},{10,... | collective-permute-start | bytes 589832 | tf_op jit(solution)/shard_map/ppermute | solution.py:677
  128.0 28.3 %all-to-all-start.3 = ((bf16[8,48,768]{2,1,0:T(8,128)(2,1)}), bf16[8,48,768]{2,1,0:T(8,128)(2,1)S(1)}, u32[]{:S(2)}, u32[]{:S(2)}) async-start(bf16[8,48,768]{2,1,0:T(8,128)(2,1)} %bitcast.13), calls=%async_computation.3 | async-start | bytes 1179648 | tf_op jit(solution)/shard_map/all_to_all | solution.py:826
  144.9 13.5 %collective-permute-start.29 = (bf16[3,96,768]{2,1,0:T(8,128)(2,1)}, bf16[3,96,768]{2,1,0:T(8,128)(2,1)S(1)}, u32[]{:S(2)}, u32[]{:S(2)}) collective-permute-start(bf16[3,96,768]{2,1,0:T(8,128)(2,1)} %get-tuple-element.112), channel_id=1, source_target_pairs={{0,4},{4,0},{8,12},{12,8},{16,20},{20,16},{24,28},{28,24},{1,5},{5... | collective-permute-start | bytes 1327112 | tf_op jit(solution)/shard_map/ppermute | solution.py:677
  147.0 7.4 %collective-permute-start.27 = (bf16[144,768]{1,0:T(8,128)(2,1)S(1)}, bf16[144,768]{1,0:T(8,128)(2,1)S(1)}, u32[]{:S(2)}, u32[]{:S(2)}) collective-permute-start(bf16[144,768]{1,0:T(8,128)(2,1)S(1)} %get-tuple-element.106), channel_id=1, source_target_pairs={{0,2},{1,3},{2,0},{3,1},{4,6},{5,7},{6,4},{7,5},{8,10},{9,11},{10,... | collective-permute-start | bytes 663560 | tf_op jit(solution)/shard_map/ppermute | solution.py:677
  158.6 9.9 %collective-permute-start.31 = (bf16[112,768]{1,0:T(8,128)(2,1)S(1)}, bf16[112,768]{1,0:T(8,128)(2,1)S(1)}, u32[]{:S(2)}, u32[]{:S(2)}) collective-permute-start(bf16[112,768]{1,0:T(8,128)(2,1)S(1)} %get-tuple-element.118), channel_id=1, source_target_pairs={{0,24},{4,28},{8,16},{12,20},{16,8},{20,12},{24,0},{28,4},{1,25},{... | collective-permute-start | bytes 516104 | tf_op jit(solution)/shard_map/ppermute | solution.py:677
  162.1 15.2 %collective-permute-start.32 = (bf16[112,768]{1,0:T(8,128)(2,1)S(1)}, bf16[112,768]{1,0:T(8,128)(2,1)S(1)}, u32[]{:S(2)}, u32[]{:S(2)}) collective-permute-start(bf16[112,768]{1,0:T(8,128)(2,1)S(1)} %get-tuple-element.119), channel_id=1, source_target_pairs={{0,16},{4,20},{8,24},{12,28},{16,0},{20,4},{24,8},{28,12},{1,17},{... | collective-permute-start | bytes 516104 | tf_op jit(solution)/shard_map/ppermute | solution.py:677
  162.2 15.1 %collective-permute-start.33 = (bf16[112,768]{1,0:T(8,128)(2,1)S(1)}, bf16[112,768]{1,0:T(8,128)(2,1)S(1)}, u32[]{:S(2)}, u32[]{:S(2)}) collective-permute-start(bf16[112,768]{1,0:T(8,128)(2,1)S(1)} %get-tuple-element.120), channel_id=1, source_target_pairs={{0,8},{4,12},{8,0},{12,4},{16,24},{20,28},{24,16},{28,20},{1,9},{5... | collective-permute-start | bytes 516104 | tf_op jit(solution)/shard_map/ppermute | solution.py:677
  (47 other events, 287.4 us)

commit v6 on v5

--- a/solution.py
+++ b/solution.py
@@ -336,53 +336,36 @@
     return jnp.sum(gate_wide, axis=1, keepdims=True)
 
 
-def own_slice_kernel(
+def expert_kernel(
     own_ref,
     mate_ref,
     pull_own,
     pull_mate,
     in_ref,
     out_ref,
+    far_in_a,
+    far_in_b,
+    far_out,
     hidden_ref,
     pre_ref,
-    total_ref,
-    sum_ref,
+    far_hidden,
+    keep_ref,
+    send_ref,
     rows_all,
     pulls_all,
+    far_in,
+    far_pre,
 ):
+    rows, width = pull_own.shape
+    split = far_in_a.shape[0]
     gate = gather_sides((own_ref, mate_ref), (pull_own, pull_mate), rows_all, pulls_all)
     gate_sum = through_slice(rows_all, pulls_all, gate, in_ref, out_ref, hidden_ref, pre_ref)
-    sum_ref[...] = jnp.broadcast_to(gate_sum, sum_ref.shape)
-    total_ref[...] = dot(pre_ref[...], in_ref[...], NT)
-
-
-def far_slice_kernel(
-    own_ref,
-    mate_ref,
-    pull_own,
-    pull_mate,
-    in_a_ref,
-    in_b_ref,
-    out_ref,
-    total_ref,
-    sum_ref,
-    hidden_ref,
-    keep_ref,
-    send_ref,
-    in_ref,
-    pre_ref,
-    rows_all,
-    pulls_all,
-):
-    rows, width = pull_own.shape
-    split = in_a_ref.shape[0]
-    in_ref[:split, :] = in_a_ref[...]
-    in_ref[split:, :] = in_b_ref[...]
-    gate = gather_sides((own_ref, mate_ref), (pull_own, pull_mate), rows_all, pulls_all)
-    gate_sum = sum_ref[:, 0:1] + through_slice(
-        rows_all, pulls_all, gate, in_ref, out_ref, hidden_ref, pre_ref
-    )
-    total = total_ref[...] + dot(pre_ref[...], in_ref[...], NT)
+    far_in[:split, :] = far_in_a[...]
+    far_in[split:, :] = far_in_b[...]
+    gate_sum = gate_sum + through_slice(
+        rows_all, pulls_all, gate, far_in, far_out, far_hidden, far_pre
+    )
+    total = dot(pre_ref[...], in_ref[...], NT) + dot(far_pre[...], far_in[...], NT)
     keep_ref[:, :width] = total[:rows, :]
     keep_ref[:, width:] = jnp.broadcast_to(gate_sum[:rows], (rows, GATE_LANES))
     send_ref[:, :width] = total[rows:, :].astype(BF16)
@@ -933,36 +916,32 @@
     slot_mate = swap(slot_own, "tensor", pieces, 1)
     payload = width + GATE_LANES
     units = in_one.shape[1]
-    expert_flops = 12 * slots * width * units
-    hidden_one, pre_one, row_total, gate_total = call(
-        own_slice_kernel,
-        [struct((2 * slots, units), BF16)] * 2
-        + [struct((2 * slots, width), F32), struct((2 * slots, GATE_LANES), F32)],
-        [pltpu.VMEM((2 * slots, width), BF16)] * 2,
-        [slot_own, slot_mate, pull_own, pull_mate, in_one, out_one],
-        flops=expert_flops,
-        name="own_slice",
+    hidden_one, pre_one, hidden_two, row_keep, row_send = call(
+        expert_kernel,
+        [struct((2 * slots, units), BF16)] * 3
+        + [struct((slots, payload), F32), struct((slots, payload), BF16)],
+        [
+            pltpu.VMEM((2 * slots, width), BF16),
+            pltpu.VMEM((2 * slots, width), BF16),
+            pltpu.VMEM((width, units), BF16),
+            pltpu.VMEM((2 * slots, units), BF16),
+        ],
+        [
+            slot_own,
+            slot_mate,
+            pull_own,
+            pull_mate,
+            in_one,
+            out_one,
+            in_two_a,
+            in_two_b,
+            out_two,
+        ],
+        name="experts",
         prompt=True,
-        held=(4, 5),
-        kept=(0, 1),
-        vmem=18,
-    )
-    hidden_two, row_keep, row_send = call(
-        far_slice_kernel,
-        [
-            struct((2 * slots, units), BF16),
-            struct((slots, payload), F32),
-            struct((slots, payload), BF16),
-        ],
-        [pltpu.VMEM((width, units), BF16), pltpu.VMEM((2 * slots, units), BF16)]
-        + [pltpu.VMEM((2 * slots, width), BF16)] * 2,
-        [slot_own, slot_mate, pull_own, pull_mate, in_two_a, in_two_b, out_two, row_total, gate_total],
-        flops=expert_flops,
-        name="far_slice",
-        prompt=True,
-        held=(4, 5, 6),
-        kept=(0,),
-        vmem=20,
+        held=(4, 5, 6, 7, 8),
+        kept=(0, 1, 2),
+        vmem=30,
     )
     row_mate = swap(row_send, "tensor", pieces, 1)
     far_own = swap(slot_own, "tensor", pieces, 2)
@@ -984,7 +963,7 @@
         flops=4 * 2 * slots * width * in_one.shape[1],
         name="expert_out",
         held=(0, 1, 2, 3),
-        after=[far_own],
+        after=[row_out],
         vmem=10,
     )
     turned = [pltpu.VMEM((width, 2 * slots), BF16), pltpu.VMEM((2 * slots, width), BF16)]
@@ -996,7 +975,7 @@
         [slot_own, slot_mate, pull_own, pull_mate, hidden_one, pre_one],
         flops=8 * slots * width * units,
         name="own_grads",
-        after=[out_send],
+        after=[out_send, far_own],
         held=(0, 1, 2, 3, 4, 5),
         vmem=24,
     )

time: 180 us -> 178 us (0.989)
  waiting for transfers between devices: 52.3 us -> 60.3 us
  starting transfers between devices: 57.1 us -> 51.7 us
  local copies, waits for them, and re-layouts: 6.73 us -> 4.31 us
  Pallas kernels: 61.7 us -> 59.9 us
    ppermute x34, waiting for transfers between devices: 37.7 us -> 44.4 us  [swap(): return lax.ppermute(value, axis, [(i, i ^ mask) for i in range(size)])]
    ppermute x34, starting transfers between devices: 36.1 us -> 31.4 us  [swap(): return lax.ppermute(value, axis, [(i, i ^ mask) for i in range(size)])]
    unnamed x66 -> x62, local copies, waits for them, and re-layouts: 5.18 us -> 2.76 us
    pallas_call x22 -> x21, Pallas kernels: 61.7 us -> 59.9 us  [call(): pl.pallas_call(run, grid=(1,), out_shape=out_shape + [jax.ShapeDtypeStruc...]
  transfers between devices with their start and end apart: 38 -> 38, of which waited for: 15 -> 19; matrix products, arithmetic and copies ran while one was open for 1% -> 1% of each run, Pallas kernels for 33% -> 32%
where the time goes in v6:
time: 178 us; the launch traced here: 177 us
  waiting for transfers between devices  60.3 us (34%)
  Pallas kernels  59.9 us (34%)
  starting transfers between devices  51.7 us (29%)
  local copies, waits for them, and re-layouts  4.31 us (2%)
    pallas_call x21, Pallas kernels, call(): pl.pallas_call(run, grid=(1,), out_shape=out_shape + [jax.ShapeDtypeStruc...  59.9 us
    ppermute x34, waiting for transfers between devices, swap(): return lax.ppermute(value, axis, [(i, i ^ mask) for i in range(size)])  44.4 us
    ppermute x34, starting transfers between devices, swap(): return lax.ppermute(value, axis, [(i, i ^ mask) for i in range(size)])  31.4 us
    all_to_all x4, starting transfers between devices, exchange(): lax.all_to_all(blocks.reshape(senders, capacity, width), 'dp', split_axis...  20.3 us
    all_to_all x4, waiting for transfers between devices, exchange(): lax.all_to_all(blocks.reshape(senders, capacity, width), 'dp', split_axis...  15.9 us
  transfers between devices with their start and end apart: 38, of which 19 were waited for; matrix products, arithmetic and copies ran while one was open for 1% of the time, Pallas kernels for 32%

profile of v6, /device:TPU:0, one launch (start us, length us, event | category | flops | bytes accessed | tf_op | source)
XLA Modules:
  0.0 177.1 jit_solution(16595689322789463716)
XLA Ops:
  0.7 3.0 %collective-permute-start.11 = (bf16[768,768]{1,0:T(8,128)(2,1)}, bf16[768,768]{1,0:T(8,128)(2,1)}, u32[]{:S(2)}, u32[]{:S(2)}) collective-permute-start(bf16[768,768]{1,0:T(8,128)(2,1)} %bitcast.43), channel_id=1, source_target_pairs={{0,2},{1,3},{2,0},{3,1},{4,6},{5,7},{6,4},{7,5},{8,10},{9,11},{10,... | collective-permute-start | bytes 3538952 | tf_op jit(solution)/shard_map/ppermute | solution.py:660
  4.9 3.7 %collective-permute-start.5 = (bf16[96,768]{1,0:T(8,128)(2,1)S(1)}, bf16[96,768]{1,0:T(8,128)(2,1)S(1)}, u32[]{:S(2)}, u32[]{:S(2)}) collective-permute-start(bf16[96,768]{1,0:T(8,128)(2,1)S(1)} %get-tuple-element.67.refs_2_), channel_id=1, source_target_pairs={{0,24},{4,28},{8,16},{12,20},{16,8},{20,12},{24,0},{28,4},{1,25},{... | collective-permute-start | bytes 442376 | tf_op jit(solution)/shard_map/ppermute | solution.py:660
  10.9 2.7 %collective-permute-done.5.refs_8_ = bf16[96,768]{1,0:T(8,128)(2,1)S(1)} collective-permute-done((bf16[96,768]{1,0:T(8,128)(2,1)S(1)}, bf16[96,768]{1,0:T(8,128)(2,1)S(1)}, u32[]{:S(2)}, u32[]{:S(2)}) %collective-permute-start.5) | collective-permute-done | bytes 147488 | tf_op jit(solution)/shard_map/ppermute | solution.py:660
  15.1 5.7 %collective-permute-done.3.refs_6_ = bf16[96,768]{1,0:T(8,128)(2,1)S(1)} collective-permute-done((bf16[96,768]{1,0:T(8,128)(2,1)S(1)}, bf16[96,768]{1,0:T(8,128)(2,1)S(1)}, u32[]{:S(2)}, u32[]{:S(2)}) %collective-permute-start.3) | collective-permute-done | bytes 147488 | tf_op jit(solution)/shard_map/ppermute | solution.py:660
  23.4 2.6 %slots.1 = (s32[128,128]{1,0:T(8,128)}, bf16[384,768]{1,0:T(8,128)(2,1)}) custom-call(s32[2,128]{1,0:T(2,128)S(1)} %bitcast.37, bf16[128,768]{1,0:T(8,128)(2,1)} %refs_7_.1), custom_call_target="tpu_custom_call" | custom-call | flops 75497472 | bytes 852992 | tf_op jit(solution)/shard_map/slots/pallas_call | solution.py:111
  30.8 4.3 %all-to-all-start = ((bf16[8,48,768]{2,1,0:T(8,128)(2,1)}), bf16[8,48,768]{2,1,0:T(8,128)(2,1)S(1)}, u32[]{:S(2)}, u32[]{:S(2)}) async-start(bf16[8,48,768]{2,1,0:T(8,128)(2,1)} %bitcast.31), calls=%async_computation | async-start | bytes 1179648 | tf_op jit(solution)/shard_map/all_to_all | solution.py:809
  36.8 6.5 %attend.1 = (bf16[768,768]{1,0:T(8,128)(2,1)}, bf16[512,768]{1,0:T(8,128)(2,1)}, bf16[512,576]{1,0:T(8,128)(2,1)}, bf16[512,192]{1,0:T(8,128)(2,1)}, f32[512,128...) custom-call(s32[512]{0:T(512)S(1)} %copy-done.20, ...), custom_call_target="tpu_custom_call" | custom-call | flops 805306368 | bytes 6167040 | tf_op jit(solution)/shard_map/attend/pallas_call | solution.py:111
  43.5 3.1 %collective-permute-done.12.refs_3_.refs_6_ = bf16[256,768]{1,0:T(8,128)(2,1)S(1)} collective-permute-done((bf16[256,768]{1,0:T(8,128)(2,1)S(1)}, bf16[256,768]{1,0:T(8,128)(2,1)S(1)}, u32[]{:S(2)}, u32[]{:S(2)}) %collective-permute-start.12) | collective-permute-done | bytes 393248 | tf_op jit(solution)/shard_map/ppermute | solution.py:660
  49.0 4.5 %collective-permute-done.13.refs_3_ = bf16[128,768]{1,0:T(8,128)(2,1)S(1)} collective-permute-done((bf16[128,768]{1,0:T(8,128)(2,1)S(1)}, bf16[128,768]{1,0:T(8,128)(2,1)S(1)}, u32[]{:S(2)}, u32[]{:S(2)}) %collective-permute-start.13) | collective-permute-done | bytes 196640 | tf_op jit(solution)/shard_map/ppermute | solution.py:660
  55.1 6.1 %all-to-all-start.1 = ((bf16[8,48,896]{2,1,0:T(8,128)(2,1)}), bf16[8,48,896]{2,1,0:T(8,128)(2,1)S(1)}, u32[]{:S(2)}, u32[]{:S(2)}) async-start(bf16[8,48,896]{2,1,0:T(8,128)(2,1)} %bitcast.8), calls=%async_computation.1 | async-start | bytes 1376256 | tf_op jit(solution)/shard_map/all_to_all | solution.py:809
  62.7 15.0 %all-to-all-done.1 = bf16[8,48,896]{2,1,0:T(8,128)(2,1)S(1)} async-done(((bf16[8,48,896]{2,1,0:T(8,128)(2,1)}), bf16[8,48,896]{2,1,0:T(8,128)(2,1)S(1)}, u32[]{:S(2)}, u32[]{:S(2)}) %all-to-all-start.1) | async-done | bytes 688160 | tf_op jit(solution)/shard_map/all_to_all | solution.py:809
  80.7 10.7 %experts.1 = (bf16[768,768]{1,0:T(8,128)(2,1)}, bf16[768,768]{1,0:T(8,128)(2,1)}, bf16[768,768]{1,0:T(8,128)(2,1)}, f32[384,896]{1,0:T(8,128)S(1)}, bf16[384,896]{1,0:T(8,128)(2,1)S(1)}) custom-call(bf16[384,896]{1,0:T(8,128)(2,1)S(1)} %bitcast.28, bf16[384,896]{1,0:T(8,128)(2,1)S(1)} %collective-permute-done.14.refs_1_, bf16[384,768]{1,0:T(8,128)(2,1)S(1)} %bitcast.24, ...), custom_call_target="tpu_custom_call" | custom-call | flops 1 | bytes 1 | tf_op jit(solution)/shard_map/experts/pallas_call | solution.py:111
  92.2 4.4 %collective-permute-done.19.refs_7_.refs_0_ = bf16[384,896]{1,0:T(8,128)(2,1)} collective-permute-done((bf16[384,896]{1,0:T(8,128)(2,1)S(1)}, bf16[384,896]{1,0:T(8,128)(2,1)}, u32[]{:S(2)}, u32[]{:S(2)}) %collective-permute-start.19) | collective-permute-done | bytes 688160 | tf_op jit(solution)/shard_map/ppermute | solution.py:660
  97.9 3.8 %all-to-all-start.2 = ((bf16[8,48,896]{2,1,0:T(8,128)(2,1)}), bf16[8,48,896]{2,1,0:T(8,128)(2,1)S(1)}, u32[]{:S(2)}, u32[]{:S(2)}) async-start(bf16[8,48,896]{2,1,0:T(8,128)(2,1)} %bitcast.11), calls=%async_computation.2 | async-start | bytes 1376256 | tf_op jit(solution)/shard_map/all_to_all | solution.py:809
  101.8 5.2 %expert_out.1 = (f32[384,768]{1,0:T(8,128)S(1)}, bf16[384,768]{1,0:T(8,128)(2,1)}) custom-call(bf16[768,768]{1,0:T(8,128)(2,1)} %get-tuple-element.75.refs_0_.refs_4_, bf16[768,768]{1,0:T(8,128)(2,1)} %get-tuple-element.76.refs_1_, bf16[768,768]{1,0:T(8,128)(2,1)} %bitcast.45, bf16[768,768]{1,0:T(8,128)(2,1)} %collective-permute-done.11.refs_2_.refs_8_.refs_3_, ...), custom_call_target="tpu_custom_call" | custom-call | flops 1811939328 | bytes 6488064 | tf_op jit(solution)/shard_map/expert_out/pallas_call | solution.py:111
  106.9 4.6 %own_grads.1 = (f32[768,768]{1,0:T(8,128)S(1)}, f32[768,768]{1,0:T(8,128)S(1)}, f32[8,128]{1,0:T(8,128)S(1)}) custom-call(bf16[384,896]{1,0:T(8,128)(2,1)} %bitcast.29, bf16[384,896]{1,0:T(8,128)(2,1)} %copy-done.7, bf16[384,768]{1,0:T(8,128)(2,1)} %bitcast.22, bf16[384,768]{1,0:T(8,128)(2,1)} %copy-done.8, ...), custom_call_target="tpu_custom_call" | custom-call | flops 1811939328 | bytes 9637888 | tf_op jit(solution)/shard_map/own_grads/pallas_call | solution.py:111
  113.7 8.8 %far_grads.1 = (f32[768,768]{1,0:T(8,128)}, f32[768,768]{1,0:T(8,128)}, f32[8,128]{1,0:T(8,128)S(1)}) custom-call(bf16[384,896]{1,0:T(8,128)(2,1)} %collective-permute-done.19.refs_7_.refs_0_, bf16[384,896]{1,0:T(8,128)(2,1)} %collective-permute-done.20.refs_1_, bf16[384,768]{1,0:T(8,128)(2,1)S(1)} %pulled.1.refs_2_, ...), custom_call_target="tpu_custom_call" | custom-call | flops 3623878656 | bytes 14356480 | tf_op jit(solution)/shard_map/far_grads/pallas_call | solution.py:111
  122.5 2.3 %combine.1 = (f32[128,768]{1,0:T(8,128)S(1)}, bf16[128,768]{1,0:T(8,128)(2,1)S(1)}, f32[16,768]{1,0:T(8,128)S(1)}) custom-call(bf16[384,896]{1,0:T(8,128)(2,1)S(1)} %bitcast.30, s32[128,128]{1,0:T(8,128)} %get-tuple-element.72.refs_7_.refs_1_, f32[128,128]{1,0:T(8,128)} %get-tuple-element.81.refs_2_, f32[128,768]{1,0:T(8,128)} %get-tuple-element.82.refs_3_, ...), custom_call_target="tpu_custom_call" | custom-call | flops 75497472 | bytes 2260992 | tf_op jit(solution)/shard_map/combine/pallas_call | solution.py:111
  126.5 6.1 %all-to-all-start.3 = ((bf16[8,48,768]{2,1,0:T(8,128)(2,1)}), bf16[8,48,768]{2,1,0:T(8,128)(2,1)S(1)}, u32[]{:S(2)}, u32[]{:S(2)}) async-start(bf16[8,48,768]{2,1,0:T(8,128)(2,1)} %bitcast.13), calls=%async_computation.3 | async-start | bytes 1179648 | tf_op jit(solution)/shard_map/all_to_all | solution.py:809
  134.3 8.8 %attend_back.1 = (f32[96,768]{1,0:T(8,128)S(1)}, f32[96,768]{1,0:T(8,128)S(1)}, f32[96,768]{1,0:T(8,128)S(1)}, f32[96,768]{1,0:T(8,128)S(1)}, bf16[3,96,768]{2,1...) custom-call(s32[512]{0:T(512)S(1)} %copy-done.20, ...), custom_call_target="tpu_custom_call" | custom-call | flops 1 | bytes 1 | tf_op jit(solution)/shard_map/attend_back/pallas_call | solution.py:111
  146.9 5.8 %collective-permute-done.27.refs_5_.refs_1_ = bf16[144,768]{1,0:T(8,128)(2,1)S(1)} collective-permute-done((bf16[144,768]{1,0:T(8,128)(2,1)S(1)}, bf16[144,768]{1,0:T(8,128)(2,1)S(1)}, u32[]{:S(2)}, u32[]{:S(2)}) %collective-permute-start.27) | collective-permute-done | bytes 221216 | tf_op jit(solution)/shard_map/ppermute | solution.py:660
  156.9 3.5 %collective-permute-start.31 = (bf16[112,768]{1,0:T(8,128)(2,1)S(1)}, bf16[112,768]{1,0:T(8,128)(2,1)S(1)}, u32[]{:S(2)}, u32[]{:S(2)}) collective-permute-start(bf16[112,768]{1,0:T(8,128)(2,1)S(1)} %get-tuple-element.114), channel_id=1, source_target_pairs={{0,24},{4,28},{8,16},{12,20},{16,8},{20,12},{24,0},{28,4},{1,25},{... | collective-permute-start | bytes 516104 | tf_op jit(solution)/shard_map/ppermute | solution.py:660
  161.4 2.3 %collective-permute-start.28 = (bf16[1,96,768]{2,1,0:T(8,128)(2,1)S(1)}, bf16[1,96,768]{2,1,0:T(8,128)(2,1)S(1)}, u32[]{:S(2)}, u32[]{:S(2)}) collective-permute-start(bf16[1,96,768]{2,1,0:T(8,128)(2,1)S(1)} %copy-done.22), channel_id=1, source_target_pairs={{0,4},{4,0},{8,12},{12,8},{16,20},{20,16},{24,28},{28,24},{1,5},{5... | collective-permute-start | bytes 442376 | tf_op jit(solution)/shard_map/ppermute | solution.py:660
  166.8 8.8 %collective-permute-done.32.refs_4_ = bf16[112,768]{1,0:T(8,128)(2,1)S(1)} collective-permute-done((bf16[112,768]{1,0:T(8,128)(2,1)S(1)}, bf16[112,768]{1,0:T(8,128)(2,1)S(1)}, u32[]{:S(2)}, u32[]{:S(2)}) %collective-permute-start.32) | collective-permute-done | bytes 172064 | tf_op jit(solution)/shard_map/ppermute | solution.py:660
  (139 shorter events, 43.9 us)
Async XLA Ops:
  0.7 46.0 %collective-permute-start.11 = (bf16[768,768]{1,0:T(8,128)(2,1)}, bf16[768,768]{1,0:T(8,128)(2,1)}, u32[]{:S(2)}, u32[]{:S(2)}) collective-permute-start(bf16[768,768]{1,0:T(8,128)(2,1)} %bitcast.43), channel_id=1, source_target_pairs={{0,2},{1,3},{2,0},{3,1},{4,6},{5,7},{6,4},{7,5},{8,10},{9,11},{10,... | collective-permute-start | bytes 3538952 | tf_op jit(solution)/shard_map/ppermute | solution.py:660
  4.9 8.7 %collective-permute-start.5 = (bf16[96,768]{1,0:T(8,128)(2,1)S(1)}, bf16[96,768]{1,0:T(8,128)(2,1)S(1)}, u32[]{:S(2)}, u32[]{:S(2)}) collective-permute-start(bf16[96,768]{1,0:T(8,128)(2,1)S(1)} %get-tuple-element.67.refs_2_), channel_id=1, source_target_pairs={{0,24},{4,28},{8,16},{12,20},{16,8},{20,12},{24,0},{28,4},{1,25},{... | collective-permute-start | bytes 442376 | tf_op jit(solution)/shard_map/ppermute | solution.py:660
  8.6 12.2 %collective-permute-start.3 = (bf16[96,768]{1,0:T(8,128)(2,1)S(1)}, bf16[96,768]{1,0:T(8,128)(2,1)S(1)}, u32[]{:S(2)}, u32[]{:S(2)}) collective-permute-start(bf16[96,768]{1,0:T(8,128)(2,1)S(1)} %get-tuple-element.67.refs_2_), channel_id=1, source_target_pairs={{0,16},{4,20},{8,24},{12,28},{16,0},{20,4},{24,8},{28,12},{1,17},{... | collective-permute-start | bytes 442376 | tf_op jit(solution)/shard_map/ppermute | solution.py:660
  8.6 13.7 %collective-permute-start.1 = (bf16[96,768]{1,0:T(8,128)(2,1)S(1)}, bf16[96,768]{1,0:T(8,128)(2,1)S(1)}, u32[]{:S(2)}, u32[]{:S(2)}) collective-permute-start(bf16[96,768]{1,0:T(8,128)(2,1)S(1)} %get-tuple-element.67.refs_2_), channel_id=1, source_target_pairs={{0,8},{4,12},{8,0},{12,4},{16,24},{20,28},{24,16},{28,20},{1,9},{5... | collective-permute-start | bytes 442376 | tf_op jit(solution)/shard_map/ppermute | solution.py:660
  9.4 13.5 %collective-permute-start = (bf16[96,768]{1,0:T(8,128)(2,1)S(1)}, bf16[96,768]{1,0:T(8,128)(2,1)S(1)}, u32[]{:S(2)}, u32[]{:S(2)}) collective-permute-start(bf16[96,768]{1,0:T(8,128)(2,1)S(1)} %get-tuple-element.67.refs_2_), channel_id=1, source_target_pairs={{0,4},{4,0},{8,12},{12,8},{16,20},{20,16},{24,28},{28,24},{1,5},{5... | collective-permute-start | bytes 442376 | tf_op jit(solution)/shard_map/ppermute | solution.py:660
  13.6 12.4 %collective-permute-start.6 = (bf16[96,768]{1,0:T(8,128)(2,1)S(1)}, bf16[96,768]{1,0:T(8,128)(2,1)S(1)}, u32[]{:S(2)}, u32[]{:S(2)}) collective-permute-start(bf16[96,768]{1,0:T(8,128)(2,1)S(1)} %collective-permute-done.5.refs_8_), channel_id=1, source_target_pairs={{0,4},{4,0},{8,12},{12,8},{16,20},{20,16},{24,28},{28,24},{1,5},{5... | collective-permute-start | bytes 442376 | tf_op jit(solution)/shard_map/ppermute | solution.py:660
  22.3 6.5 %collective-permute-start.2 = (bf16[96,768]{1,0:T(8,128)(2,1)S(1)}, bf16[96,768]{1,0:T(8,128)(2,1)S(1)}, u32[]{:S(2)}, u32[]{:S(2)}) collective-permute-start(bf16[96,768]{1,0:T(8,128)(2,1)S(1)} %collective-permute-done.1.refs_4_), channel_id=1, source_target_pairs={{0,4},{4,0},{8,12},{12,8},{16,20},{20,16},{24,28},{28,24},{1,5},{5... | collective-permute-start | bytes 442376 | tf_op jit(solution)/shard_map/ppermute | solution.py:660
  22.8 12.2 %collective-permute-start.8 = (bf16[128,768]{1,0:T(8,128)(2,1)S(1)}, bf16[128,768]{1,0:T(8,128)(2,1)S(1)}, u32[]{:S(2)}, u32[]{:S(2)}) collective-permute-start(bf16[128,768]{1,0:T(8,128)(2,1)S(1)} %copy-done.6), channel_id=1, source_target_pairs={{0,2},{1,3},{2,0},{3,1},{4,6},{5,7},{6,4},{7,5},{8,10},{9,11},{10,... | collective-permute-start | bytes 589832 | tf_op jit(solution)/shard_map/ppermute | solution.py:660
  30.8 18.2 %all-to-all-start = ((bf16[8,48,768]{2,1,0:T(8,128)(2,1)}), bf16[8,48,768]{2,1,0:T(8,128)(2,1)S(1)}, u32[]{:S(2)}, u32[]{:S(2)}) async-start(bf16[8,48,768]{2,1,0:T(8,128)(2,1)} %bitcast.31), calls=%async_computation | async-start | bytes 1179648 | tf_op jit(solution)/shard_map/all_to_all | solution.py:809
  35.6 11.1 %collective-permute-start.12 = (bf16[256,768]{1,0:T(8,128)(2,1)S(1)}, bf16[256,768]{1,0:T(8,128)(2,1)S(1)}, u32[]{:S(2)}, u32[]{:S(2)}) collective-permute-start(bf16[256,768]{1,0:T(8,128)(2,1)S(1)} %get-tuple-element.71), channel_id=1, source_target_pairs={{0,2},{1,3},{2,0},{3,1},{4,6},{5,7},{6,4},{7,5},{8,10},{9,11},{10,... | collective-permute-start | bytes 1179656 | tf_op jit(solution)/shard_map/ppermute | solution.py:660
  55.1 22.6 %all-to-all-start.1 = ((bf16[8,48,896]{2,1,0:T(8,128)(2,1)}), bf16[8,48,896]{2,1,0:T(8,128)(2,1)S(1)}, u32[]{:S(2)}, u32[]{:S(2)}) async-start(bf16[8,48,896]{2,1,0:T(8,128)(2,1)} %bitcast.8), calls=%async_computation.1 | async-start | bytes 1376256 | tf_op jit(solution)/shard_map/all_to_all | solution.py:809
  62.1 17.7 %collective-permute-start.16 = (bf16[512,768]{1,0:T(8,128)(2,1)}, bf16[512,768]{1,0:T(8,128)(2,1)S(1)}, u32[]{:S(2)}, u32[]{:S(2)}) collective-permute-start(bf16[512,768]{1,0:T(8,128)(2,1)} %slice_bitcast_fusion), channel_id=1, source_target_pairs={{0,2},{1,3},{2,0},{3,1},{4,6},{5,7},{6,4},{7,5},{8,10},{9,11},{10,... | collective-permute-start | bytes 2359304 | tf_op jit(solution)/shard_map/ppermute | solution.py:660
  78.2 18.4 %collective-permute-start.19 = (bf16[384,896]{1,0:T(8,128)(2,1)S(1)}, bf16[384,896]{1,0:T(8,128)(2,1)}, u32[]{:S(2)}, u32[]{:S(2)}) collective-permute-start(bf16[384,896]{1,0:T(8,128)(2,1)S(1)} %bitcast.27), channel_id=1, source_target_pairs={{0,2},{1,3},{2,0},{3,1},{4,6},{5,7},{6,4},{7,5},{8,10},{9,11},{10,... | collective-permute-start | bytes 2064392 | tf_op jit(solution)/shard_map/ppermute | solution.py:660
  91.6 19.9 %collective-permute-start.21 = (bf16[384,768]{1,0:T(8,128)(2,1)S(1)}, bf16[384,768]{1,0:T(8,128)(2,1)S(1)}, u32[]{:S(2)}, u32[]{:S(2)}) collective-permute-start(bf16[384,768]{1,0:T(8,128)(2,1)S(1)} %bitcast.25), channel_id=1, source_target_pairs={{0,2},{1,3},{2,0},{3,1},{4,6},{5,7},{6,4},{7,5},{8,10},{9,11},{10,... | collective-permute-start | bytes 1769480 | tf_op jit(solution)/shard_map/ppermute | solution.py:660
  96.6 15.5 %collective-permute-start.20 = (bf16[384,896]{1,0:T(8,128)(2,1)}, bf16[384,896]{1,0:T(8,128)(2,1)}, u32[]{:S(2)}, u32[]{:S(2)}) collective-permute-start(bf16[384,896]{1,0:T(8,128)(2,1)} %collective-permute-done.19.refs_7_.refs_0_), channel_id=1, source_target_pairs={{0,1},{1,0},{2,3},{3,2},{4,5},{5,4},{6,7},{7,6},{8,9},{9,8},{10,11... | collective-permute-start | bytes 2064392 | tf_op jit(solution)/shard_map/ppermute | solution.py:660
  97.9 24.6 %all-to-all-start.2 = ((bf16[8,48,896]{2,1,0:T(8,128)(2,1)}), bf16[8,48,896]{2,1,0:T(8,128)(2,1)S(1)}, u32[]{:S(2)}, u32[]{:S(2)}) async-start(bf16[8,48,896]{2,1,0:T(8,128)(2,1)} %bitcast.11), calls=%async_computation.2 | async-start | bytes 1376256 | tf_op jit(solution)/shard_map/all_to_all | solution.py:809
  112.0 13.5 %collective-permute-start.18 = (bf16[384,768]{1,0:T(8,128)(2,1)}, bf16[384,768]{1,0:T(8,128)(2,1)S(1)}, u32[]{:S(2)}, u32[]{:S(2)}) collective-permute-start(bf16[384,768]{1,0:T(8,128)(2,1)} %get-tuple-element.80.refs_6_), channel_id=1, source_target_pairs={{0,1},{1,0},{2,3},{3,2},{4,5},{5,4},{6,7},{7,6},{8,9},{9,8},{10,11... | collective-permute-start | bytes 1769480 | tf_op jit(solution)/shard_map/ppermute | solution.py:660
  124.9 7.6 %collective-permute-start.24 = (bf16[128,768]{1,0:T(8,128)(2,1)S(1)}, bf16[128,768]{1,0:T(8,128)(2,1)S(1)}, u32[]{:S(2)}, u32[]{:S(2)}) collective-permute-start(bf16[128,768]{1,0:T(8,128)(2,1)S(1)} %get-tuple-element.89.refs_2_), channel_id=1, source_target_pairs={{0,2},{1,3},{2,0},{3,1},{4,6},{5,7},{6,4},{7,5},{8,10},{9,11},{10,... | collective-permute-start | bytes 589832 | tf_op jit(solution)/shard_map/ppermute | solution.py:660
  126.5 28.1 %all-to-all-start.3 = ((bf16[8,48,768]{2,1,0:T(8,128)(2,1)}), bf16[8,48,768]{2,1,0:T(8,128)(2,1)S(1)}, u32[]{:S(2)}, u32[]{:S(2)}) async-start(bf16[8,48,768]{2,1,0:T(8,128)(2,1)} %bitcast.13), calls=%async_computation.3 | async-start | bytes 1179648 | tf_op jit(solution)/shard_map/all_to_all | solution.py:809
  143.3 13.5 %collective-permute-start.29 = (bf16[3,96,768]{2,1,0:T(8,128)(2,1)}, bf16[3,96,768]{2,1,0:T(8,128)(2,1)S(1)}, u32[]{:S(2)}, u32[]{:S(2)}) collective-permute-start(bf16[3,96,768]{2,1,0:T(8,128)(2,1)} %get-tuple-element.108), channel_id=1, source_target_pairs={{0,4},{4,0},{8,12},{12,8},{16,20},{20,16},{24,28},{28,24},{1,5},{5... | collective-permute-start | bytes 1327112 | tf_op jit(solution)/shard_map/ppermute | solution.py:660
  145.4 7.4 %collective-permute-start.27 = (bf16[144,768]{1,0:T(8,128)(2,1)S(1)}, bf16[144,768]{1,0:T(8,128)(2,1)S(1)}, u32[]{:S(2)}, u32[]{:S(2)}) collective-permute-start(bf16[144,768]{1,0:T(8,128)(2,1)S(1)} %get-tuple-element.102), channel_id=1, source_target_pairs={{0,2},{1,3},{2,0},{3,1},{4,6},{5,7},{6,4},{7,5},{8,10},{9,11},{10,... | collective-permute-start | bytes 663560 | tf_op jit(solution)/shard_map/ppermute | solution.py:660
  156.9 9.9 %collective-permute-start.31 = (bf16[112,768]{1,0:T(8,128)(2,1)S(1)}, bf16[112,768]{1,0:T(8,128)(2,1)S(1)}, u32[]{:S(2)}, u32[]{:S(2)}) collective-permute-start(bf16[112,768]{1,0:T(8,128)(2,1)S(1)} %get-tuple-element.114), channel_id=1, source_target_pairs={{0,24},{4,28},{8,16},{12,20},{16,8},{20,12},{24,0},{28,4},{1,25},{... | collective-permute-start | bytes 516104 | tf_op jit(solution)/shard_map/ppermute | solution.py:660
  160.4 15.2 %collective-permute-start.32 = (bf16[112,768]{1,0:T(8,128)(2,1)S(1)}, bf16[112,768]{1,0:T(8,128)(2,1)S(1)}, u32[]{:S(2)}, u32[]{:S(2)}) collective-permute-start(bf16[112,768]{1,0:T(8,128)(2,1)S(1)} %get-tuple-element.115), channel_id=1, source_target_pairs={{0,16},{4,20},{8,24},{12,28},{16,0},{20,4},{24,8},{28,12},{1,17},{... | collective-permute-start | bytes 516104 | tf_op jit(solution)/shard_map/ppermute | solution.py:660
  160.5 15.1 %collective-permute-start.33 = (bf16[112,768]{1,0:T(8,128)(2,1)S(1)}, bf16[112,768]{1,0:T(8,128)(2,1)S(1)}, u32[]{:S(2)}, u32[]{:S(2)}) collective-permute-start(bf16[112,768]{1,0:T(8,128)(2,1)S(1)} %get-tuple-element.116), channel_id=1, source_target_pairs={{0,8},{4,12},{8,0},{12,4},{16,24},{20,28},{24,16},{28,20},{1,9},{5... | collective-permute-start | bytes 516104 | tf_op jit(solution)/shard_map/ppermute | solution.py:660
  (45 other events, 307.7 us)
